TPU v7x, 32 devices: a whole 2x2x4 slice. The times are simulated.
32 devices in a mesh: groups: 2 (over x), shard: 16 (over z, y, core).
Axes of the slice: x: 2, y: 2, z: 4, core: 2. Of those that a mesh axis runs over, the one named last changes fastest.
Arguments:
- embeddings: bfloat16 [1280, 1024], P(('groups', 'shard')), parts along dimension 0, may hold values from -250 to 250
- probes: int32 [1280, 8], P(('groups', 'shard')), parts along dimension 0, may hold values from 0 to 15, all different within a row; in each aligned block of 40 rows (0 to 39, 40 to 79, ...) at most 40 rows name the same one
- assigned: int32 [1280], P(('groups', 'shard')), parts along dimension 0, may hold values from 0 to 1023
- prior_counts: int32 [32768], P(('groups', 'shard')), parts along dimension 0, may hold values from 1 to 16
- centroids: bfloat16 [32768, 1024], P(('groups', 'shard')), parts along dimension 0, may hold values from -30 to 30
- candidates: int32 [32768, 1], P(('groups', 'shard')), parts along dimension 0, may hold values from 0 to 47; in each aligned block of 1024 rows (0 to 1023, 1024 to 2047, ...) at most 32 rows name the same one
- centroids2: bfloat16 [12288, 1024], P(('groups', 'shard')), parts along dimension 0, may hold values from -30 to 30
Outputs:
- density: float32 [1280], P(('groups', 'shard')), parts along dimension 0
- new_centroids: bfloat16 [32768, 1024], P(('groups', 'shard')), parts along dimension 0
- new_counts: int32 [32768], P(('groups', 'shard')), parts along dimension 0
- level_two: float32 [32768], P(('groups', 'shard')), parts along dimension 0
There are 2 independent parts, one for each index of `groups`. A program takes and returns all parts, laid end to end along the dimension named above; each array names one. Nothing has to cross between parts.
Inputs may be any that keep to these rules, and one draw needn't show every extreme that they name: `probes`: each row names 8 different blocks. Among the 40 embeddings of one device no block is named more than 40 times, and in every draw some block is named exactly 40 times by one device's embeddings. `candidates`: among the 1024 level-1 centroids of one device no level-2 block is named more than 32 times, and in every draw some is named exactly 32 times.
All inputs are finite; a program needn't handle non-finite values.
Results may differ from a plain program's by a relative error of at most 0.0015.
Values may be sent and summed in bfloat16 or wider, within the bound.
No kernel may reach another device: no remote copies, remote signals or barrier semaphores. Data moves between devices by JAX's collectives and lax.ppermute only.
A program may use at most 64 MiB of HBM per device.

v0:
```python
import functools

import jax
import jax.numpy as jnp
from jax import lax
from jax.experimental import pallas as pl
from jax.experimental.pallas import tpu as pltpu
from jax.sharding import PartitionSpec as P

BLOCK = 1024
BLOCKS_DEV = 1
BLOCK2 = 128
BLOCKS2_DEV = 3


def unit_rows(values):
    wide = values.astype(jnp.float32)
    power = jnp.mean(wide * wide, axis=-1, keepdims=True) + 1e-06
    return (wide * lax.rsqrt(power)).astype(jnp.bfloat16)


def kernel_sums(rows, unit):
    scores = lax.dot_general(
        rows, unit, (((1,), (1,)), ((), ())), preferred_element_type=jnp.float32
    )
    return jnp.sum(jnp.exp((scores / rows.shape[1] - 1.0) / 0.1), axis=1)


def block_update(rows, slots, width):
    matches = slots[:, None] == jnp.arange(width, dtype=jnp.int32)[None, :]
    sums = lax.dot_general(
        matches.astype(jnp.bfloat16),
        rows,
        (((0,), (0,)), ((), ())),
        preferred_element_type=jnp.float32,
    )
    counts = jnp.sum(matches.astype(jnp.int32), axis=0)
    return (sums, counts)


def slot_ranks(targets, buckets):
    matches = (targets[:, None] == jnp.arange(buckets, dtype=jnp.int32)[None, :]).astype(jnp.int32)
    return jnp.sum(jnp.cumsum(matches, axis=0) * matches, axis=1) - 1


def general_body(embeddings, probes, assigned, prior_counts, centroids, candidates, centroids2):
    devices = lax.axis_size("shard")
    emb_rows, width = embeddings.shape
    probe_count = probes.shape[1]
    capacity = max(2, 2 * emb_rows * probe_count // (BLOCKS_DEV * devices))
    scaled = unit_rows(embeddings)
    units_old = unit_rows(centroids).reshape(BLOCKS_DEV, BLOCK, width)
    total = emb_rows * probe_count
    buckets = BLOCKS_DEV * devices
    flat = probes.reshape(-1)
    place = flat * capacity + slot_ranks(flat, buckets)
    leading = jnp.arange(total, dtype=jnp.int32) % probe_count == 0
    repeated = jnp.repeat(scaled, probe_count, axis=0)
    slot_values = jnp.where(leading, jnp.repeat(assigned, probe_count), -1)
    send_rows = jnp.zeros((buckets * capacity, width), jnp.bfloat16).at[place].set(repeated)
    send_slots = jnp.full((buckets * capacity,), -1, jnp.int32).at[place].set(slot_values)
    got_rows, got_slots = (
        lax.all_to_all(
            send_rows.reshape(devices, BLOCKS_DEV * capacity, width),
            "shard",
            split_axis=0,
            concat_axis=0,
            tiled=True,
        ),
        lax.all_to_all(
            send_slots.reshape(devices, BLOCKS_DEV * capacity),
            "shard",
            split_axis=0,
            concat_axis=0,
            tiled=True,
        ),
    )
    got_rows = got_rows.reshape(devices, BLOCKS_DEV, capacity, width)
    got_slots = got_slots.reshape(devices, BLOCKS_DEV, capacity)
    local = 0
    picked = got_rows[:, local].reshape(devices * capacity, width)
    slots = got_slots[:, local].reshape(-1)
    weights = [kernel_sums(picked, units_old[local]).reshape(devices, capacity)]
    more_sums, more_counts = block_update(picked, slots, BLOCK)
    sum_list = [more_sums]
    count_list = [more_counts]
    sums = jnp.stack(sum_list)
    counts = jnp.stack(count_list)
    returned = lax.all_to_all(
        jnp.stack(weights, axis=1).reshape(devices, BLOCKS_DEV * capacity),
        "shard",
        split_axis=0,
        concat_axis=0,
        tiled=True,
    )
    totals = jnp.sum(returned.reshape(-1)[place].reshape(emb_rows, probe_count), axis=1)
    density = jnp.log(totals / (probe_count * BLOCK))
    prior = prior_counts.reshape(BLOCKS_DEV, BLOCK)
    fresh = prior + counts
    updated = (
        prior.astype(jnp.float32)[:, :, None]
        * centroids.reshape(BLOCKS_DEV, BLOCK, width).astype(jnp.float32)
        + sums
    ) / fresh.astype(jnp.float32)[:, :, None]
    new_centroids = updated.astype(jnp.bfloat16).reshape(BLOCKS_DEV * BLOCK, width)
    units_new = unit_rows(updated).reshape(BLOCKS_DEV * BLOCK, width)
    rows_two = units_new.shape[0]
    second_capacity = max(2, 3 * rows_two // (2 * BLOCKS2_DEV * devices))
    buckets_two = BLOCKS2_DEV * devices
    chosen = candidates[:, 0]
    place_two = chosen * second_capacity + slot_ranks(chosen, buckets_two)
    send_two = (
        jnp.zeros((buckets_two * second_capacity, width), jnp.bfloat16).at[place_two].set(units_new)
    )
    send_two = send_two.reshape(devices, BLOCKS2_DEV, second_capacity, width)
    units_two = unit_rows(centroids2).reshape(BLOCKS2_DEV, BLOCK2, width)
    arrived = lax.all_to_all(send_two, "shard", split_axis=0, concat_axis=0, tiled=True)
    items = arrived.shape[2]
    weights_two = [
        kernel_sums(arrived[:, local].reshape(-1, width), units_two[local]).reshape(
            arrived.shape[0], items
        )
        for local in range(BLOCKS2_DEV)
    ]
    returned_two = lax.all_to_all(
        jnp.stack(weights_two, axis=1), "shard", split_axis=0, concat_axis=0, tiled=True
    )
    level_two = jnp.log(returned_two.reshape(-1)[place_two] / BLOCK2)
    return (density, new_centroids, fresh.reshape(-1), level_two)


NT = (((1,), (1,)), ((), ()))
PARAMS = pltpu.CompilerParams(vmem_limit_bytes=48 * 1024 * 1024)
META = 16
HBM = pl.BlockSpec(memory_space=pltpu.HBM)
ANY = pl.BlockSpec(memory_space=pl.ANY)
VMEM = pl.BlockSpec(memory_space=pltpu.VMEM)


def position():
    me = lax.axis_index("shard")
    return me, me // 4, (me // 2) % 2, me % 2


def unit_wide(wide):
    power = jnp.mean(wide * wide, axis=-1, keepdims=True) + 1e-06
    return (wide * lax.rsqrt(power)).astype(jnp.bfloat16)


def weights(scores, width):
    return jnp.exp(scores * (10.0 / width) - 10.0)


def one_hot(hits):
    return jnp.where(hits, 1.0, 0.0).astype(jnp.bfloat16)


def column(row):
    return jnp.transpose(jnp.broadcast_to(row, (8, row.shape[1])))[:, 0:1]


def fetch(pairs, sems):
    copies = [pltpu.make_async_copy(src, dst, sems.at[i]) for i, (src, dst) in enumerate(pairs)]
    for copy in copies:
        copy.start()
    return copies


def pick_rows(slot, first, count):
    return one_hot(slot == lax.broadcasted_iota(jnp.int32, (count, slot.shape[1]), 0) + first)


def pack(slot, prior, cent, first, out):
    count = out.shape[0] - META
    rows = slot.shape[1]
    ident = lax.broadcasted_iota(jnp.int32, (1, rows), 1) + 1
    line = lax.broadcasted_iota(jnp.int32, (META, rows), 0)
    facts = jnp.where(line == 0, ident >> 5, jnp.where(line == 1, ident & 31, jnp.where(line == 2, prior, 0)))
    facts = facts.astype(jnp.float32).astype(jnp.bfloat16)
    pick = pick_rows(slot, first, count)
    out[0:count, :] = jnp.dot(pick, cent, preferred_element_type=jnp.float32).astype(jnp.bfloat16)
    out[count:, :] = jnp.zeros((META, out.shape[1]), jnp.bfloat16)
    out[count:, 0:count] = lax.dot_general(facts, pick, NT, preferred_element_type=jnp.float32).astype(jnp.bfloat16)


def pack_kernel(
    cap, per, cand_any, emb_any, probes_any, assigned_any, prior_any, cent_any, mine, rows2, rows3, info,
    cand_ref, emb_ref, probes_ref, assigned_ref, prior_ref, cent_ref, sems,
):
    copies = fetch(
        (
            (cand_any, cand_ref),
            (emb_any, emb_ref),
            (probes_any, probes_ref),
            (assigned_any, assigned_ref),
            (prior_any, prior_ref),
            (cent_any, cent_ref),
        ),
        sems,
    )
    me, z, y, core = position()
    rows = cand_ref.shape[1]
    buckets = 16 * per
    before = lax.broadcasted_iota(jnp.int32, (rows, rows), 0) <= lax.broadcasted_iota(jnp.int32, (rows, rows), 1)
    before = one_hot(before)
    copies[0].wait()
    cand = cand_ref[...]
    dev = sum((cand >= per * step).astype(jnp.int32) for step in range(1, 16))
    near = dev >> 2
    plane = jnp.where(z >= 2, 3 - near, near)
    rel = (((dev >> 1) & 1) ^ y) * 2 + ((dev & 1) ^ core)
    named = cand == lax.broadcasted_iota(jnp.int32, (buckets, rows), 0)
    counted = jnp.dot(one_hot(named), before, preferred_element_type=jnp.float32)
    rank = jnp.sum(jnp.where(named, counted, 0.0), axis=0, keepdims=True).astype(jnp.int32) - 1
    kind = plane * per + cand - dev * per
    slot = (rel * 4 * per + kind) * cap + rank
    info[0:1, :] = slot
    info[1:2, :] = rel * 4 + (kind >> 2)
    info[2:3, :] = (kind & 3) * cap + rank
    for copy in copies[1:5]:
        copy.wait()
    count, width = emb_ref.shape
    probe_count = probes_ref.shape[0]
    slots = assigned_ref[...]
    facts = jnp.concatenate([probes_ref[...], slots >> 5, slots & 31], axis=0).astype(jnp.float32)
    facts = jnp.concatenate([facts, jnp.zeros((128 - probe_count - 2, count), jnp.float32)], axis=0)
    same = lax.broadcasted_iota(jnp.int32, (count, count), 0) == lax.broadcasted_iota(jnp.int32, (count, count), 1)
    mine[:, 0:width] = emb_ref[...]
    mine[:, width:] = lax.dot_general(
        one_hot(same), facts.astype(jnp.bfloat16), NT, preferred_element_type=jnp.float32
    ).astype(jnp.bfloat16)
    copies[5].wait()
    pack(slot, prior_ref[...], cent_ref[...], 2 * 4 * per * cap, rows2)
    pack(slot, prior_ref[...], cent_ref[...], 3 * 4 * per * cap, rows3)


def pack_more_kernel(part, info, prior_ref, cent_ref, rows0, rows1, late2, late3):
    for first, out in ((0, rows0), (4 * part, rows1), (11 * part, late2), (15 * part, late3)):
        pack(info[0:1, :], prior_ref[...], cent_ref[...], first, out)


def order_kernel(*refs):
    pass


def share_kernel(mine_any, other_any, cent_ref, scaled, facts, share, mine_ref, other_ref, sems):
    copies = fetch(((mine_any, mine_ref), (other_any, other_ref)), sems)
    me, z, y, core = position()
    half = mine_ref.shape[0]
    count = 2 * half
    rows, width = cent_ref.shape
    copies[0].wait()
    scaled[0:half, :] = unit_wide(mine_ref[:, 0:width].astype(jnp.float32))
    copies[1].wait()
    scaled[half:count, :] = unit_wide(other_ref[:, 0:width].astype(jnp.float32))
    aux = jnp.concatenate([mine_ref[:, width:], other_ref[:, width:]], axis=0).astype(jnp.float32)
    aux = jnp.transpose(aux)[0:16, :].astype(jnp.int32)
    facts[...] = aux
    member = jnp.sum((aux[0:8, :] == me).astype(jnp.float32), axis=0, keepdims=True)
    step = 256
    total = jnp.zeros((1, count), jnp.float32)
    for start in range(0, rows, step):
        old = cent_ref[start : start + step, :].astype(jnp.float32)
        scores = lax.dot_general(unit_wide(old), scaled[...], NT, preferred_element_type=jnp.float32)
        total = total + jnp.sum(weights(scores, width), axis=0, keepdims=True)
    piece = count // 16
    lane = lax.broadcasted_iota(jnp.int32, (16, count), 1)
    line = lax.broadcasted_iota(jnp.int32, (16, count), 0)
    apart = jnp.where((member > 0.0) & (lane >= line * piece) & (lane < (line + 1) * piece), total, 0.0)
    spot = lax.broadcasted_iota(jnp.int32, (count, 128), 0)
    block = sum((spot >= piece * step).astype(jnp.int32) for step in range(1, 16))
    together = jnp.where(spot - block * piece == lax.broadcasted_iota(jnp.int32, (count, 128), 1), 1.0, 0.0)
    share[...] = jnp.dot(apart, together, precision=lax.Precision.HIGHEST, preferred_element_type=jnp.float32)


def update_kernel(after, scaled, facts, cent_ref, prior_ref, fresh_rows, fresh_counts):
    me, z, y, core = position()
    rows, width = cent_ref.shape
    count = scaled.shape[0]
    prior = column(prior_ref[...].astype(jnp.float32))
    target = jnp.where(facts[0:1, :] == me, facts[8:9, :] * 32 + facts[9:10, :], -1)
    step = 256
    for start in range(0, rows, step):
        old = cent_ref[start : start + step, :].astype(jnp.float32)
        hits = one_hot(target == lax.broadcasted_iota(jnp.int32, (step, count), 0) + start)
        sums = jnp.dot(hits, scaled[...], preferred_element_type=jnp.float32)
        gained = jnp.sum(hits.astype(jnp.float32), axis=1, keepdims=True)
        ahead = prior[start : start + step, :]
        updated = (ahead * old + sums) / (ahead + gained)
        fresh_rows[start : start + step, :] = updated.astype(jnp.bfloat16)
        gained_row = lax.dot_general(
            jnp.ones((8, count), jnp.bfloat16), hits, NT, preferred_element_type=jnp.float32
        )
        fresh_counts[0:1, start : start + step] = prior_ref[0:1, start : start + step] + gained_row[0:1, :].astype(jnp.int32)


def level_sums(two, rows, per):
    block = two.shape[0] // per
    lines = []
    for j in range(per):
        scores = lax.dot_general(two[j * block : (j + 1) * block, :], rows(j), NT, preferred_element_type=jnp.float32)
        lines.append(jnp.sum(weights(scores, two.shape[1]), axis=0, keepdims=True))
    return jnp.concatenate(lines, axis=0)


def redo(cap, per, scaled, facts_in, source, ref, rows, first, packed, r):
    part = per * cap
    probe0 = facts_in[0:1, :]
    slots = facts_in[8:9, :] * 32 + facts_in[9:10, :]
    facts = jnp.transpose(ref[ref.shape[0] - META :, first : first + rows].astype(jnp.float32))
    hits = (facts[:, 0:1] * 32.0 + facts[:, 1:2]).astype(jnp.int32) == jnp.where(probe0 == source, slots + 1, -1)
    hits = one_hot(hits)
    gained = jnp.sum(hits.astype(jnp.float32), axis=1, keepdims=True)
    added = jnp.dot(hits, scaled[...], preferred_element_type=jnp.float32)
    ahead = facts[:, 2:3]
    wide = (ahead * ref[0:rows, :].astype(jnp.float32) + added) / jnp.maximum(ahead + gained, 1.0)
    unit = unit_wide(wide)
    for w in range(rows // part):
        for j in range(per):
            start = w * part + j * cap
            packed[w, j, r * cap : (r + 1) * cap, :] = unit[start : start + cap, :]


def second_kernel(
    cap, per, scaled, facts_in, own_any, near_any, cross_any, passed_any, any0, any1, any2, any3,
    sums, rows0, rows1, rows2, rows3, two, two_more, two_last, packed, sems,
):
    me, z, y, core = position()
    end = (z == 0) | (z == 3)
    at_end = pltpu.make_async_copy(passed_any, two_last, sems.at[6])
    at_mid = pltpu.make_async_copy(cross_any, two_last, sems.at[6])
    pl.when(end)(at_end.start)
    pl.when(jnp.logical_not(end))(at_mid.start)
    copies = fetch(
        [(any0, rows0), (any1, rows1), (any2, rows2), (any3, rows3), (own_any, two), (near_any, two_more)], sems
    )
    for r, ref in enumerate((rows0, rows1, rows2, rows3)):
        copies[r].wait()
        redo(cap, per, scaled, facts_in, me ^ r, ref, 3 * per * cap, 0, packed, r)
    copies[4].wait()
    copies[5].wait()
    own_unit = unit_wide(two[...].astype(jnp.float32))
    near_unit = unit_wide(two_more[...].astype(jnp.float32))
    first = jnp.where(end, 0, 1)
    sums[pl.ds(first * 8, per), :] = level_sums(own_unit, lambda j: packed[first, j], per)
    sums[pl.ds(8 - first * 8, per), :] = level_sums(near_unit, lambda j: packed[1 - first, j], per)
    pl.when(end)(at_end.wait)
    pl.when(jnp.logical_not(end))(at_mid.wait)
    sums[16 : 16 + per, :] = level_sums(unit_wide(two_last[...].astype(jnp.float32)), lambda j: packed[2, j], per)


def late_kernel(cap, per, scaled, facts_in, any0, any1, any2, any3, kept, rows0, rows1, rows2, rows3, sems):
    me, z, y, core = position()
    part = per * cap
    tail = pl.ds(3 * part, part + META)
    copies = fetch([(any0.at[tail], rows0), (any1.at[tail], rows1), (any2, rows2), (any3, rows3)], sems)
    for r, ref in enumerate((rows0, rows1, rows2, rows3)):
        copies[r].wait()
        redo(cap, per, scaled, facts_in, me ^ r, ref, part, 3 * part if r < 2 else 0, kept, r)


def third_kernel(cap, per, early, share, kept_any, last_any, far_any, out, kept, two, sems):
    me, z, y, core = position()
    end = (z == 0) | (z == 3)
    at_end = pltpu.make_async_copy(far_any, two, sems.at[1])
    at_mid = pltpu.make_async_copy(last_any, two, sems.at[1])
    pl.when(end)(at_end.start)
    pl.when(jnp.logical_not(end))(at_mid.start)
    copies = fetch([(kept_any, kept)], sems)
    pl.when(end)(at_end.wait)
    pl.when(jnp.logical_not(end))(at_mid.wait)
    two_unit = unit_wide(two[...].astype(jnp.float32))
    copies[0].wait()
    final = level_sums(two_unit, lambda j: kept[0, j], per)
    lines = [early[8 * w : 8 * w + per, :] for w in range(3)] + [final]
    together = jnp.concatenate(lines + [jnp.zeros((16 - 4 * per, 4 * cap), jnp.float32)], axis=0)
    lane = lax.broadcasted_iota(jnp.int32, together.shape, 1)
    line = lax.broadcasted_iota(jnp.int32, together.shape, 0)
    out[...] = jnp.zeros(out.shape, jnp.float32)
    for r in range(4):
        spread = jnp.zeros_like(together)
        for s in range(4):
            turned = together if s == r else pltpu.roll(together, ((s - r) % 4) * cap, 1)
            spread = jnp.where((line % 4 == s) & (lane >= s * cap) & (lane < (s + 1) * cap), turned, spread)
        out[me ^ r, 0:4, :] = jnp.concatenate(
            [jnp.sum(spread[4 * t : 4 * t + 4], axis=0, keepdims=True) for t in range(4)], axis=0
        )
    for b in range(16):
        apart = ((b & 1) * 4) ^ ((b >> 1 & 1) * 12) ^ ((b >> 2 & 1) * 2) ^ (b >> 3)
        out[me ^ apart, 4:5, :] = share[b : b + 1, :]


def last_kernel(cap, scale_one, scale_two, info, got, density, level_two):
    me, z, y, core = position()
    total = jnp.zeros((1, 4 * cap), jnp.float32)
    for source in range(16):
        total = total + got[source, 4:5, :]
    density[...] = jnp.log(total[:, 0 : density.shape[1]] / scale_one)
    values = jnp.concatenate([got[me ^ r, 0:4, :] for r in range(4)], axis=0)
    rows = info.shape[1]
    chosen = jnp.where(info[2:3, :] == lax.broadcasted_iota(jnp.int32, (4 * cap, rows), 0), 1.0, 0.0)
    spread = jnp.dot(values, chosen, precision=lax.Precision.HIGHEST, preferred_element_type=jnp.float32)
    found = jnp.where(info[1:2, :] == lax.broadcasted_iota(jnp.int32, (16, rows), 0), spread, 0.0)
    level_two[...] = jnp.log(jnp.sum(found, axis=0, keepdims=True) / scale_two)


def call(kernel, outs, scratch=(), in_specs=None, **kw):
    def run(*args):
        specs = in_specs or [VMEM] * len(args)
        args = [pltpu.with_memory_space_constraint(a, pltpu.HBM) if spec is HBM else a for a, spec in zip(args, specs)]
        return pl.pallas_call(
            kernel, out_shape=outs, in_specs=specs, scratch_shapes=list(scratch), compiler_params=PARAMS, **kw
        )(*args)

    return run


def in_order(*values, **kw):
    count = len(values)
    return call(
        order_kernel,
        tuple(jax.ShapeDtypeStruct(value.shape, value.dtype) for value in values),
        in_specs=[ANY] * count,
        out_specs=(ANY,) * count,
        input_output_aliases={i: i for i in range(count)},
        **kw,
    )(*values)


def line_body(embeddings, probes, assigned, prior_counts, centroids, candidates, centroids2):
    emb_rows, width = embeddings.shape
    probe_count = probes.shape[1]
    rows = centroids.shape[0]
    per = BLOCKS2_DEV
    cap = max(2, 3 * rows // (2 * per * 16))
    part = per * cap
    bf16, f32, i32 = jnp.bfloat16, jnp.float32, jnp.int32
    shape = jax.ShapeDtypeStruct

    def exchange(value, apart, sources=range(16)):
        return lax.ppermute(value, "shard", [(i, i ^ apart) for i in sources])

    def rows_of(planes):
        return shape((planes * part + META, width), bf16)

    def room(like):
        return pltpu.VMEM(like.shape, like.dtype)

    mids = range(4, 12)
    near_set = exchange(centroids2, 4)
    cross_set = exchange(centroids2, 12, mids)
    prior_row = prior_counts.reshape(1, rows)
    line = pltpu.VMEM((1, rows), i32)
    mine, early2, early3, info = call(
        functools.partial(pack_kernel, cap, per),
        (shape((emb_rows, width + 128), bf16), rows_of(3), rows_of(3), shape((8, rows), i32)),
        [
            line,
            pltpu.VMEM((emb_rows, width), bf16),
            pltpu.VMEM((probe_count, emb_rows), i32),
            pltpu.VMEM((1, emb_rows), i32),
            line,
            pltpu.VMEM((rows, width), bf16),
            pltpu.SemaphoreType.DMA((6,)),
        ],
        in_specs=[HBM] * 6,
    )(candidates.reshape(1, rows), embeddings, probes.T, assigned.reshape(1, emb_rows), prior_row, centroids)
    early2, early3 = exchange(early2, 2), exchange(early3, 3)
    rows0, rows1, late2, late3 = call(
        functools.partial(pack_more_kernel, part), (rows_of(4), rows_of(4), rows_of(1), rows_of(1))
    )(info, prior_row, centroids)
    rows1 = exchange(rows1, 1)
    mine = jnp.concatenate([mine, exchange(mine, 4)], axis=0)
    near_set, cross_set, mine = in_order(near_set, cross_set, mine)
    across = exchange(mine, 12)
    passed = exchange(cross_set, 4, mids)
    last_set = exchange(near_set, 12, mids)
    mine = jnp.concatenate([mine, across], axis=0)
    mine, early2, early3, late2, late3 = in_order(mine, early2, early3, late2, late3)
    mine = jnp.concatenate([mine, exchange(mine, 2)], axis=0)
    late2, late3 = exchange(late2, 2), exchange(late3, 3)
    other = exchange(mine, 1)
    step = pl.CostEstimate(flops=0, transcendentals=0, bytes_accessed=40 * centroids2.size * 2)
    passed, last_set = in_order(passed, last_set, cost_estimate=step)
    far_set = exchange(last_set, 4, mids)
    gathered = pltpu.VMEM((8 * emb_rows, width + 128), bf16)
    scaled, facts, share = call(
        share_kernel,
        (
            shape((16 * emb_rows, width), bf16),
            shape((16, 16 * emb_rows), i32),
            shape((16, 4 * cap), f32),
        ),
        [gathered, gathered, pltpu.SemaphoreType.DMA((2,))],
        in_specs=[ANY, ANY, VMEM],
    )(mine, other, centroids)
    block_set = pltpu.VMEM((per * BLOCK2, width), bf16)
    early = call(
        functools.partial(second_kernel, cap, per),
        shape((24, 4 * cap), f32),
        [room(rows_of(4))] * 2
        + [room(rows_of(3))] * 2
        + [block_set] * 3
        + [pltpu.VMEM((3, per, 4 * cap, width), bf16), pltpu.SemaphoreType.DMA((7,))],
        in_specs=[VMEM, VMEM, HBM] + [ANY] * 7,
    )(scaled, facts, centroids2, near_set, cross_set, passed, rows0, rows1, early2, early3)
    kept = shape((1, per, 4 * cap, width), bf16)
    kept_rows = call(
        functools.partial(late_kernel, cap, per),
        kept,
        [room(rows_of(1))] * 4 + [pltpu.SemaphoreType.DMA((4,))],
        in_specs=[VMEM, VMEM] + [ANY] * 4,
    )(scaled, facts, rows0, rows1, late2, late3)
    results = call(
        functools.partial(third_kernel, cap, per),
        shape((16, 8, 4 * cap), f32),
        [room(kept), block_set, pltpu.SemaphoreType.DMA((2,))],
        in_specs=[VMEM, VMEM, ANY, ANY, ANY],
    )(early, share, kept_rows, last_set, far_set)
    new_centroids, counts = call(
        update_kernel, (shape((rows, width), bf16), shape((1, rows), i32)), in_specs=[ANY] + [VMEM] * 4
    )(results, scaled, facts, centroids, prior_row)
    results = lax.all_to_all(results, "shard", split_axis=0, concat_axis=0, tiled=True)
    density, level_two = call(
        functools.partial(last_kernel, cap, probe_count * BLOCK, BLOCK2), (shape((1, emb_rows), f32), shape((1, rows), f32))
    )(info, results)
    return (density.reshape(-1), new_centroids, counts.reshape(-1), level_two.reshape(-1))


def solution(mesh):
    placed = (
        P(("groups", "shard"), None),
        P(("groups", "shard"), None),
        P(("groups", "shard")),
        P(("groups", "shard")),
        P(("groups", "shard"), None),
        P(("groups", "shard"), None),
        P(("groups", "shard"), None),
    )
    body = line_body if mesh.shape["shard"] == 16 else general_body
    return jax.shard_map(
        body,
        mesh=mesh,
        in_specs=placed,
        out_specs=(
            P(("groups", "shard")),
            P(("groups", "shard"), None),
            P(("groups", "shard")),
            P(("groups", "shard")),
        ),
        check_vma=False,
    )
```

profile of v0, /device:TPU:0, one launch (start us, length us, event | category | flops | bytes accessed | tf_op | source)
XLA Modules:
  0.0 91.2 jit_solution(29084738621526799)
XLA Ops:
  0.6 3.1 %collective-permute-start = (bf16[384,1024]{1,0:T(8,128)(2,1)}, bf16[384,1024]{1,0:T(8,128)(2,1)S(1)}, u32[]{:S(2)}, u32[]{:S(2)}) collective-permute-start(bf16[384,1024]{1,0:T(8,128)(2,1)} %own_any.1), channel_id=1, source_target_pairs={{0,4},{1,5},{2,6},{3,7},{4,0},{5,1},{6,2},{7,3},{8,12},{9,13},{10,... | collective-permute-start | bytes 2359304 | tf_op jit(solution)/shard_map/ppermute | solution.py:441
  3.7 0.7 collective-permute-start.1
  4.4 0.0 copy-start
  4.4 0.0 copy-start.3
  4.4 3.5 %shard_map.102 = (bf16[40,1152]{1,0:T(8,128)(2,1)S(1)}, bf16[304,1024]{1,0:T(8,128)(2,1)S(1)}, bf16[304,1024]{1,0:T(8,128)(2,1)S(1)}, s32[8,1024]{1,0:T(8,128)S(1)}) custom-call(s32[1,1024]{1,0:T(1,128)} %bitcast.10, bf16[40,1024]{1,0:T(8,128)(2,1)} %emb_any.1, s32[8,40]{1,0:T(8,128)} %bitcast.11, s32[1,40]{1,0:T(1,128)} %bitcast.12, s32[1,1024]{1,0:T(1,128)} %bitcast.7, ...), custom_call_target="tpu_custom_call" | custom-call | tf_op jit(solution)/shard_map/pallas_call | solution.py:411
  8.0 4.4 %collective-permute-start.2 = (bf16[40,1152]{1,0:T(8,128)(2,1)S(1)}, bf16[40,1152]{1,0:T(8,128)(2,1)S(1)}, u32[]{:S(2)}, u32[]{:S(2)}) collective-permute-start(bf16[40,1152]{1,0:T(8,128)(2,1)S(1)} %get-tuple-element.30), channel_id=1, source_target_pairs={{0,4},{1,5},{2,6},{3,7},{4,0},{5,1},{6,2},{7,3},{8,12},{9,13},{10,... | collective-permute-start | bytes 276488 | tf_op jit(solution)/shard_map/ppermute | solution.py:441
  12.4 1.5 %collective-permute-start.4 = (bf16[304,1024]{1,0:T(8,128)(2,1)S(1)}, bf16[304,1024]{1,0:T(8,128)(2,1)S(1)}, u32[]{:S(2)}, u32[]{:S(2)}) collective-permute-start(bf16[304,1024]{1,0:T(8,128)(2,1)S(1)} %get-tuple-element.32), channel_id=1, source_target_pairs={{0,2},{1,3},{2,0},{3,1},{4,6},{5,7},{6,4},{7,5},{8,10},{9,11},{10,... | collective-permute-start | bytes 1867784 | tf_op jit(solution)/shard_map/ppermute | solution.py:441
  13.9 0.0 collective-permute-start.5
  13.9 9.5 %collective-permute-done.2 = bf16[40,1152]{1,0:T(8,128)(2,1)S(1)} collective-permute-done((bf16[40,1152]{1,0:T(8,128)(2,1)S(1)}, bf16[40,1152]{1,0:T(8,128)(2,1)S(1)}, u32[]{:S(2)}, u32[]{:S(2)}) %collective-permute-start.2) | collective-permute-done | bytes 92192 | tf_op jit(solution)/shard_map/ppermute | solution.py:441
  23.5 0.0 collective-permute-done.refs_0_
  23.5 0.0 collective-permute-done.1.refs_1_
  23.5 3.8 %collective-permute-start.3 = (bf16[80,1152]{1,0:T(8,128)(2,1)S(1)}, bf16[80,1152]{1,0:T(8,128)(2,1)S(1)}, u32[]{:S(2)}, u32[]{:S(2)}) collective-permute-start(bf16[80,1152]{1,0:T(8,128)(2,1)S(1)} %get-tuple-element.31), channel_id=1, source_target_pairs={{0,12},{1,13},{2,14},{3,15},{4,8},{5,9},{6,10},{7,11},{8,4},{9,5},... | collective-permute-start | bytes 552968 | tf_op jit(solution)/shard_map/ppermute | solution.py:441
  27.3 1.3 %collective-permute-start.8 = (bf16[384,1024]{1,0:T(8,128)(2,1)S(1)}, bf16[384,1024]{1,0:T(8,128)(2,1)S(1)}, u32[]{:S(2)}, u32[]{:S(2)}) collective-permute-start(bf16[384,1024]{1,0:T(8,128)(2,1)S(1)} %get-tuple-element.40.cross_any), channel_id=1, source_target_pairs={{4,0},{5,1},{6,2},{7,3},{8,12},{9,13},{10,14},{11,15},{20,16},{21,... | collective-permute-start | bytes 2359304 | tf_op jit(solution)/shard_map/ppermute | solution.py:441
  28.6 0.7 collective-permute-start.9
  29.3 0.0 copy-done
  29.3 0.0 copy-done.3
  29.4 2.9 %shard_map.104 = (bf16[400,1024]{1,0:T(8,128)(2,1)S(1)}, bf16[400,1024]{1,0:T(8,128)(2,1)S(1)}, bf16[112,1024]{1,0:T(8,128)(2,1)S(1)}, bf16[112,1024]{1,0:T(8,128)(2,1)S(1)}) custom-call(s32[8,1024]{1,0:T(8,128)S(1)} %get-tuple-element.29.info, s32[1,1024]{1,0:T(1,128)S(1)} %bitcast.8, bf16[1024,1024]{1,0:T(8,128)(2,1)S(1)} %copy-done), custom_call_target="tpu_custom_call" | custom-call | tf_op jit(solution)/shard_map/pallas_call | solution.py:411
  32.3 0.0 collective-permute-done.3
  32.3 0.0 collective-permute-done.4.refs_1_
  32.3 7.4 %collective-permute-done.5.refs_2_ = bf16[304,1024]{1,0:T(8,128)(2,1)S(1)} collective-permute-done((bf16[304,1024]{1,0:T(8,128)(2,1)S(1)}, bf16[304,1024]{1,0:T(8,128)(2,1)S(1)}, u32[]{:S(2)}, u32[]{:S(2)}) %collective-permute-start.5) | collective-permute-done | bytes 622624 | tf_op jit(solution)/shard_map/ppermute | solution.py:441
  39.7 0.5 collective-permute-start.6
  40.2 1.8 %collective-permute-start.10 = (bf16[400,1024]{1,0:T(8,128)(2,1)S(1)}, bf16[400,1024]{1,0:T(8,128)(2,1)S(1)}, u32[]{:S(2)}, u32[]{:S(2)}) collective-permute-start(bf16[400,1024]{1,0:T(8,128)(2,1)S(1)} %get-tuple-element.43), channel_id=1, source_target_pairs={{0,1},{1,0},{2,3},{3,2},{4,5},{5,4},{6,7},{7,6},{8,9},{9,8},{10,11... | collective-permute-start | bytes 2457608 | tf_op jit(solution)/shard_map/ppermute | solution.py:441
  42.0 6.1 %collective-permute-done.8.refs_0_ = bf16[384,1024]{1,0:T(8,128)(2,1)S(1)} collective-permute-done((bf16[384,1024]{1,0:T(8,128)(2,1)S(1)}, bf16[384,1024]{1,0:T(8,128)(2,1)S(1)}, u32[]{:S(2)}, u32[]{:S(2)}) %collective-permute-start.8) | collective-permute-done | bytes 786464 | tf_op jit(solution)/shard_map/ppermute | solution.py:441
  48.1 0.0 collective-permute-done.9.refs_1_
  48.1 1.3 %collective-permute-start.13 = (bf16[384,1024]{1,0:T(8,128)(2,1)S(1)}, bf16[384,1024]{1,0:T(8,128)(2,1)S(1)}, u32[]{:S(2)}, u32[]{:S(2)}) collective-permute-start(bf16[384,1024]{1,0:T(8,128)(2,1)S(1)} %get-tuple-element.49.last_any), channel_id=1, source_target_pairs={{4,0},{5,1},{6,2},{7,3},{8,12},{9,13},{10,14},{11,15},{20,16},{21,... | collective-permute-start | bytes 2359304 | tf_op jit(solution)/shard_map/ppermute | solution.py:441
  49.4 1.6 %collective-permute-done.6 = bf16[160,1152]{1,0:T(8,128)(2,1)S(1)} collective-permute-done((bf16[160,1152]{1,0:T(8,128)(2,1)S(1)}, bf16[160,1152]{1,0:T(8,128)(2,1)S(1)}, u32[]{:S(2)}, u32[]{:S(2)}) %collective-permute-start.6) | collective-permute-done | bytes 368672 | tf_op jit(solution)/shard_map/ppermute | solution.py:441
  51.1 0.2 collective-permute-start.7
  51.3 0.3 collective-permute-start.11
  51.6 1.4 %collective-permute-start.12 = (bf16[112,1024]{1,0:T(8,128)(2,1)S(1)}, bf16[112,1024]{1,0:T(8,128)(2,1)S(1)}, u32[]{:S(2)}, u32[]{:S(2)}) collective-permute-start(bf16[112,1024]{1,0:T(8,128)(2,1)S(1)} %get-tuple-element.48), channel_id=1, source_target_pairs={{0,3},{1,2},{2,1},{3,0},{4,7},{5,6},{6,5},{7,4},{8,11},{9,10},{10,... | collective-permute-start | bytes 688136 | tf_op jit(solution)/shard_map/ppermute | solution.py:441
  53.0 0.4 collective-permute-done.7.other_any
  53.4 3.2 %shard_map.106 = (bf16[640,1024]{1,0:T(8,128)(2,1)S(1)}, s32[16,640]{1,0:T(8,128)S(1)}, f32[16,128]{1,0:T(8,128)S(1)}) custom-call(bf16[320,1152]{1,0:T(8,128)(2,1)S(1)} %constant_dynamic-update-slice_fusion.mine_any, bf16[320,1152]{1,0:T(8,128)(2,1)S(1)} %collective-permute-done.7.other_any, bf16[1024,1024]{1,0:T(8,128)(2,1)S(1)} %copy-done), custom_call_target="tpu_custom_call" | custom-call | tf_op jit(solution)/shard_map/pallas_call | solution.py:411
  56.6 0.0 copy-start.1
  56.6 0.0 collective-permute-done.10.any1
  56.6 3.1 %collective-permute-done.11.any2 = bf16[112,1024]{1,0:T(8,128)(2,1)S(1)} collective-permute-done((bf16[112,1024]{1,0:T(8,128)(2,1)S(1)}, bf16[112,1024]{1,0:T(8,128)(2,1)S(1)}, u32[]{:S(2)}, u32[]{:S(2)}) %collective-permute-start.11) | collective-permute-done | bytes 229408 | tf_op jit(solution)/shard_map/ppermute | solution.py:441
  59.7 3.8 %collective-permute-done.12.any3 = bf16[112,1024]{1,0:T(8,128)(2,1)S(1)} collective-permute-done((bf16[112,1024]{1,0:T(8,128)(2,1)S(1)}, bf16[112,1024]{1,0:T(8,128)(2,1)S(1)}, u32[]{:S(2)}, u32[]{:S(2)}) %collective-permute-start.12) | collective-permute-done | bytes 229408 | tf_op jit(solution)/shard_map/ppermute | solution.py:441
  63.5 3.9 %shard_map.109.kept_any = bf16[1,3,128,1024]{3,2,1,0:T(8,128)(2,1)S(1)} custom-call(bf16[640,1024]{1,0:T(8,128)(2,1)S(1)} %get-tuple-element.37.scaled, s32[16,640]{1,0:T(8,128)S(1)} %get-tuple-element.38.facts_in.facts, bf16[400,1024]{1,0:T(8,128)(2,1)S(1)} %get-tuple-element.42.any0, bf16[400,1024]{1,0:T(8,128)(2,1)S(1)} %collective-permute-done.10.any1, ...), custom_call_target="tpu_custom_call" | custom-call | tf_op jit(solution)/shard_map/pallas_call | solution.py:411
  67.5 0.0 copy-done.1
  67.5 8.1 %shard_map.108.early = f32[24,128]{1,0:T(8,128)S(1)} custom-call(bf16[640,1024]{1,0:T(8,128)(2,1)} %copy-done.1, s32[16,640]{1,0:T(8,128)S(1)} %get-tuple-element.38.facts_in.facts, bf16[384,1024]{1,0:T(8,128)(2,1)} %own_any.1, bf16[384,1024]{1,0:T(8,128)(2,1)S(1)} %get-tuple-element.39.near_any, bf16[384,1024]{1,0:T(8,128)(2,1)S(1)} %get-tuple-element.40.cross_any, ...), custom_call_target="tpu_custom_call" | custom-call | tf_op jit(solution)/shard_map/pallas_call | solution.py:411
  75.6 0.0 copy-start.2
  75.6 0.0 collective-permute-done.13.far_any
  75.6 1.5 %shard_map.110.after = f32[16,8,128]{2,1,0:T(8,128)} custom-call(f32[24,128]{1,0:T(8,128)S(1)} %shard_map.108.early, f32[16,128]{1,0:T(8,128)S(1)} %get-tuple-element.46.share, bf16[1,3,128,1024]{3,2,1,0:T(8,128)(2,1)S(1)} %shard_map.109.kept_any, bf16[384,1024]{1,0:T(8,128)(2,1)S(1)} %get-tuple-element.49.last_any, ...), custom_call_target="tpu_custom_call" | custom-call | tf_op jit(solution)/shard_map/pallas_call | solution.py:411
  77.1 6.1 %all-to-all-start = ((f32[16,8,128]{2,1,0:T(8,128)}), f32[16,8,128]{2,1,0:T(8,128)S(1)}, u32[]{:S(2)}, u32[]{:S(2)}) async-start(f32[16,8,128]{2,1,0:T(8,128)} %shard_map.110.after), calls=%async_computation | async-start | bytes 131072 | tf_op jit(solution)/shard_map/all_to_all | solution.py:523
  83.3 0.0 copy-done.2
  83.3 3.6 %shard_map.112 = (bf16[1024,1024]{1,0:T(8,128)(2,1)}, s32[1,1024]{1,0:T(1,128)}) custom-call(f32[16,8,128]{2,1,0:T(8,128)} %shard_map.110.after, bf16[640,1024]{1,0:T(8,128)(2,1)S(1)} %copy-done.2, s32[16,640]{1,0:T(8,128)S(1)} %get-tuple-element.38.facts_in.facts, bf16[1024,1024]{1,0:T(8,128)(2,1)S(1)} %copy-done, s32[1,1024]{1,0:T(1,128)S(1)} %bitcast.9), custom_call_target="tpu_custom_call" | custom-call | tf_op jit(solution)/shard_map/pallas_call | solution.py:411
  86.9 3.3 %all-to-all-done.got = f32[16,8,128]{2,1,0:T(8,128)S(1)} async-done(((f32[16,8,128]{2,1,0:T(8,128)}), f32[16,8,128]{2,1,0:T(8,128)S(1)}, u32[]{:S(2)}, u32[]{:S(2)}) %all-to-all-start) | async-done | bytes 65568 | tf_op jit(solution)/shard_map/all_to_all | solution.py:523
  90.2 1.0 %shard_map.111 = (f32[1,40]{1,0:T(1,128)}, f32[1,1024]{1,0:T(1,128)}) custom-call(s32[8,1024]{1,0:T(8,128)S(1)} %get-tuple-element.29.info, f32[16,8,128]{2,1,0:T(8,128)S(1)} %all-to-all-done.got), custom_call_target="tpu_custom_call" | custom-call | tf_op jit(solution)/shard_map/pallas_call | solution.py:411
  (7 shorter events, 0.1 us)
Async XLA Ops:
  0.6 22.8 %collective-permute-start = (bf16[384,1024]{1,0:T(8,128)(2,1)}, bf16[384,1024]{1,0:T(8,128)(2,1)S(1)}, u32[]{:S(2)}, u32[]{:S(2)}) collective-permute-start(bf16[384,1024]{1,0:T(8,128)(2,1)} %own_any.1), channel_id=1, source_target_pairs={{0,4},{1,5},{2,6},{3,7},{4,0},{5,1},{6,2},{7,3},{8,12},{9,13},{10,... | collective-permute-start | bytes 2359304 | tf_op jit(solution)/shard_map/ppermute | solution.py:441
  3.7 19.8 %collective-permute-start.1 = (bf16[384,1024]{1,0:T(8,128)(2,1)}, bf16[384,1024]{1,0:T(8,128)(2,1)S(1)}, u32[]{:S(2)}, u32[]{:S(2)}) collective-permute-start(bf16[384,1024]{1,0:T(8,128)(2,1)} %own_any.1), channel_id=1, source_target_pairs={{4,8},{5,9},{6,10},{7,11},{8,4},{9,5},{10,6},{11,7},{20,24},{21,25... | collective-permute-start | bytes 2359304 | tf_op jit(solution)/shard_map/ppermute | solution.py:441
  4.4 24.9 %copy-start = (bf16[1024,1024]{1,0:T(8,128)(2,1)S(1)}, bf16[1024,1024]{1,0:T(8,128)(2,1)}, u32[]{:S(2)}) copy-start(bf16[1024,1024]{1,0:T(8,128)(2,1)} %cent_ref.5) | copy-start | bytes 6291460
  4.4 24.9 %copy-start.3 = (s32[1024]{0:T(1024)S(1)}, s32[1024]{0:T(1024)}, u32[]{:S(2)}) copy-start(s32[1024]{0:T(1024)} %param.10) | copy-start | bytes 12292
  8.0 15.5 %collective-permute-start.2 = (bf16[40,1152]{1,0:T(8,128)(2,1)S(1)}, bf16[40,1152]{1,0:T(8,128)(2,1)S(1)}, u32[]{:S(2)}, u32[]{:S(2)}) collective-permute-start(bf16[40,1152]{1,0:T(8,128)(2,1)S(1)} %get-tuple-element.30), channel_id=1, source_target_pairs={{0,4},{1,5},{2,6},{3,7},{4,0},{5,1},{6,2},{7,3},{8,12},{9,13},{10,... | collective-permute-start | bytes 276488 | tf_op jit(solution)/shard_map/ppermute | solution.py:441
  12.4 20.0 %collective-permute-start.4 = (bf16[304,1024]{1,0:T(8,128)(2,1)S(1)}, bf16[304,1024]{1,0:T(8,128)(2,1)S(1)}, u32[]{:S(2)}, u32[]{:S(2)}) collective-permute-start(bf16[304,1024]{1,0:T(8,128)(2,1)S(1)} %get-tuple-element.32), channel_id=1, source_target_pairs={{0,2},{1,3},{2,0},{3,1},{4,6},{5,7},{6,4},{7,5},{8,10},{9,11},{10,... | collective-permute-start | bytes 1867784 | tf_op jit(solution)/shard_map/ppermute | solution.py:441
  13.9 25.8 %collective-permute-start.5 = (bf16[304,1024]{1,0:T(8,128)(2,1)S(1)}, bf16[304,1024]{1,0:T(8,128)(2,1)S(1)}, u32[]{:S(2)}, u32[]{:S(2)}) collective-permute-start(bf16[304,1024]{1,0:T(8,128)(2,1)S(1)} %get-tuple-element.33), channel_id=1, source_target_pairs={{0,3},{1,2},{2,1},{3,0},{4,7},{5,6},{6,5},{7,4},{8,11},{9,10},{10,... | collective-permute-start | bytes 1867784 | tf_op jit(solution)/shard_map/ppermute | solution.py:441
  23.5 8.8 %collective-permute-start.3 = (bf16[80,1152]{1,0:T(8,128)(2,1)S(1)}, bf16[80,1152]{1,0:T(8,128)(2,1)S(1)}, u32[]{:S(2)}, u32[]{:S(2)}) collective-permute-start(bf16[80,1152]{1,0:T(8,128)(2,1)S(1)} %get-tuple-element.31), channel_id=1, source_target_pairs={{0,12},{1,13},{2,14},{3,15},{4,8},{5,9},{6,10},{7,11},{8,4},{9,5},... | collective-permute-start | bytes 552968 | tf_op jit(solution)/shard_map/ppermute | solution.py:441
  27.3 20.8 %collective-permute-start.8 = (bf16[384,1024]{1,0:T(8,128)(2,1)S(1)}, bf16[384,1024]{1,0:T(8,128)(2,1)S(1)}, u32[]{:S(2)}, u32[]{:S(2)}) collective-permute-start(bf16[384,1024]{1,0:T(8,128)(2,1)S(1)} %get-tuple-element.40.cross_any), channel_id=1, source_target_pairs={{4,0},{5,1},{6,2},{7,3},{8,12},{9,13},{10,14},{11,15},{20,16},{21,... | collective-permute-start | bytes 2359304 | tf_op jit(solution)/shard_map/ppermute | solution.py:441
  28.6 19.5 %collective-permute-start.9 = (bf16[384,1024]{1,0:T(8,128)(2,1)S(1)}, bf16[384,1024]{1,0:T(8,128)(2,1)S(1)}, u32[]{:S(2)}, u32[]{:S(2)}) collective-permute-start(bf16[384,1024]{1,0:T(8,128)(2,1)S(1)} %get-tuple-element.39.near_any), channel_id=1, source_target_pairs={{4,8},{5,9},{6,10},{7,11},{8,4},{9,5},{10,6},{11,7},{20,24},{21,25... | collective-permute-start | bytes 2359304 | tf_op jit(solution)/shard_map/ppermute | solution.py:441
  39.7 11.4 %collective-permute-start.6 = (bf16[160,1152]{1,0:T(8,128)(2,1)S(1)}, bf16[160,1152]{1,0:T(8,128)(2,1)S(1)}, u32[]{:S(2)}, u32[]{:S(2)}) collective-permute-start(bf16[160,1152]{1,0:T(8,128)(2,1)S(1)} %get-tuple-element.36), channel_id=1, source_target_pairs={{0,2},{1,3},{2,0},{3,1},{4,6},{5,7},{6,4},{7,5},{8,10},{9,11},{10,... | collective-permute-start | bytes 1105928 | tf_op jit(solution)/shard_map/ppermute | solution.py:441
  40.2 16.4 %collective-permute-start.10 = (bf16[400,1024]{1,0:T(8,128)(2,1)S(1)}, bf16[400,1024]{1,0:T(8,128)(2,1)S(1)}, u32[]{:S(2)}, u32[]{:S(2)}) collective-permute-start(bf16[400,1024]{1,0:T(8,128)(2,1)S(1)} %get-tuple-element.43), channel_id=1, source_target_pairs={{0,1},{1,0},{2,3},{3,2},{4,5},{5,4},{6,7},{7,6},{8,9},{9,8},{10,11... | collective-permute-start | bytes 2457608 | tf_op jit(solution)/shard_map/ppermute | solution.py:441
  48.1 27.5 %collective-permute-start.13 = (bf16[384,1024]{1,0:T(8,128)(2,1)S(1)}, bf16[384,1024]{1,0:T(8,128)(2,1)S(1)}, u32[]{:S(2)}, u32[]{:S(2)}) collective-permute-start(bf16[384,1024]{1,0:T(8,128)(2,1)S(1)} %get-tuple-element.49.last_any), channel_id=1, source_target_pairs={{4,0},{5,1},{6,2},{7,3},{8,12},{9,13},{10,14},{11,15},{20,16},{21,... | collective-permute-start | bytes 2359304 | tf_op jit(solution)/shard_map/ppermute | solution.py:441
  51.1 2.3 %collective-permute-start.7 = (bf16[320,1152]{1,0:T(8,128)(2,1)S(1)}, bf16[320,1152]{1,0:T(8,128)(2,1)S(1)}, u32[]{:S(2)}, u32[]{:S(2)}) collective-permute-start(bf16[320,1152]{1,0:T(8,128)(2,1)S(1)} %constant_dynamic-update-slice_fusion.mine_any), channel_id=1, source_target_pairs={{0,1},{1,0},{2,3},{3,2},{4,5},{5,4},{6,7},{7,6},{8,9},{9,8},{10,11... | collective-permute-start | bytes 2211848 | tf_op jit(solution)/shard_map/ppermute | solution.py:441
  51.3 8.5 %collective-permute-start.11 = (bf16[112,1024]{1,0:T(8,128)(2,1)S(1)}, bf16[112,1024]{1,0:T(8,128)(2,1)S(1)}, u32[]{:S(2)}, u32[]{:S(2)}) collective-permute-start(bf16[112,1024]{1,0:T(8,128)(2,1)S(1)} %get-tuple-element.47), channel_id=1, source_target_pairs={{0,2},{1,3},{2,0},{3,1},{4,6},{5,7},{6,4},{7,5},{8,10},{9,11},{10,... | collective-permute-start | bytes 688136 | tf_op jit(solution)/shard_map/ppermute | solution.py:441
  51.6 12.0 %collective-permute-start.12 = (bf16[112,1024]{1,0:T(8,128)(2,1)S(1)}, bf16[112,1024]{1,0:T(8,128)(2,1)S(1)}, u32[]{:S(2)}, u32[]{:S(2)}) collective-permute-start(bf16[112,1024]{1,0:T(8,128)(2,1)S(1)} %get-tuple-element.48), channel_id=1, source_target_pairs={{0,3},{1,2},{2,1},{3,0},{4,7},{5,6},{6,5},{7,4},{8,11},{9,10},{10,... | collective-permute-start | bytes 688136 | tf_op jit(solution)/shard_map/ppermute | solution.py:441
  56.6 10.9 %copy-start.1 = (bf16[640,1024]{1,0:T(8,128)(2,1)}, bf16[640,1024]{1,0:T(8,128)(2,1)S(1)}, u32[]{:S(2)}) copy-start(bf16[640,1024]{1,0:T(8,128)(2,1)S(1)} %get-tuple-element.37.scaled) | copy-start | bytes 3932164
  75.6 7.7 %copy-start.2 = (bf16[640,1024]{1,0:T(8,128)(2,1)S(1)}, bf16[640,1024]{1,0:T(8,128)(2,1)}, u32[]{:S(2)}) copy-start(bf16[640,1024]{1,0:T(8,128)(2,1)} %copy-done.1) | copy-start | bytes 3932164
  77.1 13.0 %all-to-all-start = ((f32[16,8,128]{2,1,0:T(8,128)}), f32[16,8,128]{2,1,0:T(8,128)S(1)}, u32[]{:S(2)}, u32[]{:S(2)}) async-start(f32[16,8,128]{2,1,0:T(8,128)} %shard_map.110.after), calls=%async_computation | async-start | bytes 131072 | tf_op jit(solution)/shard_map/all_to_all | solution.py:523
where the time goes:
time: 91.5 us; the launch traced here: 91.2 us
  waiting for transfers between devices  35.2 us (38%)
  Pallas kernels  27.8 us (30%)
  starting transfers between devices  27.2 us (30%)
    ppermute x14, waiting for transfers between devices, exchange(): return lax.ppermute(value, 'shard', [(i, i ^ apart) for i in sources])  31.9 us
    pallas_call x11, Pallas kernels, run(): pl.pallas_call(kernel, out_shape=outs, in_specs=specs, scratch_shapes=lis...  27.8 us
    ppermute x14, starting transfers between devices, exchange(): return lax.ppermute(value, 'shard', [(i, i ^ apart) for i in sources])  21.1 us
    all_to_all x1, starting transfers between devices, line_body(): lax.all_to_all(results, 'shard', split_axis=0, concat_axis=0, tiled=True)  6.13 us
    all_to_all x1, waiting for transfers between devices, line_body(): lax.all_to_all(results, 'shard', split_axis=0, concat_axis=0, tiled=True)  3.29 us
  transfers between devices with their start and end apart: 15, of which 8 were waited for; matrix products, arithmetic and copies ran while one was open for 0% of the time, Pallas kernels for 28%

commit v1 on v0

--- a/solution.py
+++ b/solution.py
@@ -132,6 +132,8 @@
 NT = (((1,), (1,)), ((), ()))
 PARAMS = pltpu.CompilerParams(vmem_limit_bytes=48 * 1024 * 1024)
 META = 16
+LATE = 5
+STEP = 3
 HBM = pl.BlockSpec(memory_space=pltpu.HBM)
 ANY = pl.BlockSpec(memory_space=pl.ANY)
 VMEM = pl.BlockSpec(memory_space=pltpu.VMEM)
@@ -235,7 +237,7 @@
 
 
 def pack_more_kernel(part, info, prior_ref, cent_ref, rows0, rows1, late2, late3):
-    for first, out in ((0, rows0), (4 * part, rows1), (11 * part, late2), (15 * part, late3)):
+    for first, out in ((0, rows0), (4 * part, rows1), (10 * part, late2), (14 * part, late3)):
         pack(info[0:1, :], prior_ref[...], cent_ref[...], first, out)
 
 
@@ -286,7 +288,7 @@
         sums = jnp.dot(hits, scaled[...], preferred_element_type=jnp.float32)
         gained = jnp.sum(hits.astype(jnp.float32), axis=1, keepdims=True)
         ahead = prior[start : start + step, :]
-        updated = (ahead * old + sums) / (ahead + gained)
+        updated = (ahead * old + sums) * (1.0 / (ahead + gained))
         fresh_rows[start : start + step, :] = updated.astype(jnp.bfloat16)
         gained_row = lax.dot_general(
             jnp.ones((8, count), jnp.bfloat16), hits, NT, preferred_element_type=jnp.float32
@@ -303,63 +305,71 @@
     return jnp.concatenate(lines, axis=0)
 
 
-def redo(cap, per, scaled, facts_in, source, ref, rows, first, packed, r):
+def redo(cap, per, scaled, facts_in, me, refs, firsts, packed):
     part = per * cap
+    count = 2 * part
     probe0 = facts_in[0:1, :]
     slots = facts_in[8:9, :] * 32 + facts_in[9:10, :]
-    facts = jnp.transpose(ref[ref.shape[0] - META :, first : first + rows].astype(jnp.float32))
-    hits = (facts[:, 0:1] * 32.0 + facts[:, 1:2]).astype(jnp.int32) == jnp.where(probe0 == source, slots + 1, -1)
-    hits = one_hot(hits)
-    gained = jnp.sum(hits.astype(jnp.float32), axis=1, keepdims=True)
-    added = jnp.dot(hits, scaled[...], preferred_element_type=jnp.float32)
-    ahead = facts[:, 2:3]
-    wide = (ahead * ref[0:rows, :].astype(jnp.float32) + added) / jnp.maximum(ahead + gained, 1.0)
-    unit = unit_wide(wide)
-    for w in range(rows // part):
-        for j in range(per):
-            start = w * part + j * cap
-            packed[w, j, r * cap : (r + 1) * cap, :] = unit[start : start + cap, :]
-
-
-def second_kernel(
-    cap, per, scaled, facts_in, own_any, near_any, cross_any, passed_any, any0, any1, any2, any3,
-    sums, rows0, rows1, rows2, rows3, two, two_more, two_last, packed, sems,
+    for r, (ref, first) in enumerate(zip(refs, firsts)):
+        facts = jnp.transpose(ref[ref.shape[0] - META :, first : first + count].astype(jnp.float32))
+        hits = (facts[:, 0:1] * 32.0 + facts[:, 1:2]).astype(jnp.int32) == jnp.where(probe0 == (me ^ r), slots + 1, -1)
+        hits = one_hot(hits)
+        gained = jnp.sum(hits.astype(jnp.float32), axis=1, keepdims=True)
+        ahead = facts[:, 2:3]
+        fresh = jnp.maximum(ahead + gained, 1.0)
+        floor = fresh * fresh * 1e-06
+        added = jnp.dot(hits, scaled[...], preferred_element_type=jnp.float32)
+        whole = ahead * ref[0:count, :].astype(jnp.float32) + added
+        power = jnp.mean(whole * whole, axis=-1, keepdims=True) + floor
+        unit = (whole * lax.rsqrt(power)).astype(jnp.bfloat16)
+        for w in range(2):
+            for j in range(per):
+                start = w * part + j * cap
+                packed[w, j, r * cap : (r + 1) * cap, :] = unit[start : start + cap, :]
+
+
+def early_kernel(
+    cap, per, scaled, facts_in, own_any, near_any, any0, any1, any2, any3,
+    sums, rows0, rows1, rows2, rows3, two, two_more, packed, sems,
 ):
     me, z, y, core = position()
     end = (z == 0) | (z == 3)
-    at_end = pltpu.make_async_copy(passed_any, two_last, sems.at[6])
-    at_mid = pltpu.make_async_copy(cross_any, two_last, sems.at[6])
-    pl.when(end)(at_end.start)
-    pl.when(jnp.logical_not(end))(at_mid.start)
-    copies = fetch(
-        [(any0, rows0), (any1, rows1), (any2, rows2), (any3, rows3), (own_any, two), (near_any, two_more)], sems
-    )
-    for r, ref in enumerate((rows0, rows1, rows2, rows3)):
-        copies[r].wait()
-        redo(cap, per, scaled, facts_in, me ^ r, ref, 3 * per * cap, 0, packed, r)
-    copies[4].wait()
-    copies[5].wait()
+    refs = (rows0, rows1, rows2, rows3)
+    copies = fetch(list(zip((any0, any1, any2, any3, own_any, near_any), (*refs, two, two_more))), sems)
+    for copy in copies:
+        copy.wait()
+    redo(cap, per, scaled, facts_in, me, refs, (0, 0, 0, 0), packed)
     own_unit = unit_wide(two[...].astype(jnp.float32))
     near_unit = unit_wide(two_more[...].astype(jnp.float32))
     first = jnp.where(end, 0, 1)
     sums[pl.ds(first * 8, per), :] = level_sums(own_unit, lambda j: packed[first, j], per)
     sums[pl.ds(8 - first * 8, per), :] = level_sums(near_unit, lambda j: packed[1 - first, j], per)
+
+
+def late_kernel(
+    cap, per, scaled, facts_in, cross_any, passed_any, any0, any1, any2, any3, after,
+    sums, kept, rows0, rows1, rows2, rows3, two, packed, sems,
+):
+    me, z, y, core = position()
+    end = (z == 0) | (z == 3)
+    part = per * cap
+    at_end = pltpu.make_async_copy(passed_any, two, sems.at[4])
+    at_mid = pltpu.make_async_copy(cross_any, two, sems.at[4])
+    pl.when(end)(at_end.start)
+    pl.when(jnp.logical_not(end))(at_mid.start)
+    tail = pl.ds(2 * part, 2 * part + META)
+    refs = (rows0, rows1, rows2, rows3)
+    copies = fetch(list(zip((any0.at[tail], any1.at[tail], any2, any3), refs)), sems)
+    for copy in copies:
+        copy.wait()
+    redo(cap, per, scaled, facts_in, me, refs, (2 * part, 2 * part, 0, 0), packed)
+    kept[...] = packed[1]
     pl.when(end)(at_end.wait)
     pl.when(jnp.logical_not(end))(at_mid.wait)
-    sums[16 : 16 + per, :] = level_sums(unit_wide(two_last[...].astype(jnp.float32)), lambda j: packed[2, j], per)
-
-
-def late_kernel(cap, per, scaled, facts_in, any0, any1, any2, any3, kept, rows0, rows1, rows2, rows3, sems):
-    me, z, y, core = position()
-    part = per * cap
-    tail = pl.ds(3 * part, part + META)
-    copies = fetch([(any0.at[tail], rows0), (any1.at[tail], rows1), (any2, rows2), (any3, rows3)], sems)
-    for r, ref in enumerate((rows0, rows1, rows2, rows3)):
-        copies[r].wait()
-        redo(cap, per, scaled, facts_in, me ^ r, ref, part, 3 * part if r < 2 else 0, kept, r)
-
-
-def third_kernel(cap, per, early, share, kept_any, last_any, far_any, out, kept, two, sems):
+    sums[0:per, :] = level_sums(unit_wide(two[...].astype(jnp.float32)), lambda j: packed[0, j], per)
+
+
+def third_kernel(cap, per, early, later, share, kept_any, last_any, far_any, out, kept, two, sems):
     me, z, y, core = position()
     end = (z == 0) | (z == 3)
     at_end = pltpu.make_async_copy(far_any, two, sems.at[1])
@@ -371,8 +381,8 @@
     pl.when(jnp.logical_not(end))(at_mid.wait)
     two_unit = unit_wide(two[...].astype(jnp.float32))
     copies[0].wait()
-    final = level_sums(two_unit, lambda j: kept[0, j], per)
-    lines = [early[8 * w : 8 * w + per, :] for w in range(3)] + [final]
+    final = level_sums(two_unit, lambda j: kept[j], per)
+    lines = [early[0:per, :], early[8 : 8 + per, :], later[0:per, :], final]
     together = jnp.concatenate(lines + [jnp.zeros((16 - 4 * per, 4 * cap), jnp.float32)], axis=0)
     lane = lax.broadcasted_iota(jnp.int32, together.shape, 1)
     line = lax.broadcasted_iota(jnp.int32, together.shape, 0)
@@ -415,6 +425,10 @@
     return run
 
 
+def lasting(micros):
+    return pl.CostEstimate(flops=0, transcendentals=0, bytes_accessed=int(micros * 3_690_000))
+
+
 def in_order(*values, **kw):
     count = len(values)
     return call(
@@ -453,7 +467,7 @@
     line = pltpu.VMEM((1, rows), i32)
     mine, early2, early3, info = call(
         functools.partial(pack_kernel, cap, per),
-        (shape((emb_rows, width + 128), bf16), rows_of(3), rows_of(3), shape((8, rows), i32)),
+        (shape((emb_rows, width + 128), bf16), rows_of(2), rows_of(2), shape((8, rows), i32)),
         [
             line,
             pltpu.VMEM((emb_rows, width), bf16),
@@ -467,7 +481,7 @@
     )(candidates.reshape(1, rows), embeddings, probes.T, assigned.reshape(1, emb_rows), prior_row, centroids)
     early2, early3 = exchange(early2, 2), exchange(early3, 3)
     rows0, rows1, late2, late3 = call(
-        functools.partial(pack_more_kernel, part), (rows_of(4), rows_of(4), rows_of(1), rows_of(1))
+        functools.partial(pack_more_kernel, part), (rows_of(4), rows_of(4), rows_of(2), rows_of(2))
     )(info, prior_row, centroids)
     rows1 = exchange(rows1, 1)
     mine = jnp.concatenate([mine, exchange(mine, 4)], axis=0)
@@ -479,10 +493,9 @@
     mine, early2, early3, late2, late3 = in_order(mine, early2, early3, late2, late3)
     mine = jnp.concatenate([mine, exchange(mine, 2)], axis=0)
     late2, late3 = exchange(late2, 2), exchange(late3, 3)
+    passed, last_set, mine = in_order(passed, last_set, mine, cost_estimate=lasting(STEP))
+    far_set = exchange(last_set, 4, mids)
     other = exchange(mine, 1)
-    step = pl.CostEstimate(flops=0, transcendentals=0, bytes_accessed=40 * centroids2.size * 2)
-    passed, last_set = in_order(passed, last_set, cost_estimate=step)
-    far_set = exchange(last_set, 4, mids)
     gathered = pltpu.VMEM((8 * emb_rows, width + 128), bf16)
     scaled, facts, share = call(
         share_kernel,
@@ -493,30 +506,32 @@
         ),
         [gathered, gathered, pltpu.SemaphoreType.DMA((2,))],
         in_specs=[ANY, ANY, VMEM],
+        cost_estimate=lasting(3),
     )(mine, other, centroids)
     block_set = pltpu.VMEM((per * BLOCK2, width), bf16)
+    packed = pltpu.VMEM((2, per, 4 * cap, width), bf16)
     early = call(
-        functools.partial(second_kernel, cap, per),
-        shape((24, 4 * cap), f32),
-        [room(rows_of(4))] * 2
-        + [room(rows_of(3))] * 2
-        + [block_set] * 3
-        + [pltpu.VMEM((3, per, 4 * cap, width), bf16), pltpu.SemaphoreType.DMA((7,))],
-        in_specs=[VMEM, VMEM, HBM] + [ANY] * 7,
-    )(scaled, facts, centroids2, near_set, cross_set, passed, rows0, rows1, early2, early3)
-    kept = shape((1, per, 4 * cap, width), bf16)
-    kept_rows = call(
+        functools.partial(early_kernel, cap, per),
+        shape((16, 4 * cap), f32),
+        [room(rows_of(4))] * 2 + [room(rows_of(2))] * 2 + [block_set] * 2 + [packed, pltpu.SemaphoreType.DMA((6,))],
+        in_specs=[VMEM, VMEM, HBM] + [ANY] * 5,
+        cost_estimate=lasting(5),
+    )(scaled, facts, centroids2, near_set, rows0, rows1, early2, early3)
+    kept = shape((per, 4 * cap, width), bf16)
+    later, kept_rows = call(
         functools.partial(late_kernel, cap, per),
-        kept,
-        [room(rows_of(1))] * 4 + [pltpu.SemaphoreType.DMA((4,))],
-        in_specs=[VMEM, VMEM] + [ANY] * 4,
-    )(scaled, facts, rows0, rows1, late2, late3)
+        (shape((8, 4 * cap), f32), kept),
+        [room(rows_of(2))] * 4 + [block_set, packed, pltpu.SemaphoreType.DMA((5,))],
+        in_specs=[VMEM, VMEM] + [ANY] * 7,
+        cost_estimate=lasting(LATE),
+    )(scaled, facts, cross_set, passed, rows0, rows1, late2, late3, early)
     results = call(
         functools.partial(third_kernel, cap, per),
         shape((16, 8, 4 * cap), f32),
         [room(kept), block_set, pltpu.SemaphoreType.DMA((2,))],
-        in_specs=[VMEM, VMEM, ANY, ANY, ANY],
-    )(early, share, kept_rows, last_set, far_set)
+        in_specs=[VMEM, VMEM, VMEM, ANY, ANY, ANY],
+        cost_estimate=lasting(1),
+    )(early, later, share, kept_rows, last_set, far_set)
     new_centroids, counts = call(
         update_kernel, (shape((rows, width), bf16), shape((1, rows), i32)), in_specs=[ANY] + [VMEM] * 4
     )(results, scaled, facts, centroids, prior_row)

time: 91.5 us -> 92.8 us (1.014)
  waiting for transfers between devices: 35.2 us -> 40.6 us
  Pallas kernels: 27.8 us -> 24.5 us
    ppermute x14, waiting for transfers between devices: 31.9 us -> 37.3 us  [exchange(): return lax.ppermute(value, 'shard', [(i, i ^ apart) for i in sources])]
    pallas_call x11, Pallas kernels: 27.8 us -> 24.5 us  [run(): pl.pallas_call(kernel, out_shape=outs, in_specs=specs, scratch_shapes=lis...]
  transfers between devices with their start and end apart: 15 -> 15, of which waited for: 8 -> 7; matrix products, arithmetic and copies ran while one was open for 0% -> 0% of each run, Pallas kernels for 28% -> 24%
where the time goes in v1:
time: 92.8 us; the launch traced here: 92.5 us
  waiting for transfers between devices  40.6 us (44%)
  starting transfers between devices  26.5 us (29%)
  Pallas kernels  24.5 us (26%)
    ppermute x14, waiting for transfers between devices, exchange(): return lax.ppermute(value, 'shard', [(i, i ^ apart) for i in sources])  37.3 us
    pallas_call x11, Pallas kernels, run(): pl.pallas_call(kernel, out_shape=outs, in_specs=specs, scratch_shapes=lis...  24.5 us
    ppermute x14, starting transfers between devices, exchange(): return lax.ppermute(value, 'shard', [(i, i ^ apart) for i in sources])  20.4 us
    all_to_all x1, starting transfers between devices, line_body(): lax.all_to_all(results, 'shard', split_axis=0, concat_axis=0, tiled=True)  6.11 us
    all_to_all x1, waiting for transfers between devices, line_body(): lax.all_to_all(results, 'shard', split_axis=0, concat_axis=0, tiled=True)  3.3 us
  transfers between devices with their start and end apart: 15, of which 7 were waited for; matrix products, arithmetic and copies ran while one was open for 0% of the time, Pallas kernels for 24%

profile of v1, /device:TPU:0, one launch (start us, length us, event | category | flops | bytes accessed | tf_op | source)
XLA Modules:
  0.0 92.5 jit_solution(3795543214254114700)
XLA Ops:
  0.6 3.1 %collective-permute-start = (bf16[384,1024]{1,0:T(8,128)(2,1)}, bf16[384,1024]{1,0:T(8,128)(2,1)S(1)}, u32[]{:S(2)}, u32[]{:S(2)}) collective-permute-start(bf16[384,1024]{1,0:T(8,128)(2,1)} %own_any.1), channel_id=1, source_target_pairs={{0,4},{1,5},{2,6},{3,7},{4,0},{5,1},{6,2},{7,3},{8,12},{9,13},{10,... | collective-permute-start | bytes 2359304 | tf_op jit(solution)/shard_map/ppermute | solution.py:455
  3.7 0.7 collective-permute-start.1
  4.4 2.9 %shard_map.102 = (bf16[40,1152]{1,0:T(8,128)(2,1)S(1)}, bf16[208,1024]{1,0:T(8,128)(2,1)S(1)}, bf16[208,1024]{1,0:T(8,128)(2,1)S(1)}, s32[8,1024]{1,0:T(8,128)S(1)}) custom-call(s32[1,1024]{1,0:T(1,128)} %bitcast.10, bf16[40,1024]{1,0:T(8,128)(2,1)} %emb_any.1, s32[8,40]{1,0:T(8,128)} %bitcast.11, s32[1,40]{1,0:T(1,128)} %bitcast.12, s32[1,1024]{1,0:T(1,128)} %bitcast.7, ...), custom_call_target="tpu_custom_call" | custom-call | tf_op jit(solution)/shard_map/pallas_call | solution.py:421
  7.4 0.0 copy-start
  7.4 0.0 copy-start.1
  7.4 4.4 %collective-permute-start.2 = (bf16[40,1152]{1,0:T(8,128)(2,1)S(1)}, bf16[40,1152]{1,0:T(8,128)(2,1)S(1)}, u32[]{:S(2)}, u32[]{:S(2)}) collective-permute-start(bf16[40,1152]{1,0:T(8,128)(2,1)S(1)} %get-tuple-element.33), channel_id=1, source_target_pairs={{0,4},{1,5},{2,6},{3,7},{4,0},{5,1},{6,2},{7,3},{8,12},{9,13},{10,... | collective-permute-start | bytes 276488 | tf_op jit(solution)/shard_map/ppermute | solution.py:455
  11.8 1.5 %collective-permute-start.6 = (bf16[208,1024]{1,0:T(8,128)(2,1)S(1)}, bf16[208,1024]{1,0:T(8,128)(2,1)S(1)}, u32[]{:S(2)}, u32[]{:S(2)}) collective-permute-start(bf16[208,1024]{1,0:T(8,128)(2,1)S(1)} %get-tuple-element.37), channel_id=1, source_target_pairs={{0,2},{1,3},{2,0},{3,1},{4,6},{5,7},{6,4},{7,5},{8,10},{9,11},{10,... | collective-permute-start | bytes 1277960 | tf_op jit(solution)/shard_map/ppermute | solution.py:455
  13.3 0.0 collective-permute-start.7
  13.3 10.1 %collective-permute-done.2 = bf16[40,1152]{1,0:T(8,128)(2,1)S(1)} collective-permute-done((bf16[40,1152]{1,0:T(8,128)(2,1)S(1)}, bf16[40,1152]{1,0:T(8,128)(2,1)S(1)}, u32[]{:S(2)}, u32[]{:S(2)}) %collective-permute-start.2) | collective-permute-done | bytes 92192 | tf_op jit(solution)/shard_map/ppermute | solution.py:455
  23.5 0.0 collective-permute-done.refs_0_
  23.5 0.0 collective-permute-done.1.refs_1_
  23.5 3.8 %collective-permute-start.5 = (bf16[80,1152]{1,0:T(8,128)(2,1)S(1)}, bf16[80,1152]{1,0:T(8,128)(2,1)S(1)}, u32[]{:S(2)}, u32[]{:S(2)}) collective-permute-start(bf16[80,1152]{1,0:T(8,128)(2,1)S(1)} %get-tuple-element.36), channel_id=1, source_target_pairs={{0,12},{1,13},{2,14},{3,15},{4,8},{5,9},{6,10},{7,11},{8,4},{9,5},... | collective-permute-start | bytes 552968 | tf_op jit(solution)/shard_map/ppermute | solution.py:455
  27.3 0.0 copy-done
  27.3 0.0 copy-done.1
  27.3 3.2 %shard_map.104 = (bf16[400,1024]{1,0:T(8,128)(2,1)S(1)}, bf16[400,1024]{1,0:T(8,128)(2,1)S(1)}, bf16[208,1024]{1,0:T(8,128)(2,1)S(1)}, bf16[208,1024]{1,0:T(8,128)(2,1)S(1)}) custom-call(s32[8,1024]{1,0:T(8,128)S(1)} %get-tuple-element.32.info, s32[1,1024]{1,0:T(1,128)S(1)} %bitcast.8, bf16[1024,1024]{1,0:T(8,128)(2,1)S(1)} %copy-done), custom_call_target="tpu_custom_call" | custom-call | tf_op jit(solution)/shard_map/pallas_call | solution.py:421
  30.6 1.3 %collective-permute-start.3 = (bf16[384,1024]{1,0:T(8,128)(2,1)S(1)}, bf16[384,1024]{1,0:T(8,128)(2,1)S(1)}, u32[]{:S(2)}, u32[]{:S(2)}) collective-permute-start(bf16[384,1024]{1,0:T(8,128)(2,1)S(1)} %get-tuple-element.34.cross_any), channel_id=1, source_target_pairs={{4,0},{5,1},{6,2},{7,3},{8,12},{9,13},{10,14},{11,15},{20,16},{21,... | collective-permute-start | bytes 2359304 | tf_op jit(solution)/shard_map/ppermute | solution.py:455
  31.9 0.7 collective-permute-start.4
  32.6 0.0 collective-permute-done.5
  32.6 0.0 collective-permute-done.6.refs_1_
  32.6 0.0 collective-permute-done.7.refs_2_
  32.7 1.6 %collective-permute-start.8 = (bf16[160,1152]{1,0:T(8,128)(2,1)S(1)}, bf16[160,1152]{1,0:T(8,128)(2,1)S(1)}, u32[]{:S(2)}, u32[]{:S(2)}) collective-permute-start(bf16[160,1152]{1,0:T(8,128)(2,1)S(1)} %get-tuple-element.41), channel_id=1, source_target_pairs={{0,2},{1,3},{2,0},{3,1},{4,6},{5,7},{6,4},{7,5},{8,10},{9,11},{10,... | collective-permute-start | bytes 1105928 | tf_op jit(solution)/shard_map/ppermute | solution.py:455
  34.2 0.0 collective-permute-start.10
  34.2 7.7 %collective-permute-done.8 = bf16[160,1152]{1,0:T(8,128)(2,1)S(1)} collective-permute-done((bf16[160,1152]{1,0:T(8,128)(2,1)S(1)}, bf16[160,1152]{1,0:T(8,128)(2,1)S(1)}, u32[]{:S(2)}, u32[]{:S(2)}) %collective-permute-start.8) | collective-permute-done | bytes 368672 | tf_op jit(solution)/shard_map/ppermute | solution.py:455
  42.0 0.1 pad_maximum_fusion.refs_2_
  42.0 8.5 %collective-permute-done.3.refs_0_ = bf16[384,1024]{1,0:T(8,128)(2,1)S(1)} collective-permute-done((bf16[384,1024]{1,0:T(8,128)(2,1)S(1)}, bf16[384,1024]{1,0:T(8,128)(2,1)S(1)}, u32[]{:S(2)}, u32[]{:S(2)}) %collective-permute-start.3) | collective-permute-done | bytes 786464 | tf_op jit(solution)/shard_map/ppermute | solution.py:455
  50.6 0.0 collective-permute-done.4.refs_1_
  50.6 1.3 %collective-permute-start.13 = (bf16[384,1024]{1,0:T(8,128)(2,1)S(1)}, bf16[384,1024]{1,0:T(8,128)(2,1)S(1)}, u32[]{:S(2)}, u32[]{:S(2)}) collective-permute-start(bf16[384,1024]{1,0:T(8,128)(2,1)S(1)} %get-tuple-element.55.last_any), channel_id=1, source_target_pairs={{4,0},{5,1},{6,2},{7,3},{8,12},{9,13},{10,14},{11,15},{20,16},{21,... | collective-permute-start | bytes 2359304 | tf_op jit(solution)/shard_map/ppermute | solution.py:455
  51.9 0.1 collective-permute-start.9
  51.9 1.6 %collective-permute-start.11 = (bf16[208,1024]{1,0:T(8,128)(2,1)S(1)}, bf16[208,1024]{1,0:T(8,128)(2,1)S(1)}, u32[]{:S(2)}, u32[]{:S(2)}) collective-permute-start(bf16[208,1024]{1,0:T(8,128)(2,1)S(1)} %get-tuple-element.50), channel_id=1, source_target_pairs={{0,2},{1,3},{2,0},{3,1},{4,6},{5,7},{6,4},{7,5},{8,10},{9,11},{10,... | collective-permute-start | bytes 1277960 | tf_op jit(solution)/shard_map/ppermute | solution.py:455
  53.5 0.3 collective-permute-start.12
  53.8 0.3 collective-permute-done.9.other_any
  54.2 3.2 %shard_map.107 = (bf16[640,1024]{1,0:T(8,128)(2,1)S(1)}, s32[16,640]{1,0:T(8,128)S(1)}, f32[16,128]{1,0:T(8,128)S(1)}) custom-call(bf16[320,1152]{1,0:T(8,128)(2,1)S(1)} %get-tuple-element.42.mine_any, bf16[320,1152]{1,0:T(8,128)(2,1)S(1)} %collective-permute-done.9.other_any, bf16[1024,1024]{1,0:T(8,128)(2,1)S(1)} %copy-done), custom_call_target="tpu_custom_call" | custom-call | bytes 11070000 | tf_op jit(solution)/shard_map/pallas_call | solution.py:421
  57.4 0.0 collective-permute-done.10.any1
  57.4 5.0 %shard_map.108.after.early = f32[16,128]{1,0:T(8,128)S(1)} custom-call(bf16[640,1024]{1,0:T(8,128)(2,1)S(1)} %get-tuple-element.43.scaled, s32[16,640]{1,0:T(8,128)S(1)} %get-tuple-element.44.facts_in.facts, bf16[384,1024]{1,0:T(8,128)(2,1)} %own_any.1, bf16[384,1024]{1,0:T(8,128)(2,1)S(1)} %get-tuple-element.35.near_any, ...), custom_call_target="tpu_custom_call" | custom-call | bytes 18450000 | tf_op jit(solution)/shard_map/pallas_call | solution.py:421
  62.3 2.3 %collective-permute-done.11.any2 = bf16[208,1024]{1,0:T(8,128)(2,1)S(1)} collective-permute-done((bf16[208,1024]{1,0:T(8,128)(2,1)S(1)}, bf16[208,1024]{1,0:T(8,128)(2,1)S(1)}, u32[]{:S(2)}, u32[]{:S(2)}) %collective-permute-start.11) | collective-permute-done | bytes 426016 | tf_op jit(solution)/shard_map/ppermute | solution.py:455
  64.6 8.2 %collective-permute-done.12.any3 = bf16[208,1024]{1,0:T(8,128)(2,1)S(1)} collective-permute-done((bf16[208,1024]{1,0:T(8,128)(2,1)S(1)}, bf16[208,1024]{1,0:T(8,128)(2,1)S(1)}, u32[]{:S(2)}, u32[]{:S(2)}) %collective-permute-start.12) | collective-permute-done | bytes 426016 | tf_op jit(solution)/shard_map/ppermute | solution.py:455
  72.9 4.0 %shard_map.109 = (f32[8,128]{1,0:T(8,128)S(1)}, bf16[3,128,1024]{2,1,0:T(8,128)(2,1)S(1)}) custom-call(bf16[640,1024]{1,0:T(8,128)(2,1)S(1)} %get-tuple-element.43.scaled, s32[16,640]{1,0:T(8,128)S(1)} %get-tuple-element.44.facts_in.facts, bf16[384,1024]{1,0:T(8,128)(2,1)S(1)} %get-tuple-element.34.cross_any, ...), custom_call_target="tpu_custom_call" | custom-call | bytes 18450000 | tf_op jit(solution)/shard_map/pallas_call | solution.py:421
  76.9 0.0 collective-permute-done.13.far_any
  76.9 1.5 %shard_map.110.after = f32[16,8,128]{2,1,0:T(8,128)} custom-call(f32[16,128]{1,0:T(8,128)S(1)} %shard_map.108.after.early, f32[8,128]{1,0:T(8,128)S(1)} %get-tuple-element.52.later, f32[16,128]{1,0:T(8,128)S(1)} %get-tuple-element.53.share, bf16[3,128,1024]{2,1,0:T(8,128)(2,1)S(1)} %get-tuple-element.54.kept_any, ...), custom_call_target="tpu_custom_call" | custom-call | bytes 3690000 | tf_op jit(solution)/shard_map/pallas_call | solution.py:421
  78.4 6.1 %all-to-all-start = ((f32[16,8,128]{2,1,0:T(8,128)}), f32[16,8,128]{2,1,0:T(8,128)S(1)}, u32[]{:S(2)}, u32[]{:S(2)}) async-start(f32[16,8,128]{2,1,0:T(8,128)} %shard_map.110.after), calls=%async_computation | async-start | bytes 131072 | tf_op jit(solution)/shard_map/all_to_all | solution.py:538
  84.5 3.6 %shard_map.112 = (bf16[1024,1024]{1,0:T(8,128)(2,1)}, s32[1,1024]{1,0:T(1,128)}) custom-call(f32[16,8,128]{2,1,0:T(8,128)} %shard_map.110.after, bf16[640,1024]{1,0:T(8,128)(2,1)S(1)} %get-tuple-element.43.scaled, s32[16,640]{1,0:T(8,128)S(1)} %get-tuple-element.44.facts_in.facts, bf16[1024,1024]{1,0:T(8,128)(2,1)S(1)} %copy-done, s32[1,1024]{1,0:T(1,128)S(1)} %bitcast.9), custom_call_target="tpu_custom_call" | custom-call | tf_op jit(solution)/shard_map/pallas_call | solution.py:421
  88.1 3.3 %all-to-all-done.got = f32[16,8,128]{2,1,0:T(8,128)S(1)} async-done(((f32[16,8,128]{2,1,0:T(8,128)}), f32[16,8,128]{2,1,0:T(8,128)S(1)}, u32[]{:S(2)}, u32[]{:S(2)}) %all-to-all-start) | async-done | bytes 65568 | tf_op jit(solution)/shard_map/all_to_all | solution.py:538
  91.4 1.0 %shard_map.111 = (f32[1,40]{1,0:T(1,128)}, f32[1,1024]{1,0:T(1,128)}) custom-call(s32[8,1024]{1,0:T(8,128)S(1)} %get-tuple-element.32.info, f32[16,8,128]{2,1,0:T(8,128)S(1)} %all-to-all-done.got), custom_call_target="tpu_custom_call" | custom-call | tf_op jit(solution)/shard_map/pallas_call | solution.py:421
  (5 shorter events, 0.1 us)
Async XLA Ops:
  0.6 22.8 %collective-permute-start = (bf16[384,1024]{1,0:T(8,128)(2,1)}, bf16[384,1024]{1,0:T(8,128)(2,1)S(1)}, u32[]{:S(2)}, u32[]{:S(2)}) collective-permute-start(bf16[384,1024]{1,0:T(8,128)(2,1)} %own_any.1), channel_id=1, source_target_pairs={{0,4},{1,5},{2,6},{3,7},{4,0},{5,1},{6,2},{7,3},{8,12},{9,13},{10,... | collective-permute-start | bytes 2359304 | tf_op jit(solution)/shard_map/ppermute | solution.py:455
  3.7 19.8 %collective-permute-start.1 = (bf16[384,1024]{1,0:T(8,128)(2,1)}, bf16[384,1024]{1,0:T(8,128)(2,1)S(1)}, u32[]{:S(2)}, u32[]{:S(2)}) collective-permute-start(bf16[384,1024]{1,0:T(8,128)(2,1)} %own_any.1), channel_id=1, source_target_pairs={{4,8},{5,9},{6,10},{7,11},{8,4},{9,5},{10,6},{11,7},{20,24},{21,25... | collective-permute-start | bytes 2359304 | tf_op jit(solution)/shard_map/ppermute | solution.py:455
  7.4 20.0 %copy-start = (bf16[1024,1024]{1,0:T(8,128)(2,1)S(1)}, bf16[1024,1024]{1,0:T(8,128)(2,1)}, u32[]{:S(2)}) copy-start(bf16[1024,1024]{1,0:T(8,128)(2,1)} %cent_ref.5) | copy-start | bytes 6291460
  7.4 19.9 %copy-start.1 = (s32[1024]{0:T(1024)S(1)}, s32[1024]{0:T(1024)}, u32[]{:S(2)}) copy-start(s32[1024]{0:T(1024)} %param.10) | copy-start | bytes 12292
  7.4 16.1 %collective-permute-start.2 = (bf16[40,1152]{1,0:T(8,128)(2,1)S(1)}, bf16[40,1152]{1,0:T(8,128)(2,1)S(1)}, u32[]{:S(2)}, u32[]{:S(2)}) collective-permute-start(bf16[40,1152]{1,0:T(8,128)(2,1)S(1)} %get-tuple-element.33), channel_id=1, source_target_pairs={{0,4},{1,5},{2,6},{3,7},{4,0},{5,1},{6,2},{7,3},{8,12},{9,13},{10,... | collective-permute-start | bytes 276488 | tf_op jit(solution)/shard_map/ppermute | solution.py:455
  11.8 20.8 %collective-permute-start.6 = (bf16[208,1024]{1,0:T(8,128)(2,1)S(1)}, bf16[208,1024]{1,0:T(8,128)(2,1)S(1)}, u32[]{:S(2)}, u32[]{:S(2)}) collective-permute-start(bf16[208,1024]{1,0:T(8,128)(2,1)S(1)} %get-tuple-element.37), channel_id=1, source_target_pairs={{0,2},{1,3},{2,0},{3,1},{4,6},{5,7},{6,4},{7,5},{8,10},{9,11},{10,... | collective-permute-start | bytes 1277960 | tf_op jit(solution)/shard_map/ppermute | solution.py:455
  13.3 19.3 %collective-permute-start.7 = (bf16[208,1024]{1,0:T(8,128)(2,1)S(1)}, bf16[208,1024]{1,0:T(8,128)(2,1)S(1)}, u32[]{:S(2)}, u32[]{:S(2)}) collective-permute-start(bf16[208,1024]{1,0:T(8,128)(2,1)S(1)} %get-tuple-element.38), channel_id=1, source_target_pairs={{0,3},{1,2},{2,1},{3,0},{4,7},{5,6},{6,5},{7,4},{8,11},{9,10},{10,... | collective-permute-start | bytes 1277960 | tf_op jit(solution)/shard_map/ppermute | solution.py:455
  23.5 9.1 %collective-permute-start.5 = (bf16[80,1152]{1,0:T(8,128)(2,1)S(1)}, bf16[80,1152]{1,0:T(8,128)(2,1)S(1)}, u32[]{:S(2)}, u32[]{:S(2)}) collective-permute-start(bf16[80,1152]{1,0:T(8,128)(2,1)S(1)} %get-tuple-element.36), channel_id=1, source_target_pairs={{0,12},{1,13},{2,14},{3,15},{4,8},{5,9},{6,10},{7,11},{8,4},{9,5},... | collective-permute-start | bytes 552968 | tf_op jit(solution)/shard_map/ppermute | solution.py:455
  30.6 20.0 %collective-permute-start.3 = (bf16[384,1024]{1,0:T(8,128)(2,1)S(1)}, bf16[384,1024]{1,0:T(8,128)(2,1)S(1)}, u32[]{:S(2)}, u32[]{:S(2)}) collective-permute-start(bf16[384,1024]{1,0:T(8,128)(2,1)S(1)} %get-tuple-element.34.cross_any), channel_id=1, source_target_pairs={{4,0},{5,1},{6,2},{7,3},{8,12},{9,13},{10,14},{11,15},{20,16},{21,... | collective-permute-start | bytes 2359304 | tf_op jit(solution)/shard_map/ppermute | solution.py:455
  31.9 18.7 %collective-permute-start.4 = (bf16[384,1024]{1,0:T(8,128)(2,1)S(1)}, bf16[384,1024]{1,0:T(8,128)(2,1)S(1)}, u32[]{:S(2)}, u32[]{:S(2)}) collective-permute-start(bf16[384,1024]{1,0:T(8,128)(2,1)S(1)} %get-tuple-element.35.near_any), channel_id=1, source_target_pairs={{4,8},{5,9},{6,10},{7,11},{8,4},{9,5},{10,6},{11,7},{20,24},{21,25... | collective-permute-start | bytes 2359304 | tf_op jit(solution)/shard_map/ppermute | solution.py:455
  32.7 9.3 %collective-permute-start.8 = (bf16[160,1152]{1,0:T(8,128)(2,1)S(1)}, bf16[160,1152]{1,0:T(8,128)(2,1)S(1)}, u32[]{:S(2)}, u32[]{:S(2)}) collective-permute-start(bf16[160,1152]{1,0:T(8,128)(2,1)S(1)} %get-tuple-element.41), channel_id=1, source_target_pairs={{0,2},{1,3},{2,0},{3,1},{4,6},{5,7},{6,4},{7,5},{8,10},{9,11},{10,... | collective-permute-start | bytes 1105928 | tf_op jit(solution)/shard_map/ppermute | solution.py:455
  34.2 23.1 %collective-permute-start.10 = (bf16[400,1024]{1,0:T(8,128)(2,1)S(1)}, bf16[400,1024]{1,0:T(8,128)(2,1)S(1)}, u32[]{:S(2)}, u32[]{:S(2)}) collective-permute-start(bf16[400,1024]{1,0:T(8,128)(2,1)S(1)} %get-tuple-element.46), channel_id=1, source_target_pairs={{0,1},{1,0},{2,3},{3,2},{4,5},{5,4},{6,7},{7,6},{8,9},{9,8},{10,11... | collective-permute-start | bytes 2457608 | tf_op jit(solution)/shard_map/ppermute | solution.py:455
  50.6 26.3 %collective-permute-start.13 = (bf16[384,1024]{1,0:T(8,128)(2,1)S(1)}, bf16[384,1024]{1,0:T(8,128)(2,1)S(1)}, u32[]{:S(2)}, u32[]{:S(2)}) collective-permute-start(bf16[384,1024]{1,0:T(8,128)(2,1)S(1)} %get-tuple-element.55.last_any), channel_id=1, source_target_pairs={{4,0},{5,1},{6,2},{7,3},{8,12},{9,13},{10,14},{11,15},{20,16},{21,... | collective-permute-start | bytes 2359304 | tf_op jit(solution)/shard_map/ppermute | solution.py:455
  51.9 2.3 %collective-permute-start.9 = (bf16[320,1152]{1,0:T(8,128)(2,1)S(1)}, bf16[320,1152]{1,0:T(8,128)(2,1)S(1)}, u32[]{:S(2)}, u32[]{:S(2)}) collective-permute-start(bf16[320,1152]{1,0:T(8,128)(2,1)S(1)} %get-tuple-element.42.mine_any), channel_id=1, source_target_pairs={{0,1},{1,0},{2,3},{3,2},{4,5},{5,4},{6,7},{7,6},{8,9},{9,8},{10,11... | collective-permute-start | bytes 2211848 | tf_op jit(solution)/shard_map/ppermute | solution.py:455
  51.9 12.7 %collective-permute-start.11 = (bf16[208,1024]{1,0:T(8,128)(2,1)S(1)}, bf16[208,1024]{1,0:T(8,128)(2,1)S(1)}, u32[]{:S(2)}, u32[]{:S(2)}) collective-permute-start(bf16[208,1024]{1,0:T(8,128)(2,1)S(1)} %get-tuple-element.50), channel_id=1, source_target_pairs={{0,2},{1,3},{2,0},{3,1},{4,6},{5,7},{6,4},{7,5},{8,10},{9,11},{10,... | collective-permute-start | bytes 1277960 | tf_op jit(solution)/shard_map/ppermute | solution.py:455
  53.5 19.3 %collective-permute-start.12 = (bf16[208,1024]{1,0:T(8,128)(2,1)S(1)}, bf16[208,1024]{1,0:T(8,128)(2,1)S(1)}, u32[]{:S(2)}, u32[]{:S(2)}) collective-permute-start(bf16[208,1024]{1,0:T(8,128)(2,1)S(1)} %get-tuple-element.51), channel_id=1, source_target_pairs={{0,3},{1,2},{2,1},{3,0},{4,7},{5,6},{6,5},{7,4},{8,11},{9,10},{10,... | collective-permute-start | bytes 1277960 | tf_op jit(solution)/shard_map/ppermute | solution.py:455
  78.4 13.0 %all-to-all-start = ((f32[16,8,128]{2,1,0:T(8,128)}), f32[16,8,128]{2,1,0:T(8,128)S(1)}, u32[]{:S(2)}, u32[]{:S(2)}) async-start(f32[16,8,128]{2,1,0:T(8,128)} %shard_map.110.after), calls=%async_computation | async-start | bytes 131072 | tf_op jit(solution)/shard_map/all_to_all | solution.py:538

commit v2 on v1

--- a/solution.py
+++ b/solution.py
@@ -133,7 +133,7 @@
 PARAMS = pltpu.CompilerParams(vmem_limit_bytes=48 * 1024 * 1024)
 META = 16
 LATE = 5
-STEP = 3
+STEP = 40
 HBM = pl.BlockSpec(memory_space=pltpu.HBM)
 ANY = pl.BlockSpec(memory_space=pl.ANY)
 VMEM = pl.BlockSpec(memory_space=pltpu.VMEM)
@@ -483,18 +483,19 @@
     rows0, rows1, late2, late3 = call(
         functools.partial(pack_more_kernel, part), (rows_of(4), rows_of(4), rows_of(2), rows_of(2))
     )(info, prior_row, centroids)
-    rows1 = exchange(rows1, 1)
     mine = jnp.concatenate([mine, exchange(mine, 4)], axis=0)
-    near_set, cross_set, mine = in_order(near_set, cross_set, mine)
+    near_set, cross_set, mine, rows0 = in_order(near_set, cross_set, mine, rows0)
     across = exchange(mine, 12)
     passed = exchange(cross_set, 4, mids)
     last_set = exchange(near_set, 12, mids)
     mine = jnp.concatenate([mine, across], axis=0)
-    mine, early2, early3, late2, late3 = in_order(mine, early2, early3, late2, late3)
+    mine, early2, early3, late2 = in_order(mine, early2, early3, late2)
+    late2 = exchange(late2, 2)
     mine = jnp.concatenate([mine, exchange(mine, 2)], axis=0)
-    late2, late3 = exchange(late2, 2), exchange(late3, 3)
-    passed, last_set, mine = in_order(passed, last_set, mine, cost_estimate=lasting(STEP))
+    passed, last_set, mine, late2, late3, rows1 = in_order(passed, last_set, mine, late2, late3, rows1)
     far_set = exchange(last_set, 4, mids)
+    late3 = exchange(late3, 3)
+    rows1 = exchange(rows1, 1)
     other = exchange(mine, 1)
     gathered = pltpu.VMEM((8 * emb_rows, width + 128), bf16)
     scaled, facts, share = call(

time: 92.8 us -> 88.3 us (0.952)
  waiting for transfers between devices: 40.6 us -> 38.3 us
  starting transfers between devices: 26.5 us -> 24.3 us
    all_to_all x1, starting transfers between devices: 6.11 us -> 3.51 us  [line_body(): lax.all_to_all(results, 'shard', split_axis=0, concat_axis=0, tiled=True)]
    ppermute x14, waiting for transfers between devices: 37.3 us -> 35 us  [exchange(): return lax.ppermute(value, 'shard', [(i, i ^ apart) for i in sources])]
  transfers between devices with their start and end apart: 15 -> 15, of which waited for: 7 -> 8; matrix products, arithmetic and copies ran while one was open for 0% -> 0% of each run, Pallas kernels for 24% -> 25%
where the time goes in v2:
time: 88.3 us; the launch traced here: 87.9 us
  waiting for transfers between devices  38.3 us (43%)
  Pallas kernels  24.5 us (28%)
  starting transfers between devices  24.3 us (28%)
    ppermute x14, waiting for transfers between devices, exchange(): return lax.ppermute(value, 'shard', [(i, i ^ apart) for i in sources])  35 us
    pallas_call x11, Pallas kernels, run(): pl.pallas_call(kernel, out_shape=outs, in_specs=specs, scratch_shapes=lis...  24.5 us
    ppermute x14, starting transfers between devices, exchange(): return lax.ppermute(value, 'shard', [(i, i ^ apart) for i in sources])  20.7 us
    all_to_all x1, starting transfers between devices, line_body(): lax.all_to_all(results, 'shard', split_axis=0, concat_axis=0, tiled=True)  3.51 us
    all_to_all x1, waiting for transfers between devices, line_body(): lax.all_to_all(results, 'shard', split_axis=0, concat_axis=0, tiled=True)  3.27 us
  transfers between devices with their start and end apart: 15, of which 8 were waited for; matrix products, arithmetic and copies ran while one was open for 0% of the time, Pallas kernels for 25%

profile of v2, /device:TPU:0, one launch (start us, length us, event | category | flops | bytes accessed | tf_op | source)
XLA Modules:
  0.0 87.9 jit_solution(2032970736091884327)
XLA Ops:
  0.6 0.0 copy-start
  0.6 0.0 copy-start.1
  0.7 3.1 %collective-permute-start = (bf16[384,1024]{1,0:T(8,128)(2,1)}, bf16[384,1024]{1,0:T(8,128)(2,1)S(1)}, u32[]{:S(2)}, u32[]{:S(2)}) collective-permute-start(bf16[384,1024]{1,0:T(8,128)(2,1)} %own_any.1), channel_id=1, source_target_pairs={{0,4},{1,5},{2,6},{3,7},{4,0},{5,1},{6,2},{7,3},{8,12},{9,13},{10,... | collective-permute-start | bytes 2359304 | tf_op jit(solution)/shard_map/ppermute | solution.py:455
  3.7 0.7 collective-permute-start.1
  4.4 2.9 %shard_map.102 = (bf16[40,1152]{1,0:T(8,128)(2,1)S(1)}, bf16[208,1024]{1,0:T(8,128)(2,1)S(1)}, bf16[208,1024]{1,0:T(8,128)(2,1)S(1)}, s32[8,1024]{1,0:T(8,128)S(1)}) custom-call(s32[1,1024]{1,0:T(1,128)} %bitcast.10, bf16[40,1024]{1,0:T(8,128)(2,1)} %emb_any.1, s32[8,40]{1,0:T(8,128)} %bitcast.11, s32[1,40]{1,0:T(1,128)} %bitcast.12, s32[1,1024]{1,0:T(1,128)} %bitcast.7, ...), custom_call_target="tpu_custom_call" | custom-call | tf_op jit(solution)/shard_map/pallas_call | solution.py:421
  7.4 4.4 %collective-permute-start.2 = (bf16[40,1152]{1,0:T(8,128)(2,1)S(1)}, bf16[40,1152]{1,0:T(8,128)(2,1)S(1)}, u32[]{:S(2)}, u32[]{:S(2)}) collective-permute-start(bf16[40,1152]{1,0:T(8,128)(2,1)S(1)} %get-tuple-element.36), channel_id=1, source_target_pairs={{0,4},{1,5},{2,6},{3,7},{4,0},{5,1},{6,2},{7,3},{8,12},{9,13},{10,... | collective-permute-start | bytes 276488 | tf_op jit(solution)/shard_map/ppermute | solution.py:455
  11.8 1.5 %collective-permute-start.6 = (bf16[208,1024]{1,0:T(8,128)(2,1)S(1)}, bf16[208,1024]{1,0:T(8,128)(2,1)S(1)}, u32[]{:S(2)}, u32[]{:S(2)}) collective-permute-start(bf16[208,1024]{1,0:T(8,128)(2,1)S(1)} %get-tuple-element.41), channel_id=1, source_target_pairs={{0,2},{1,3},{2,0},{3,1},{4,6},{5,7},{6,4},{7,5},{8,10},{9,11},{10,... | collective-permute-start | bytes 1277960 | tf_op jit(solution)/shard_map/ppermute | solution.py:455
  13.3 0.0 collective-permute-start.7
  13.3 0.0 copy-done
  13.3 0.0 copy-done.1
  13.3 3.2 %shard_map.103 = (bf16[400,1024]{1,0:T(8,128)(2,1)S(1)}, bf16[400,1024]{1,0:T(8,128)(2,1)S(1)}, bf16[208,1024]{1,0:T(8,128)(2,1)S(1)}, bf16[208,1024]{1,0:T(8,128)(2,1)S(1)}) custom-call(s32[8,1024]{1,0:T(8,128)S(1)} %get-tuple-element.35.info, s32[1,1024]{1,0:T(1,128)S(1)} %bitcast.8, bf16[1024,1024]{1,0:T(8,128)(2,1)S(1)} %copy-done), custom_call_target="tpu_custom_call" | custom-call | tf_op jit(solution)/shard_map/pallas_call | solution.py:421
  16.6 6.9 %collective-permute-done.2 = bf16[40,1152]{1,0:T(8,128)(2,1)S(1)} collective-permute-done((bf16[40,1152]{1,0:T(8,128)(2,1)S(1)}, bf16[40,1152]{1,0:T(8,128)(2,1)S(1)}, u32[]{:S(2)}, u32[]{:S(2)}) %collective-permute-start.2) | collective-permute-done | bytes 92192 | tf_op jit(solution)/shard_map/ppermute | solution.py:455
  23.5 0.0 collective-permute-done.refs_0_
  23.5 0.0 collective-permute-done.1.refs_1_
  23.5 3.8 %collective-permute-start.5 = (bf16[80,1152]{1,0:T(8,128)(2,1)S(1)}, bf16[80,1152]{1,0:T(8,128)(2,1)S(1)}, u32[]{:S(2)}, u32[]{:S(2)}) collective-permute-start(bf16[80,1152]{1,0:T(8,128)(2,1)S(1)} %get-tuple-element.40), channel_id=1, source_target_pairs={{0,12},{1,13},{2,14},{3,15},{4,8},{5,9},{6,10},{7,11},{8,4},{9,5},... | collective-permute-start | bytes 552968 | tf_op jit(solution)/shard_map/ppermute | solution.py:455
  27.4 1.3 %collective-permute-start.3 = (bf16[384,1024]{1,0:T(8,128)(2,1)S(1)}, bf16[384,1024]{1,0:T(8,128)(2,1)S(1)}, u32[]{:S(2)}, u32[]{:S(2)}) collective-permute-start(bf16[384,1024]{1,0:T(8,128)(2,1)S(1)} %get-tuple-element.38.cross_any), channel_id=1, source_target_pairs={{4,0},{5,1},{6,2},{7,3},{8,12},{9,13},{10,14},{11,15},{20,16},{21,... | collective-permute-start | bytes 2359304 | tf_op jit(solution)/shard_map/ppermute | solution.py:455
  28.6 0.7 collective-permute-start.4
  29.4 2.0 %collective-permute-done.5 = bf16[80,1152]{1,0:T(8,128)(2,1)S(1)} collective-permute-done((bf16[80,1152]{1,0:T(8,128)(2,1)S(1)}, bf16[80,1152]{1,0:T(8,128)(2,1)S(1)}, u32[]{:S(2)}, u32[]{:S(2)}) %collective-permute-start.5) | collective-permute-done | bytes 184352 | tf_op jit(solution)/shard_map/ppermute | solution.py:455
  31.4 0.0 collective-permute-done.6.refs_1_
  31.4 0.0 collective-permute-done.7.refs_2_
  31.5 1.5 %collective-permute-start.8 = (bf16[160,1152]{1,0:T(8,128)(2,1)S(1)}, bf16[160,1152]{1,0:T(8,128)(2,1)S(1)}, u32[]{:S(2)}, u32[]{:S(2)}) collective-permute-start(bf16[160,1152]{1,0:T(8,128)(2,1)S(1)} %get-tuple-element.44), channel_id=1, source_target_pairs={{0,2},{1,3},{2,0},{3,1},{4,6},{5,7},{6,4},{7,5},{8,10},{9,11},{10,... | collective-permute-start | bytes 1105928 | tf_op jit(solution)/shard_map/ppermute | solution.py:455
  32.9 0.6 collective-permute-start.9
  33.6 9.4 %collective-permute-done.8 = bf16[160,1152]{1,0:T(8,128)(2,1)S(1)} collective-permute-done((bf16[160,1152]{1,0:T(8,128)(2,1)S(1)}, bf16[160,1152]{1,0:T(8,128)(2,1)S(1)}, u32[]{:S(2)}, u32[]{:S(2)}) %collective-permute-start.8) | collective-permute-done | bytes 368672 | tf_op jit(solution)/shard_map/ppermute | solution.py:455
  43.0 0.1 pad_maximum_fusion.refs_2_
  43.0 8.1 %collective-permute-done.9.refs_3_ = bf16[208,1024]{1,0:T(8,128)(2,1)S(1)} collective-permute-done((bf16[208,1024]{1,0:T(8,128)(2,1)S(1)}, bf16[208,1024]{1,0:T(8,128)(2,1)S(1)}, u32[]{:S(2)}, u32[]{:S(2)}) %collective-permute-start.9) | collective-permute-done | bytes 426016 | tf_op jit(solution)/shard_map/ppermute | solution.py:455
  51.1 0.0 collective-permute-done.3.refs_0_
  51.1 0.0 collective-permute-done.4.refs_1_
  51.1 0.1 collective-permute-start.11
  51.2 1.3 %collective-permute-start.13 = (bf16[384,1024]{1,0:T(8,128)(2,1)S(1)}, bf16[384,1024]{1,0:T(8,128)(2,1)S(1)}, u32[]{:S(2)}, u32[]{:S(2)}) collective-permute-start(bf16[384,1024]{1,0:T(8,128)(2,1)S(1)} %get-tuple-element.61.last_any), channel_id=1, source_target_pairs={{4,0},{5,1},{6,2},{7,3},{8,12},{9,13},{10,14},{11,15},{20,16},{21,... | collective-permute-start | bytes 2359304 | tf_op jit(solution)/shard_map/ppermute | solution.py:455
  52.5 0.6 collective-permute-start.10
  53.0 1.2 %collective-permute-start.12 = (bf16[208,1024]{1,0:T(8,128)(2,1)S(1)}, bf16[208,1024]{1,0:T(8,128)(2,1)S(1)}, u32[]{:S(2)}, u32[]{:S(2)}) collective-permute-start(bf16[208,1024]{1,0:T(8,128)(2,1)S(1)} %get-tuple-element.57), channel_id=1, source_target_pairs={{0,3},{1,2},{2,1},{3,0},{4,7},{5,6},{6,5},{7,4},{8,11},{9,10},{10,... | collective-permute-start | bytes 1277960 | tf_op jit(solution)/shard_map/ppermute | solution.py:455
  54.2 0.6 collective-permute-done.10.other_any
  54.9 3.2 %shard_map.107 = (bf16[640,1024]{1,0:T(8,128)(2,1)S(1)}, s32[16,640]{1,0:T(8,128)S(1)}, f32[16,128]{1,0:T(8,128)S(1)}) custom-call(bf16[320,1152]{1,0:T(8,128)(2,1)S(1)} %get-tuple-element.48.mine_any, bf16[320,1152]{1,0:T(8,128)(2,1)S(1)} %collective-permute-done.10.other_any, bf16[1024,1024]{1,0:T(8,128)(2,1)S(1)} %copy-done), custom_call_target="tpu_custom_call" | custom-call | bytes 11070000 | tf_op jit(solution)/shard_map/pallas_call | solution.py:421
  58.1 0.0 collective-permute-done.11.any1
  58.1 5.0 %shard_map.108.after.early = f32[16,128]{1,0:T(8,128)S(1)} custom-call(bf16[640,1024]{1,0:T(8,128)(2,1)S(1)} %get-tuple-element.49.scaled, s32[16,640]{1,0:T(8,128)S(1)} %get-tuple-element.50.facts_in.facts, bf16[384,1024]{1,0:T(8,128)(2,1)} %own_any.1, bf16[384,1024]{1,0:T(8,128)(2,1)S(1)} %get-tuple-element.39.near_any, ...), custom_call_target="tpu_custom_call" | custom-call | bytes 18450000 | tf_op jit(solution)/shard_map/pallas_call | solution.py:421
  63.1 1.8 %collective-permute-done.12.any3 = bf16[208,1024]{1,0:T(8,128)(2,1)S(1)} collective-permute-done((bf16[208,1024]{1,0:T(8,128)(2,1)S(1)}, bf16[208,1024]{1,0:T(8,128)(2,1)S(1)}, u32[]{:S(2)}, u32[]{:S(2)}) %collective-permute-start.12) | collective-permute-done | bytes 426016 | tf_op jit(solution)/shard_map/ppermute | solution.py:455
  64.9 4.0 %shard_map.109 = (f32[8,128]{1,0:T(8,128)S(1)}, bf16[3,128,1024]{2,1,0:T(8,128)(2,1)S(1)}) custom-call(bf16[640,1024]{1,0:T(8,128)(2,1)S(1)} %get-tuple-element.49.scaled, s32[16,640]{1,0:T(8,128)S(1)} %get-tuple-element.50.facts_in.facts, bf16[384,1024]{1,0:T(8,128)(2,1)S(1)} %get-tuple-element.38.cross_any, ...), custom_call_target="tpu_custom_call" | custom-call | bytes 18450000 | tf_op jit(solution)/shard_map/pallas_call | solution.py:421
  68.9 6.1 %collective-permute-done.13.far_any = bf16[384,1024]{1,0:T(8,128)(2,1)S(1)} collective-permute-done((bf16[384,1024]{1,0:T(8,128)(2,1)S(1)}, bf16[384,1024]{1,0:T(8,128)(2,1)S(1)}, u32[]{:S(2)}, u32[]{:S(2)}) %collective-permute-start.13) | collective-permute-done | bytes 786464 | tf_op jit(solution)/shard_map/ppermute | solution.py:455
  75.0 1.5 %shard_map.110.after = f32[16,8,128]{2,1,0:T(8,128)} custom-call(f32[16,128]{1,0:T(8,128)S(1)} %shard_map.108.after.early, f32[8,128]{1,0:T(8,128)S(1)} %get-tuple-element.58.later, f32[16,128]{1,0:T(8,128)S(1)} %get-tuple-element.59.share, bf16[3,128,1024]{2,1,0:T(8,128)(2,1)S(1)} %get-tuple-element.60.kept_any, ...), custom_call_target="tpu_custom_call" | custom-call | bytes 3690000 | tf_op jit(solution)/shard_map/pallas_call | solution.py:421
  76.5 3.5 %all-to-all-start = ((f32[16,8,128]{2,1,0:T(8,128)}), f32[16,8,128]{2,1,0:T(8,128)S(1)}, u32[]{:S(2)}, u32[]{:S(2)}) async-start(f32[16,8,128]{2,1,0:T(8,128)} %shard_map.110.after), calls=%async_computation | async-start | bytes 131072 | tf_op jit(solution)/shard_map/all_to_all | solution.py:539
  80.1 3.6 %shard_map.112 = (bf16[1024,1024]{1,0:T(8,128)(2,1)}, s32[1,1024]{1,0:T(1,128)}) custom-call(f32[16,8,128]{2,1,0:T(8,128)} %shard_map.110.after, bf16[640,1024]{1,0:T(8,128)(2,1)S(1)} %get-tuple-element.49.scaled, s32[16,640]{1,0:T(8,128)S(1)} %get-tuple-element.50.facts_in.facts, bf16[1024,1024]{1,0:T(8,128)(2,1)S(1)} %copy-done, s32[1,1024]{1,0:T(1,128)S(1)} %bitcast.9), custom_call_target="tpu_custom_call" | custom-call | tf_op jit(solution)/shard_map/pallas_call | solution.py:421
  83.6 3.3 %all-to-all-done.got = f32[16,8,128]{2,1,0:T(8,128)S(1)} async-done(((f32[16,8,128]{2,1,0:T(8,128)}), f32[16,8,128]{2,1,0:T(8,128)S(1)}, u32[]{:S(2)}, u32[]{:S(2)}) %all-to-all-start) | async-done | bytes 65568 | tf_op jit(solution)/shard_map/all_to_all | solution.py:539
  86.9 1.0 %shard_map.111 = (f32[1,40]{1,0:T(1,128)}, f32[1,1024]{1,0:T(1,128)}) custom-call(s32[8,1024]{1,0:T(8,128)S(1)} %get-tuple-element.35.info, f32[16,8,128]{2,1,0:T(8,128)S(1)} %all-to-all-done.got), custom_call_target="tpu_custom_call" | custom-call | tf_op jit(solution)/shard_map/pallas_call | solution.py:421
  (5 shorter events, 0.1 us)
Async XLA Ops:
  0.6 12.7 %copy-start = (bf16[1024,1024]{1,0:T(8,128)(2,1)S(1)}, bf16[1024,1024]{1,0:T(8,128)(2,1)}, u32[]{:S(2)}) copy-start(bf16[1024,1024]{1,0:T(8,128)(2,1)} %cent_ref.5) | copy-start | bytes 6291460
  0.6 12.7 %copy-start.1 = (s32[1024]{0:T(1024)S(1)}, s32[1024]{0:T(1024)}, u32[]{:S(2)}) copy-start(s32[1024]{0:T(1024)} %param.10) | copy-start | bytes 12292
  0.7 22.8 %collective-permute-start = (bf16[384,1024]{1,0:T(8,128)(2,1)}, bf16[384,1024]{1,0:T(8,128)(2,1)S(1)}, u32[]{:S(2)}, u32[]{:S(2)}) collective-permute-start(bf16[384,1024]{1,0:T(8,128)(2,1)} %own_any.1), channel_id=1, source_target_pairs={{0,4},{1,5},{2,6},{3,7},{4,0},{5,1},{6,2},{7,3},{8,12},{9,13},{10,... | collective-permute-start | bytes 2359304 | tf_op jit(solution)/shard_map/ppermute | solution.py:455
  3.7 19.8 %collective-permute-start.1 = (bf16[384,1024]{1,0:T(8,128)(2,1)}, bf16[384,1024]{1,0:T(8,128)(2,1)S(1)}, u32[]{:S(2)}, u32[]{:S(2)}) collective-permute-start(bf16[384,1024]{1,0:T(8,128)(2,1)} %own_any.1), channel_id=1, source_target_pairs={{4,8},{5,9},{6,10},{7,11},{8,4},{9,5},{10,6},{11,7},{20,24},{21,25... | collective-permute-start | bytes 2359304 | tf_op jit(solution)/shard_map/ppermute | solution.py:455
  7.4 16.1 %collective-permute-start.2 = (bf16[40,1152]{1,0:T(8,128)(2,1)S(1)}, bf16[40,1152]{1,0:T(8,128)(2,1)S(1)}, u32[]{:S(2)}, u32[]{:S(2)}) collective-permute-start(bf16[40,1152]{1,0:T(8,128)(2,1)S(1)} %get-tuple-element.36), channel_id=1, source_target_pairs={{0,4},{1,5},{2,6},{3,7},{4,0},{5,1},{6,2},{7,3},{8,12},{9,13},{10,... | collective-permute-start | bytes 276488 | tf_op jit(solution)/shard_map/ppermute | solution.py:455
  11.8 19.6 %collective-permute-start.6 = (bf16[208,1024]{1,0:T(8,128)(2,1)S(1)}, bf16[208,1024]{1,0:T(8,128)(2,1)S(1)}, u32[]{:S(2)}, u32[]{:S(2)}) collective-permute-start(bf16[208,1024]{1,0:T(8,128)(2,1)S(1)} %get-tuple-element.41), channel_id=1, source_target_pairs={{0,2},{1,3},{2,0},{3,1},{4,6},{5,7},{6,4},{7,5},{8,10},{9,11},{10,... | collective-permute-start | bytes 1277960 | tf_op jit(solution)/shard_map/ppermute | solution.py:455
  13.3 18.1 %collective-permute-start.7 = (bf16[208,1024]{1,0:T(8,128)(2,1)S(1)}, bf16[208,1024]{1,0:T(8,128)(2,1)S(1)}, u32[]{:S(2)}, u32[]{:S(2)}) collective-permute-start(bf16[208,1024]{1,0:T(8,128)(2,1)S(1)} %get-tuple-element.42), channel_id=1, source_target_pairs={{0,3},{1,2},{2,1},{3,0},{4,7},{5,6},{6,5},{7,4},{8,11},{9,10},{10,... | collective-permute-start | bytes 1277960 | tf_op jit(solution)/shard_map/ppermute | solution.py:455
  23.5 7.9 %collective-permute-start.5 = (bf16[80,1152]{1,0:T(8,128)(2,1)S(1)}, bf16[80,1152]{1,0:T(8,128)(2,1)S(1)}, u32[]{:S(2)}, u32[]{:S(2)}) collective-permute-start(bf16[80,1152]{1,0:T(8,128)(2,1)S(1)} %get-tuple-element.40), channel_id=1, source_target_pairs={{0,12},{1,13},{2,14},{3,15},{4,8},{5,9},{6,10},{7,11},{8,4},{9,5},... | collective-permute-start | bytes 552968 | tf_op jit(solution)/shard_map/ppermute | solution.py:455
  27.4 23.8 %collective-permute-start.3 = (bf16[384,1024]{1,0:T(8,128)(2,1)S(1)}, bf16[384,1024]{1,0:T(8,128)(2,1)S(1)}, u32[]{:S(2)}, u32[]{:S(2)}) collective-permute-start(bf16[384,1024]{1,0:T(8,128)(2,1)S(1)} %get-tuple-element.38.cross_any), channel_id=1, source_target_pairs={{4,0},{5,1},{6,2},{7,3},{8,12},{9,13},{10,14},{11,15},{20,16},{21,... | collective-permute-start | bytes 2359304 | tf_op jit(solution)/shard_map/ppermute | solution.py:455
  28.6 22.5 %collective-permute-start.4 = (bf16[384,1024]{1,0:T(8,128)(2,1)S(1)}, bf16[384,1024]{1,0:T(8,128)(2,1)S(1)}, u32[]{:S(2)}, u32[]{:S(2)}) collective-permute-start(bf16[384,1024]{1,0:T(8,128)(2,1)S(1)} %get-tuple-element.39.near_any), channel_id=1, source_target_pairs={{4,8},{5,9},{6,10},{7,11},{8,4},{9,5},{10,6},{11,7},{20,24},{21,25... | collective-permute-start | bytes 2359304 | tf_op jit(solution)/shard_map/ppermute | solution.py:455
  31.5 11.5 %collective-permute-start.8 = (bf16[160,1152]{1,0:T(8,128)(2,1)S(1)}, bf16[160,1152]{1,0:T(8,128)(2,1)S(1)}, u32[]{:S(2)}, u32[]{:S(2)}) collective-permute-start(bf16[160,1152]{1,0:T(8,128)(2,1)S(1)} %get-tuple-element.44), channel_id=1, source_target_pairs={{0,2},{1,3},{2,0},{3,1},{4,6},{5,7},{6,4},{7,5},{8,10},{9,11},{10,... | collective-permute-start | bytes 1105928 | tf_op jit(solution)/shard_map/ppermute | solution.py:455
  32.9 18.2 %collective-permute-start.9 = (bf16[208,1024]{1,0:T(8,128)(2,1)S(1)}, bf16[208,1024]{1,0:T(8,128)(2,1)S(1)}, u32[]{:S(2)}, u32[]{:S(2)}) collective-permute-start(bf16[208,1024]{1,0:T(8,128)(2,1)S(1)} %get-tuple-element.45), channel_id=1, source_target_pairs={{0,2},{1,3},{2,0},{3,1},{4,6},{5,7},{6,4},{7,5},{8,10},{9,11},{10,... | collective-permute-start | bytes 1277960 | tf_op jit(solution)/shard_map/ppermute | solution.py:455
  51.1 7.0 %collective-permute-start.11 = (bf16[400,1024]{1,0:T(8,128)(2,1)S(1)}, bf16[400,1024]{1,0:T(8,128)(2,1)S(1)}, u32[]{:S(2)}, u32[]{:S(2)}) collective-permute-start(bf16[400,1024]{1,0:T(8,128)(2,1)S(1)} %get-tuple-element.52), channel_id=1, source_target_pairs={{0,1},{1,0},{2,3},{3,2},{4,5},{5,4},{6,7},{7,6},{8,9},{9,8},{10,11... | collective-permute-start | bytes 2457608 | tf_op jit(solution)/shard_map/ppermute | solution.py:455
  51.2 23.8 %collective-permute-start.13 = (bf16[384,1024]{1,0:T(8,128)(2,1)S(1)}, bf16[384,1024]{1,0:T(8,128)(2,1)S(1)}, u32[]{:S(2)}, u32[]{:S(2)}) collective-permute-start(bf16[384,1024]{1,0:T(8,128)(2,1)S(1)} %get-tuple-element.61.last_any), channel_id=1, source_target_pairs={{4,0},{5,1},{6,2},{7,3},{8,12},{9,13},{10,14},{11,15},{20,16},{21,... | collective-permute-start | bytes 2359304 | tf_op jit(solution)/shard_map/ppermute | solution.py:455
  52.5 2.4 %collective-permute-start.10 = (bf16[320,1152]{1,0:T(8,128)(2,1)S(1)}, bf16[320,1152]{1,0:T(8,128)(2,1)S(1)}, u32[]{:S(2)}, u32[]{:S(2)}) collective-permute-start(bf16[320,1152]{1,0:T(8,128)(2,1)S(1)} %get-tuple-element.48.mine_any), channel_id=1, source_target_pairs={{0,1},{1,0},{2,3},{3,2},{4,5},{5,4},{6,7},{7,6},{8,9},{9,8},{10,11... | collective-permute-start | bytes 2211848 | tf_op jit(solution)/shard_map/ppermute | solution.py:455
  53.0 11.9 %collective-permute-start.12 = (bf16[208,1024]{1,0:T(8,128)(2,1)S(1)}, bf16[208,1024]{1,0:T(8,128)(2,1)S(1)}, u32[]{:S(2)}, u32[]{:S(2)}) collective-permute-start(bf16[208,1024]{1,0:T(8,128)(2,1)S(1)} %get-tuple-element.57), channel_id=1, source_target_pairs={{0,3},{1,2},{2,1},{3,0},{4,7},{5,6},{6,5},{7,4},{8,11},{9,10},{10,... | collective-permute-start | bytes 1277960 | tf_op jit(solution)/shard_map/ppermute | solution.py:455
  76.5 10.4 %all-to-all-start = ((f32[16,8,128]{2,1,0:T(8,128)}), f32[16,8,128]{2,1,0:T(8,128)S(1)}, u32[]{:S(2)}, u32[]{:S(2)}) async-start(f32[16,8,128]{2,1,0:T(8,128)} %shard_map.110.after), calls=%async_computation | async-start | bytes 131072 | tf_op jit(solution)/shard_map/all_to_all | solution.py:539

commit v3 on v2

--- a/solution.py
+++ b/solution.py
@@ -237,7 +237,7 @@
 
 
 def pack_more_kernel(part, info, prior_ref, cent_ref, rows0, rows1, late2, late3):
-    for first, out in ((0, rows0), (4 * part, rows1), (10 * part, late2), (14 * part, late3)):
+    for first, out in ((0, rows0), (4 * part, rows1), (11 * part, late2), (15 * part, late3)):
         pack(info[0:1, :], prior_ref[...], cent_ref[...], first, out)
 
 
@@ -307,7 +307,8 @@
 
 def redo(cap, per, scaled, facts_in, me, refs, firsts, packed):
     part = per * cap
-    count = 2 * part
+    planes = packed.shape[0]
+    count = planes * part
     probe0 = facts_in[0:1, :]
     slots = facts_in[8:9, :] * 32 + facts_in[9:10, :]
     for r, (ref, first) in enumerate(zip(refs, firsts)):
@@ -322,20 +323,24 @@
         whole = ahead * ref[0:count, :].astype(jnp.float32) + added
         power = jnp.mean(whole * whole, axis=-1, keepdims=True) + floor
         unit = (whole * lax.rsqrt(power)).astype(jnp.bfloat16)
-        for w in range(2):
+        for w in range(planes):
             for j in range(per):
                 start = w * part + j * cap
                 packed[w, j, r * cap : (r + 1) * cap, :] = unit[start : start + cap, :]
 
 
 def early_kernel(
-    cap, per, scaled, facts_in, own_any, near_any, any0, any1, any2, any3,
-    sums, rows0, rows1, rows2, rows3, two, two_more, packed, sems,
+    cap, per, scaled, facts_in, own_any, near_any, cross_any, passed_any, any0, any1, any2, any3,
+    sums, rows0, rows1, rows2, rows3, two, two_more, two_last, packed, sems,
 ):
     me, z, y, core = position()
     end = (z == 0) | (z == 3)
     refs = (rows0, rows1, rows2, rows3)
+    at_end = pltpu.make_async_copy(passed_any, two_last, sems.at[6])
+    at_mid = pltpu.make_async_copy(cross_any, two_last, sems.at[6])
     copies = fetch(list(zip((any0, any1, any2, any3, own_any, near_any), (*refs, two, two_more))), sems)
+    pl.when(end)(at_end.start)
+    pl.when(jnp.logical_not(end))(at_mid.start)
     for copy in copies:
         copy.wait()
     redo(cap, per, scaled, facts_in, me, refs, (0, 0, 0, 0), packed)
@@ -344,32 +349,25 @@
     first = jnp.where(end, 0, 1)
     sums[pl.ds(first * 8, per), :] = level_sums(own_unit, lambda j: packed[first, j], per)
     sums[pl.ds(8 - first * 8, per), :] = level_sums(near_unit, lambda j: packed[1 - first, j], per)
+    pl.when(end)(at_end.wait)
+    pl.when(jnp.logical_not(end))(at_mid.wait)
+    sums[16 : 16 + per, :] = level_sums(unit_wide(two_last[...].astype(jnp.float32)), lambda j: packed[2, j], per)
 
 
 def late_kernel(
-    cap, per, scaled, facts_in, cross_any, passed_any, any0, any1, any2, any3, after,
-    sums, kept, rows0, rows1, rows2, rows3, two, packed, sems,
+    cap, per, scaled, facts_in, any0, any1, any2, any3, after, packed, rows0, rows1, rows2, rows3, sems
 ):
     me, z, y, core = position()
-    end = (z == 0) | (z == 3)
     part = per * cap
-    at_end = pltpu.make_async_copy(passed_any, two, sems.at[4])
-    at_mid = pltpu.make_async_copy(cross_any, two, sems.at[4])
-    pl.when(end)(at_end.start)
-    pl.when(jnp.logical_not(end))(at_mid.start)
-    tail = pl.ds(2 * part, 2 * part + META)
+    tail = pl.ds(3 * part, part + META)
     refs = (rows0, rows1, rows2, rows3)
     copies = fetch(list(zip((any0.at[tail], any1.at[tail], any2, any3), refs)), sems)
     for copy in copies:
         copy.wait()
-    redo(cap, per, scaled, facts_in, me, refs, (2 * part, 2 * part, 0, 0), packed)
-    kept[...] = packed[1]
-    pl.when(end)(at_end.wait)
-    pl.when(jnp.logical_not(end))(at_mid.wait)
-    sums[0:per, :] = level_sums(unit_wide(two[...].astype(jnp.float32)), lambda j: packed[0, j], per)
-
-
-def third_kernel(cap, per, early, later, share, kept_any, last_any, far_any, out, kept, two, sems):
+    redo(cap, per, scaled, facts_in, me, refs, (3 * part, 3 * part, 0, 0), packed)
+
+
+def third_kernel(cap, per, early, kept_any, last_any, far_any, out0, out1, out2, out3, kept, two, sems):
     me, z, y, core = position()
     end = (z == 0) | (z == 3)
     at_end = pltpu.make_async_copy(far_any, two, sems.at[1])
@@ -381,32 +379,23 @@
     pl.when(jnp.logical_not(end))(at_mid.wait)
     two_unit = unit_wide(two[...].astype(jnp.float32))
     copies[0].wait()
-    final = level_sums(two_unit, lambda j: kept[j], per)
-    lines = [early[0:per, :], early[8 : 8 + per, :], later[0:per, :], final]
+    final = level_sums(two_unit, lambda j: kept[0, j], per)
+    lines = [early[8 * w : 8 * w + per, :] for w in range(3)] + [final]
     together = jnp.concatenate(lines + [jnp.zeros((16 - 4 * per, 4 * cap), jnp.float32)], axis=0)
     lane = lax.broadcasted_iota(jnp.int32, together.shape, 1)
     line = lax.broadcasted_iota(jnp.int32, together.shape, 0)
-    out[...] = jnp.zeros(out.shape, jnp.float32)
-    for r in range(4):
+    for r, out in enumerate((out0, out1, out2, out3)):
         spread = jnp.zeros_like(together)
         for s in range(4):
             turned = together if s == r else pltpu.roll(together, ((s - r) % 4) * cap, 1)
             spread = jnp.where((line % 4 == s) & (lane >= s * cap) & (lane < (s + 1) * cap), turned, spread)
-        out[me ^ r, 0:4, :] = jnp.concatenate(
-            [jnp.sum(spread[4 * t : 4 * t + 4], axis=0, keepdims=True) for t in range(4)], axis=0
-        )
-    for b in range(16):
-        apart = ((b & 1) * 4) ^ ((b >> 1 & 1) * 12) ^ ((b >> 2 & 1) * 2) ^ (b >> 3)
-        out[me ^ apart, 4:5, :] = share[b : b + 1, :]
-
-
-def last_kernel(cap, scale_one, scale_two, info, got, density, level_two):
-    me, z, y, core = position()
-    total = jnp.zeros((1, 4 * cap), jnp.float32)
-    for source in range(16):
-        total = total + got[source, 4:5, :]
-    density[...] = jnp.log(total[:, 0 : density.shape[1]] / scale_one)
-    values = jnp.concatenate([got[me ^ r, 0:4, :] for r in range(4)], axis=0)
+        for t in range(4):
+            out[t : t + 1, :] = jnp.sum(spread[4 * t : 4 * t + 4], axis=0, keepdims=True)
+
+
+def last_kernel(cap, scale_one, scale_two, info, got0, got1, got2, got3, shares, density, level_two):
+    density[...] = jnp.log(shares[:, 0 : density.shape[1]] / scale_one)
+    values = jnp.concatenate([got[0:4, :] for got in (got0, got1, got2, got3)], axis=0)
     rows = info.shape[1]
     chosen = jnp.where(info[2:3, :] == lax.broadcasted_iota(jnp.int32, (4 * cap, rows), 0), 1.0, 0.0)
     spread = jnp.dot(values, chosen, precision=lax.Precision.HIGHEST, preferred_element_type=jnp.float32)
@@ -467,7 +456,7 @@
     line = pltpu.VMEM((1, rows), i32)
     mine, early2, early3, info = call(
         functools.partial(pack_kernel, cap, per),
-        (shape((emb_rows, width + 128), bf16), rows_of(2), rows_of(2), shape((8, rows), i32)),
+        (shape((emb_rows, width + 128), bf16), rows_of(3), rows_of(3), shape((8, rows), i32)),
         [
             line,
             pltpu.VMEM((emb_rows, width), bf16),
@@ -481,7 +470,7 @@
     )(candidates.reshape(1, rows), embeddings, probes.T, assigned.reshape(1, emb_rows), prior_row, centroids)
     early2, early3 = exchange(early2, 2), exchange(early3, 3)
     rows0, rows1, late2, late3 = call(
-        functools.partial(pack_more_kernel, part), (rows_of(4), rows_of(4), rows_of(2), rows_of(2))
+        functools.partial(pack_more_kernel, part), (rows_of(4), rows_of(4), rows_of(1), rows_of(1))
     )(info, prior_row, centroids)
     mine = jnp.concatenate([mine, exchange(mine, 4)], axis=0)
     near_set, cross_set, mine, rows0 = in_order(near_set, cross_set, mine, rows0)
@@ -489,13 +478,12 @@
     passed = exchange(cross_set, 4, mids)
     last_set = exchange(near_set, 12, mids)
     mine = jnp.concatenate([mine, across], axis=0)
-    mine, early2, early3, late2 = in_order(mine, early2, early3, late2)
-    late2 = exchange(late2, 2)
+    mine, early2, early3, late2, late3, rows1 = in_order(mine, early2, early3, late2, late3, rows1)
     mine = jnp.concatenate([mine, exchange(mine, 2)], axis=0)
-    passed, last_set, mine, late2, late3, rows1 = in_order(passed, last_set, mine, late2, late3, rows1)
+    late2, late3 = exchange(late2, 2), exchange(late3, 3)
+    rows1 = exchange(rows1, 1)
+    passed, last_set, mine = in_order(passed, last_set, mine)
     far_set = exchange(last_set, 4, mids)
-    late3 = exchange(late3, 3)
-    rows1 = exchange(rows1, 1)
     other = exchange(mine, 1)
     gathered = pltpu.VMEM((8 * emb_rows, width + 128), bf16)
     scaled, facts, share = call(
@@ -509,37 +497,47 @@
         in_specs=[ANY, ANY, VMEM],
         cost_estimate=lasting(3),
     )(mine, other, centroids)
+
+    def gather(share, apart):
+        half = share.shape[0] // 2
+        return share[:half] + exchange(share[half:], apart)
+
     block_set = pltpu.VMEM((per * BLOCK2, width), bf16)
-    packed = pltpu.VMEM((2, per, 4 * cap, width), bf16)
+    packed = pltpu.VMEM((3, per, 4 * cap, width), bf16)
     early = call(
         functools.partial(early_kernel, cap, per),
-        shape((16, 4 * cap), f32),
-        [room(rows_of(4))] * 2 + [room(rows_of(2))] * 2 + [block_set] * 2 + [packed, pltpu.SemaphoreType.DMA((6,))],
-        in_specs=[VMEM, VMEM, HBM] + [ANY] * 5,
-        cost_estimate=lasting(5),
-    )(scaled, facts, centroids2, near_set, rows0, rows1, early2, early3)
-    kept = shape((per, 4 * cap, width), bf16)
-    later, kept_rows = call(
+        shape((24, 4 * cap), f32),
+        [room(rows_of(4))] * 2 + [room(rows_of(3))] * 2 + [block_set] * 3 + [packed, pltpu.SemaphoreType.DMA((7,))],
+        in_specs=[VMEM, VMEM, HBM] + [ANY] * 7,
+        cost_estimate=lasting(7),
+    )(scaled, facts, centroids2, near_set, cross_set, passed, rows0, rows1, early2, early3)
+    share, early = in_order(gather(share, 1), early)
+    kept = shape((1, per, 4 * cap, width), bf16)
+    kept_rows = call(
         functools.partial(late_kernel, cap, per),
-        (shape((8, 4 * cap), f32), kept),
-        [room(rows_of(2))] * 4 + [block_set, packed, pltpu.SemaphoreType.DMA((5,))],
-        in_specs=[VMEM, VMEM] + [ANY] * 7,
-        cost_estimate=lasting(LATE),
-    )(scaled, facts, cross_set, passed, rows0, rows1, late2, late3, early)
-    results = call(
+        kept,
+        [room(rows_of(1))] * 4 + [pltpu.SemaphoreType.DMA((4,))],
+        in_specs=[VMEM] * 2 + [ANY] * 5,
+        cost_estimate=lasting(3),
+    )(scaled, facts, rows0, rows1, late2, late3, early)
+    share, kept_rows = in_order(gather(share, 2), kept_rows)
+    tile = shape((8, 4 * cap), f32)
+    tiles = call(
         functools.partial(third_kernel, cap, per),
-        shape((16, 8, 4 * cap), f32),
+        (tile,) * 4,
         [room(kept), block_set, pltpu.SemaphoreType.DMA((2,))],
-        in_specs=[VMEM, VMEM, VMEM, ANY, ANY, ANY],
+        in_specs=[VMEM, ANY, ANY, ANY],
         cost_estimate=lasting(1),
-    )(early, later, share, kept_rows, last_set, far_set)
+    )(early, kept_rows, last_set, far_set)
+    share, *tiles = in_order(gather(share, 12), *tiles)
     new_centroids, counts = call(
         update_kernel, (shape((rows, width), bf16), shape((1, rows), i32)), in_specs=[ANY] + [VMEM] * 4
-    )(results, scaled, facts, centroids, prior_row)
-    results = lax.all_to_all(results, "shard", split_axis=0, concat_axis=0, tiled=True)
+    )(tiles[0], scaled, facts, centroids, prior_row)
+    tiles = [tile if r == 0 else exchange(tile, r) for r, tile in enumerate(tiles)]
+    share = gather(share, 4)
     density, level_two = call(
         functools.partial(last_kernel, cap, probe_count * BLOCK, BLOCK2), (shape((1, emb_rows), f32), shape((1, rows), f32))
-    )(info, results)
+    )(info, *tiles, share)
     return (density.reshape(-1), new_centroids, counts.reshape(-1), level_two.reshape(-1))
 
 

time: 88.3 us -> 86.5 us (0.980)
  waiting for transfers between devices: 38.3 us -> 33 us
  Pallas kernels: 24.5 us -> 26 us
  local copies, waits for them, and re-layouts: 0.01 us -> 1.08 us
    ppermute x14 -> x21, starting transfers between devices: 20.7 us -> 25.1 us  [exchange(): return lax.ppermute(value, 'shard', [(i, i ^ apart) for i in sources])]
    all_to_all x1 -> x0, starting transfers between devices: 3.51 us -> none  [line_body(): lax.all_to_all(results, 'shard', split_axis=0, concat_axis=0, tiled=True)]
    all_to_all x1 -> x0, waiting for transfers between devices: 3.27 us -> none  [line_body(): lax.all_to_all(results, 'shard', split_axis=0, concat_axis=0, tiled=True)]
    ppermute x14 -> x21, waiting for transfers between devices: 35 us -> 33 us  [exchange(): return lax.ppermute(value, 'shard', [(i, i ^ apart) for i in sources])]
    pallas_call x11 -> x14, Pallas kernels: 24.5 us -> 26 us  [run(): pl.pallas_call(kernel, out_shape=outs, in_specs=specs, scratch_shapes=lis...]
    unnamed x4 -> x8, local copies, waits for them, and re-layouts: 0.01 us -> 1.06 us
  transfers between devices with their start and end apart: 15 -> 21, of which waited for: 8 -> 7; matrix products, arithmetic and copies ran while one was open for 0% -> 0% of each run, Pallas kernels for 25% -> 28%
where the time goes in v3:
time: 86.5 us; the launch traced here: 86.2 us
  waiting for transfers between devices  33 us (38%)
  Pallas kernels  26 us (30%)
  starting transfers between devices  25.1 us (29%)
  local copies, waits for them, and re-layouts  1.08 us (1%)
  between operations  0.92 us (1%)
    ppermute x21, waiting for transfers between devices, exchange(): return lax.ppermute(value, 'shard', [(i, i ^ apart) for i in sources])  33 us
    pallas_call x14, Pallas kernels, run(): pl.pallas_call(kernel, out_shape=outs, in_specs=specs, scratch_shapes=lis...  26 us
    ppermute x21, starting transfers between devices, exchange(): return lax.ppermute(value, 'shard', [(i, i ^ apart) for i in sources])  25.1 us
  transfers between devices with their start and end apart: 21, of which 7 were waited for; matrix products, arithmetic and copies ran while one was open for 0% of the time, Pallas kernels for 28%

profile of v3, /device:TPU:0, one launch (start us, length us, event | category | flops | bytes accessed | tf_op | source)
XLA Modules:
  0.0 86.2 jit_solution(17420627849944267219)
XLA Ops:
  0.6 0.0 copy-start
  0.6 0.0 copy-start.3
  0.7 3.1 %collective-permute-start = (bf16[384,1024]{1,0:T(8,128)(2,1)}, bf16[384,1024]{1,0:T(8,128)(2,1)S(1)}, u32[]{:S(2)}, u32[]{:S(2)}) collective-permute-start(bf16[384,1024]{1,0:T(8,128)(2,1)} %own_any.1), channel_id=1, source_target_pairs={{0,4},{1,5},{2,6},{3,7},{4,0},{5,1},{6,2},{7,3},{8,12},{9,13},{10,... | collective-permute-start | bytes 2359304 | tf_op jit(solution)/shard_map/ppermute | solution.py:444
  3.7 0.7 collective-permute-start.1
  4.4 3.4 %shard_map.102 = (bf16[40,1152]{1,0:T(8,128)(2,1)S(1)}, bf16[304,1024]{1,0:T(8,128)(2,1)S(1)}, bf16[304,1024]{1,0:T(8,128)(2,1)S(1)}, s32[8,1024]{1,0:T(8,128)S(1)}) custom-call(s32[1,1024]{1,0:T(1,128)} %bitcast.10, bf16[40,1024]{1,0:T(8,128)(2,1)} %emb_any.1, s32[8,40]{1,0:T(8,128)} %bitcast.11, s32[1,40]{1,0:T(1,128)} %bitcast.12, s32[1,1024]{1,0:T(1,128)} %bitcast.7, ...), custom_call_target="tpu_custom_call" | custom-call | tf_op jit(solution)/shard_map/pallas_call | solution.py:410
  7.8 4.4 %collective-permute-start.2 = (bf16[40,1152]{1,0:T(8,128)(2,1)S(1)}, bf16[40,1152]{1,0:T(8,128)(2,1)S(1)}, u32[]{:S(2)}, u32[]{:S(2)}) collective-permute-start(bf16[40,1152]{1,0:T(8,128)(2,1)S(1)} %get-tuple-element.46), channel_id=1, source_target_pairs={{0,4},{1,5},{2,6},{3,7},{4,0},{5,1},{6,2},{7,3},{8,12},{9,13},{10,... | collective-permute-start | bytes 276488 | tf_op jit(solution)/shard_map/ppermute | solution.py:444
  12.2 1.5 %collective-permute-start.6 = (bf16[304,1024]{1,0:T(8,128)(2,1)S(1)}, bf16[304,1024]{1,0:T(8,128)(2,1)S(1)}, u32[]{:S(2)}, u32[]{:S(2)}) collective-permute-start(bf16[304,1024]{1,0:T(8,128)(2,1)S(1)} %get-tuple-element.51), channel_id=1, source_target_pairs={{0,2},{1,3},{2,0},{3,1},{4,6},{5,7},{6,4},{7,5},{8,10},{9,11},{10,... | collective-permute-start | bytes 1867784 | tf_op jit(solution)/shard_map/ppermute | solution.py:444
  13.8 0.0 collective-permute-start.7
  13.8 0.0 copy-done
  13.8 0.0 copy-done.3
  13.8 2.9 %shard_map.103 = (bf16[400,1024]{1,0:T(8,128)(2,1)S(1)}, bf16[400,1024]{1,0:T(8,128)(2,1)S(1)}, bf16[112,1024]{1,0:T(8,128)(2,1)S(1)}, bf16[112,1024]{1,0:T(8,128)(2,1)S(1)}) custom-call(s32[8,1024]{1,0:T(8,128)S(1)} %get-tuple-element.45.info, s32[1,1024]{1,0:T(1,128)S(1)} %bitcast.8, bf16[1024,1024]{1,0:T(8,128)(2,1)S(1)} %copy-done), custom_call_target="tpu_custom_call" | custom-call | tf_op jit(solution)/shard_map/pallas_call | solution.py:410
  16.7 6.7 %collective-permute-done.2 = bf16[40,1152]{1,0:T(8,128)(2,1)S(1)} collective-permute-done((bf16[40,1152]{1,0:T(8,128)(2,1)S(1)}, bf16[40,1152]{1,0:T(8,128)(2,1)S(1)}, u32[]{:S(2)}, u32[]{:S(2)}) %collective-permute-start.2) | collective-permute-done | bytes 92192 | tf_op jit(solution)/shard_map/ppermute | solution.py:444
  23.5 0.0 collective-permute-done.refs_0_
  23.5 0.0 collective-permute-done.1.refs_1_
  23.5 3.8 %collective-permute-start.5 = (bf16[80,1152]{1,0:T(8,128)(2,1)S(1)}, bf16[80,1152]{1,0:T(8,128)(2,1)S(1)}, u32[]{:S(2)}, u32[]{:S(2)}) collective-permute-start(bf16[80,1152]{1,0:T(8,128)(2,1)S(1)} %get-tuple-element.50), channel_id=1, source_target_pairs={{0,12},{1,13},{2,14},{3,15},{4,8},{5,9},{6,10},{7,11},{8,4},{9,5},... | collective-permute-start | bytes 552968 | tf_op jit(solution)/shard_map/ppermute | solution.py:444
  27.4 1.3 %collective-permute-start.3 = (bf16[384,1024]{1,0:T(8,128)(2,1)S(1)}, bf16[384,1024]{1,0:T(8,128)(2,1)S(1)}, u32[]{:S(2)}, u32[]{:S(2)}) collective-permute-start(bf16[384,1024]{1,0:T(8,128)(2,1)S(1)} %get-tuple-element.48.cross_any), channel_id=1, source_target_pairs={{4,0},{5,1},{6,2},{7,3},{8,12},{9,13},{10,14},{11,15},{20,16},{21,... | collective-permute-start | bytes 2359304 | tf_op jit(solution)/shard_map/ppermute | solution.py:444
  28.6 0.7 collective-permute-start.4
  29.4 2.0 %collective-permute-done.5 = bf16[80,1152]{1,0:T(8,128)(2,1)S(1)} collective-permute-done((bf16[80,1152]{1,0:T(8,128)(2,1)S(1)}, bf16[80,1152]{1,0:T(8,128)(2,1)S(1)}, u32[]{:S(2)}, u32[]{:S(2)}) %collective-permute-start.5) | collective-permute-done | bytes 184352 | tf_op jit(solution)/shard_map/ppermute | solution.py:444
  31.4 0.0 collective-permute-done.6.refs_1_
  31.4 8.1 %collective-permute-done.7.refs_2_ = bf16[304,1024]{1,0:T(8,128)(2,1)S(1)} collective-permute-done((bf16[304,1024]{1,0:T(8,128)(2,1)S(1)}, bf16[304,1024]{1,0:T(8,128)(2,1)S(1)}, u32[]{:S(2)}, u32[]{:S(2)}) %collective-permute-start.7) | collective-permute-done | bytes 622624 | tf_op jit(solution)/shard_map/ppermute | solution.py:444
  39.6 0.5 collective-permute-start.8
  40.1 1.8 %collective-permute-start.11 = (bf16[400,1024]{1,0:T(8,128)(2,1)S(1)}, bf16[400,1024]{1,0:T(8,128)(2,1)S(1)}, u32[]{:S(2)}, u32[]{:S(2)}) collective-permute-start(bf16[400,1024]{1,0:T(8,128)(2,1)S(1)} %get-tuple-element.63), channel_id=1, source_target_pairs={{0,1},{1,0},{2,3},{3,2},{4,5},{5,4},{6,7},{7,6},{8,9},{9,8},{10,11... | collective-permute-start | bytes 2457608 | tf_op jit(solution)/shard_map/ppermute | solution.py:444
  41.9 9.0 %collective-permute-done.8 = bf16[160,1152]{1,0:T(8,128)(2,1)S(1)} collective-permute-done((bf16[160,1152]{1,0:T(8,128)(2,1)S(1)}, bf16[160,1152]{1,0:T(8,128)(2,1)S(1)}, u32[]{:S(2)}, u32[]{:S(2)}) %collective-permute-start.8) | collective-permute-done | bytes 368672 | tf_op jit(solution)/shard_map/ppermute | solution.py:444
  50.9 0.1 pad_maximum_fusion.refs_2_
  51.0 0.0 collective-permute-done.3.refs_0_
  51.0 0.0 collective-permute-done.4.refs_1_
  51.0 0.2 collective-permute-start.9
  51.2 1.3 %collective-permute-start.16 = (bf16[384,1024]{1,0:T(8,128)(2,1)S(1)}, bf16[384,1024]{1,0:T(8,128)(2,1)S(1)}, u32[]{:S(2)}, u32[]{:S(2)}) collective-permute-start(bf16[384,1024]{1,0:T(8,128)(2,1)S(1)} %get-tuple-element.72.last_any), channel_id=1, source_target_pairs={{4,0},{5,1},{6,2},{7,3},{8,12},{9,13},{10,14},{11,15},{20,16},{21,... | collective-permute-start | bytes 2359304 | tf_op jit(solution)/shard_map/ppermute | solution.py:444
  52.5 0.8 collective-permute-done.9.other_any
  53.3 3.2 %shard_map.107 = (bf16[640,1024]{1,0:T(8,128)(2,1)S(1)}, s32[16,640]{1,0:T(8,128)S(1)}, f32[16,128]{1,0:T(8,128)S(1)}) custom-call(bf16[320,1152]{1,0:T(8,128)(2,1)S(1)} %get-tuple-element.57.mine_any, bf16[320,1152]{1,0:T(8,128)(2,1)S(1)} %collective-permute-done.9.other_any, bf16[1024,1024]{1,0:T(8,128)(2,1)S(1)} %copy-done), custom_call_target="tpu_custom_call" | custom-call | bytes 11070000 | tf_op jit(solution)/shard_map/pallas_call | solution.py:410
  56.5 0.0 copy-start.1
  56.5 1.0 %copy-done.1 = bf16[640,1024]{1,0:T(8,128)(2,1)} copy-done((bf16[640,1024]{1,0:T(8,128)(2,1)}, bf16[640,1024]{1,0:T(8,128)(2,1)S(1)}, u32[]{:S(2)}) %copy-start.1) | copy-done | bytes 1310744
  57.6 0.1 collective-permute-start.10
  57.7 0.3 collective-permute-start.13
  58.0 1.4 %collective-permute-start.14 = (bf16[112,1024]{1,0:T(8,128)(2,1)S(1)}, bf16[112,1024]{1,0:T(8,128)(2,1)S(1)}, u32[]{:S(2)}, u32[]{:S(2)}) collective-permute-start(bf16[112,1024]{1,0:T(8,128)(2,1)S(1)} %get-tuple-element.68), channel_id=1, source_target_pairs={{0,3},{1,2},{2,1},{3,0},{4,7},{5,6},{6,5},{7,4},{8,11},{9,10},{10,... | collective-permute-start | bytes 688136 | tf_op jit(solution)/shard_map/ppermute | solution.py:444
  59.5 0.0 collective-permute-done.11.any1
  59.5 0.0 copy-start.2
  59.5 7.9 %shard_map.108.refs_1_ = f32[24,128]{1,0:T(8,128)S(1)} custom-call(bf16[640,1024]{1,0:T(8,128)(2,1)} %copy-done.1, s32[16,640]{1,0:T(8,128)S(1)} %get-tuple-element.60.facts_in.facts, bf16[384,1024]{1,0:T(8,128)(2,1)} %own_any.1, bf16[384,1024]{1,0:T(8,128)(2,1)S(1)} %get-tuple-element.49.near_any, bf16[384,1024]{1,0:T(8,128)(2,1)S(1)} %get-tuple-element.48.cross_any, ...), custom_call_target="tpu_custom_call" | custom-call | bytes 25830000 | tf_op jit(solution)/shard_map/pallas_call | solution.py:410
  67.4 0.0 collective-permute-done.10
  67.4 0.4 collective-permute-start.12
  67.9 0.0 collective-permute-done.13.any2
  67.9 2.1 %collective-permute-done.14.any3 = bf16[112,1024]{1,0:T(8,128)(2,1)S(1)} collective-permute-done((bf16[112,1024]{1,0:T(8,128)(2,1)S(1)}, bf16[112,1024]{1,0:T(8,128)(2,1)S(1)}, u32[]{:S(2)}, u32[]{:S(2)}) %collective-permute-start.14) | collective-permute-done | bytes 229408 | tf_op jit(solution)/shard_map/ppermute | solution.py:444
  70.0 0.0 copy-done.2
  70.0 3.0 %shard_map.110.refs_1_ = bf16[1,3,128,1024]{3,2,1,0:T(8,128)(2,1)S(1)} custom-call(bf16[640,1024]{1,0:T(8,128)(2,1)S(1)} %copy-done.2, s32[16,640]{1,0:T(8,128)S(1)} %get-tuple-element.60.facts_in.facts, bf16[400,1024]{1,0:T(8,128)(2,1)S(1)} %get-tuple-element.62.any0, bf16[400,1024]{1,0:T(8,128)(2,1)S(1)} %collective-permute-done.11.any1, ...), custom_call_target="tpu_custom_call" | custom-call | bytes 11070000 | tf_op jit(solution)/shard_map/pallas_call | solution.py:410
  72.9 0.0 collective-permute-done.12
  73.0 1.3 %collective-permute-start.15 = (f32[2,128]{1,0:T(2,128)S(1)}, f32[2,128]{1,0:T(2,128)S(1)}, u32[]{:S(2)}, u32[]{:S(2)}) collective-permute-start(f32[2,128]{1,0:T(2,128)S(1)} %slice.29), channel_id=1, source_target_pairs={{0,12},{1,13},{2,14},{3,15},{4,8},{5,9},{6,10},{7,11},{8,4},{9,5},... | collective-permute-start | bytes 3080 | tf_op jit(solution)/shard_map/ppermute | solution.py:444
  74.2 4.2 %collective-permute-done.15 = f32[2,128]{1,0:T(2,128)S(1)} collective-permute-done((f32[2,128]{1,0:T(2,128)S(1)}, f32[2,128]{1,0:T(2,128)S(1)}, u32[]{:S(2)}, u32[]{:S(2)}) %collective-permute-start.15) | collective-permute-done | bytes 1056 | tf_op jit(solution)/shard_map/ppermute | solution.py:444
  78.4 0.0 collective-permute-done.16.far_any
  78.4 0.9 %shard_map.112 = (f32[8,128]{1,0:T(8,128)S(1)}, f32[8,128]{1,0:T(8,128)S(1)}, f32[8,128]{1,0:T(8,128)S(1)}, f32[8,128]{1,0:T(8,128)S(1)}) custom-call(f32[24,128]{1,0:T(8,128)S(1)} %get-tuple-element.69.after.early, bf16[1,3,128,1024]{3,2,1,0:T(8,128)(2,1)S(1)} %get-tuple-element.71.kept_any, bf16[384,1024]{1,0:T(8,128)(2,1)S(1)} %get-tuple-element.72.last_any, ...), custom_call_target="tpu_custom_call" | custom-call | bytes 3690000 | tf_op jit(solution)/shard_map/pallas_call | solution.py:410
  79.3 0.3 collective-permute-start.20
  79.6 0.0 collective-permute-start.17
  79.6 0.9 %collective-permute-start.18 = (f32[8,128]{1,0:T(8,128)S(1)}, f32[8,128]{1,0:T(8,128)S(1)}, u32[]{:S(2)}, u32[]{:S(2)}) collective-permute-start(f32[8,128]{1,0:T(8,128)S(1)} %get-tuple-element.79), channel_id=1, source_target_pairs={{0,2},{1,3},{2,0},{3,1},{4,6},{5,7},{6,4},{7,5},{8,10},{9,11},{10,... | collective-permute-start | bytes 12296 | tf_op jit(solution)/shard_map/ppermute | solution.py:444
  80.5 0.9 %collective-permute-start.19 = (f32[8,128]{1,0:T(8,128)S(1)}, f32[8,128]{1,0:T(8,128)S(1)}, u32[]{:S(2)}, u32[]{:S(2)}) collective-permute-start(f32[8,128]{1,0:T(8,128)S(1)} %get-tuple-element.80), channel_id=1, source_target_pairs={{0,3},{1,2},{2,1},{3,0},{4,7},{5,6},{6,5},{7,4},{8,11},{9,10},{10,... | collective-permute-start | bytes 12296 | tf_op jit(solution)/shard_map/ppermute | solution.py:444
  81.5 3.7 %shard_map.115 = (bf16[1024,1024]{1,0:T(8,128)(2,1)}, s32[1,1024]{1,0:T(1,128)}) custom-call(f32[8,128]{1,0:T(8,128)S(1)} %get-tuple-element.77.got0.after, bf16[640,1024]{1,0:T(8,128)(2,1)S(1)} %copy-done.2, s32[16,640]{1,0:T(8,128)S(1)} %get-tuple-element.60.facts_in.facts, bf16[1024,1024]{1,0:T(8,128)(2,1)S(1)} %copy-done, s32[1,1024]{1,0:T(1,128)S(1)} %bitcast.9), custom_call_target="tpu_custom_call" | custom-call | tf_op jit(solution)/shard_map/pallas_call | solution.py:410
  85.2 0.0 collective-permute-done.20
  85.2 0.0 collective-permute-done.17.got1
  85.2 0.0 collective-permute-done.18.got2
  85.2 0.0 collective-permute-done.19.got3
  85.2 1.0 %shard_map.114 = (f32[1,40]{1,0:T(1,128)}, f32[1,1024]{1,0:T(1,128)}) custom-call(s32[8,1024]{1,0:T(8,128)S(1)} %get-tuple-element.45.info, f32[8,128]{1,0:T(8,128)S(1)} %get-tuple-element.77.got0.after, f32[8,128]{1,0:T(8,128)S(1)} %collective-permute-done.17.got1, f32[8,128]{1,0:T(8,128)S(1)} %collective-permute-done.18.got2, ...), custom_call_target="tpu_custom_call" | custom-call | tf_op jit(solution)/shard_map/pallas_call | solution.py:410
  (16 shorter events, 0.1 us)
Async XLA Ops:
  0.6 13.1 %copy-start = (bf16[1024,1024]{1,0:T(8,128)(2,1)S(1)}, bf16[1024,1024]{1,0:T(8,128)(2,1)}, u32[]{:S(2)}) copy-start(bf16[1024,1024]{1,0:T(8,128)(2,1)} %cent_ref.5) | copy-start | bytes 6291460
  0.6 13.1 %copy-start.3 = (s32[1024]{0:T(1024)S(1)}, s32[1024]{0:T(1024)}, u32[]{:S(2)}) copy-start(s32[1024]{0:T(1024)} %param.10) | copy-start | bytes 12292
  0.7 22.8 %collective-permute-start = (bf16[384,1024]{1,0:T(8,128)(2,1)}, bf16[384,1024]{1,0:T(8,128)(2,1)S(1)}, u32[]{:S(2)}, u32[]{:S(2)}) collective-permute-start(bf16[384,1024]{1,0:T(8,128)(2,1)} %own_any.1), channel_id=1, source_target_pairs={{0,4},{1,5},{2,6},{3,7},{4,0},{5,1},{6,2},{7,3},{8,12},{9,13},{10,... | collective-permute-start | bytes 2359304 | tf_op jit(solution)/shard_map/ppermute | solution.py:444
  3.7 19.8 %collective-permute-start.1 = (bf16[384,1024]{1,0:T(8,128)(2,1)}, bf16[384,1024]{1,0:T(8,128)(2,1)S(1)}, u32[]{:S(2)}, u32[]{:S(2)}) collective-permute-start(bf16[384,1024]{1,0:T(8,128)(2,1)} %own_any.1), channel_id=1, source_target_pairs={{4,8},{5,9},{6,10},{7,11},{8,4},{9,5},{10,6},{11,7},{20,24},{21,25... | collective-permute-start | bytes 2359304 | tf_op jit(solution)/shard_map/ppermute | solution.py:444
  7.8 15.6 %collective-permute-start.2 = (bf16[40,1152]{1,0:T(8,128)(2,1)S(1)}, bf16[40,1152]{1,0:T(8,128)(2,1)S(1)}, u32[]{:S(2)}, u32[]{:S(2)}) collective-permute-start(bf16[40,1152]{1,0:T(8,128)(2,1)S(1)} %get-tuple-element.46), channel_id=1, source_target_pairs={{0,4},{1,5},{2,6},{3,7},{4,0},{5,1},{6,2},{7,3},{8,12},{9,13},{10,... | collective-permute-start | bytes 276488 | tf_op jit(solution)/shard_map/ppermute | solution.py:444
  12.2 19.2 %collective-permute-start.6 = (bf16[304,1024]{1,0:T(8,128)(2,1)S(1)}, bf16[304,1024]{1,0:T(8,128)(2,1)S(1)}, u32[]{:S(2)}, u32[]{:S(2)}) collective-permute-start(bf16[304,1024]{1,0:T(8,128)(2,1)S(1)} %get-tuple-element.51), channel_id=1, source_target_pairs={{0,2},{1,3},{2,0},{3,1},{4,6},{5,7},{6,4},{7,5},{8,10},{9,11},{10,... | collective-permute-start | bytes 1867784 | tf_op jit(solution)/shard_map/ppermute | solution.py:444
  13.8 25.8 %collective-permute-start.7 = (bf16[304,1024]{1,0:T(8,128)(2,1)S(1)}, bf16[304,1024]{1,0:T(8,128)(2,1)S(1)}, u32[]{:S(2)}, u32[]{:S(2)}) collective-permute-start(bf16[304,1024]{1,0:T(8,128)(2,1)S(1)} %get-tuple-element.52), channel_id=1, source_target_pairs={{0,3},{1,2},{2,1},{3,0},{4,7},{5,6},{6,5},{7,4},{8,11},{9,10},{10,... | collective-permute-start | bytes 1867784 | tf_op jit(solution)/shard_map/ppermute | solution.py:444
  23.5 7.9 %collective-permute-start.5 = (bf16[80,1152]{1,0:T(8,128)(2,1)S(1)}, bf16[80,1152]{1,0:T(8,128)(2,1)S(1)}, u32[]{:S(2)}, u32[]{:S(2)}) collective-permute-start(bf16[80,1152]{1,0:T(8,128)(2,1)S(1)} %get-tuple-element.50), channel_id=1, source_target_pairs={{0,12},{1,13},{2,14},{3,15},{4,8},{5,9},{6,10},{7,11},{8,4},{9,5},... | collective-permute-start | bytes 552968 | tf_op jit(solution)/shard_map/ppermute | solution.py:444
  27.4 23.6 %collective-permute-start.3 = (bf16[384,1024]{1,0:T(8,128)(2,1)S(1)}, bf16[384,1024]{1,0:T(8,128)(2,1)S(1)}, u32[]{:S(2)}, u32[]{:S(2)}) collective-permute-start(bf16[384,1024]{1,0:T(8,128)(2,1)S(1)} %get-tuple-element.48.cross_any), channel_id=1, source_target_pairs={{4,0},{5,1},{6,2},{7,3},{8,12},{9,13},{10,14},{11,15},{20,16},{21,... | collective-permute-start | bytes 2359304 | tf_op jit(solution)/shard_map/ppermute | solution.py:444
  28.6 22.4 %collective-permute-start.4 = (bf16[384,1024]{1,0:T(8,128)(2,1)S(1)}, bf16[384,1024]{1,0:T(8,128)(2,1)S(1)}, u32[]{:S(2)}, u32[]{:S(2)}) collective-permute-start(bf16[384,1024]{1,0:T(8,128)(2,1)S(1)} %get-tuple-element.49.near_any), channel_id=1, source_target_pairs={{4,8},{5,9},{6,10},{7,11},{8,4},{9,5},{10,6},{11,7},{20,24},{21,25... | collective-permute-start | bytes 2359304 | tf_op jit(solution)/shard_map/ppermute | solution.py:444
  39.6 11.4 %collective-permute-start.8 = (bf16[160,1152]{1,0:T(8,128)(2,1)S(1)}, bf16[160,1152]{1,0:T(8,128)(2,1)S(1)}, u32[]{:S(2)}, u32[]{:S(2)}) collective-permute-start(bf16[160,1152]{1,0:T(8,128)(2,1)S(1)} %get-tuple-element.56), channel_id=1, source_target_pairs={{0,2},{1,3},{2,0},{3,1},{4,6},{5,7},{6,4},{7,5},{8,10},{9,11},{10,... | collective-permute-start | bytes 1105928 | tf_op jit(solution)/shard_map/ppermute | solution.py:444
  40.1 19.4 %collective-permute-start.11 = (bf16[400,1024]{1,0:T(8,128)(2,1)S(1)}, bf16[400,1024]{1,0:T(8,128)(2,1)S(1)}, u32[]{:S(2)}, u32[]{:S(2)}) collective-permute-start(bf16[400,1024]{1,0:T(8,128)(2,1)S(1)} %get-tuple-element.63), channel_id=1, source_target_pairs={{0,1},{1,0},{2,3},{3,2},{4,5},{5,4},{6,7},{7,6},{8,9},{9,8},{10,11... | collective-permute-start | bytes 2457608 | tf_op jit(solution)/shard_map/ppermute | solution.py:444
  51.0 2.3 %collective-permute-start.9 = (bf16[320,1152]{1,0:T(8,128)(2,1)S(1)}, bf16[320,1152]{1,0:T(8,128)(2,1)S(1)}, u32[]{:S(2)}, u32[]{:S(2)}) collective-permute-start(bf16[320,1152]{1,0:T(8,128)(2,1)S(1)} %get-tuple-element.57.mine_any), channel_id=1, source_target_pairs={{0,1},{1,0},{2,3},{3,2},{4,5},{5,4},{6,7},{7,6},{8,9},{9,8},{10,11... | collective-permute-start | bytes 2211848 | tf_op jit(solution)/shard_map/ppermute | solution.py:444
  51.2 27.2 %collective-permute-start.16 = (bf16[384,1024]{1,0:T(8,128)(2,1)S(1)}, bf16[384,1024]{1,0:T(8,128)(2,1)S(1)}, u32[]{:S(2)}, u32[]{:S(2)}) collective-permute-start(bf16[384,1024]{1,0:T(8,128)(2,1)S(1)} %get-tuple-element.72.last_any), channel_id=1, source_target_pairs={{4,0},{5,1},{6,2},{7,3},{8,12},{9,13},{10,14},{11,15},{20,16},{21,... | collective-permute-start | bytes 2359304 | tf_op jit(solution)/shard_map/ppermute | solution.py:444
  56.5 1.1 %copy-start.1 = (bf16[640,1024]{1,0:T(8,128)(2,1)}, bf16[640,1024]{1,0:T(8,128)(2,1)S(1)}, u32[]{:S(2)}) copy-start(bf16[640,1024]{1,0:T(8,128)(2,1)S(1)} %get-tuple-element.59.scaled) | copy-start | bytes 3932164
  57.6 9.8 %collective-permute-start.10 = (f32[8,128]{1,0:T(8,128)S(1)}, f32[8,128]{1,0:T(8,128)S(1)}, u32[]{:S(2)}, u32[]{:S(2)}) collective-permute-start(f32[8,128]{1,0:T(8,128)S(1)} %slice.25), channel_id=1, source_target_pairs={{0,1},{1,0},{2,3},{3,2},{4,5},{5,4},{6,7},{7,6},{8,9},{9,8},{10,11... | collective-permute-start | bytes 12296 | tf_op jit(solution)/shard_map/ppermute | solution.py:444
  57.7 10.1 %collective-permute-start.13 = (bf16[112,1024]{1,0:T(8,128)(2,1)S(1)}, bf16[112,1024]{1,0:T(8,128)(2,1)S(1)}, u32[]{:S(2)}, u32[]{:S(2)}) collective-permute-start(bf16[112,1024]{1,0:T(8,128)(2,1)S(1)} %get-tuple-element.67), channel_id=1, source_target_pairs={{0,2},{1,3},{2,0},{3,1},{4,6},{5,7},{6,4},{7,5},{8,10},{9,11},{10,... | collective-permute-start | bytes 688136 | tf_op jit(solution)/shard_map/ppermute | solution.py:444
  58.0 11.9 %collective-permute-start.14 = (bf16[112,1024]{1,0:T(8,128)(2,1)S(1)}, bf16[112,1024]{1,0:T(8,128)(2,1)S(1)}, u32[]{:S(2)}, u32[]{:S(2)}) collective-permute-start(bf16[112,1024]{1,0:T(8,128)(2,1)S(1)} %get-tuple-element.68), channel_id=1, source_target_pairs={{0,3},{1,2},{2,1},{3,0},{4,7},{5,6},{6,5},{7,4},{8,11},{9,10},{10,... | collective-permute-start | bytes 688136 | tf_op jit(solution)/shard_map/ppermute | solution.py:444
  59.5 10.5 %copy-start.2 = (bf16[640,1024]{1,0:T(8,128)(2,1)S(1)}, bf16[640,1024]{1,0:T(8,128)(2,1)}, u32[]{:S(2)}) copy-start(bf16[640,1024]{1,0:T(8,128)(2,1)} %copy-done.1) | copy-start | bytes 3932164
  67.4 5.5 %collective-permute-start.12 = (f32[4,128]{1,0:T(4,128)S(1)}, f32[4,128]{1,0:T(4,128)S(1)}, u32[]{:S(2)}, u32[]{:S(2)}) collective-permute-start(f32[4,128]{1,0:T(4,128)S(1)} %slice.27), channel_id=1, source_target_pairs={{0,2},{1,3},{2,0},{3,1},{4,6},{5,7},{6,4},{7,5},{8,10},{9,11},{10,... | collective-permute-start | bytes 6152 | tf_op jit(solution)/shard_map/ppermute | solution.py:444
  73.0 5.4 %collective-permute-start.15 = (f32[2,128]{1,0:T(2,128)S(1)}, f32[2,128]{1,0:T(2,128)S(1)}, u32[]{:S(2)}, u32[]{:S(2)}) collective-permute-start(f32[2,128]{1,0:T(2,128)S(1)} %slice.29), channel_id=1, source_target_pairs={{0,12},{1,13},{2,14},{3,15},{4,8},{5,9},{6,10},{7,11},{8,4},{9,5},... | collective-permute-start | bytes 3080 | tf_op jit(solution)/shard_map/ppermute | solution.py:444
  79.3 5.9 %collective-permute-start.20 = (f32[1,128]{1,0:T(1,128)S(1)}, f32[1,128]{1,0:T(1,128)S(1)}, u32[]{:S(2)}, u32[]{:S(2)}) collective-permute-start(f32[1,128]{1,0:T(1,128)S(1)} %slice.31), channel_id=1, source_target_pairs={{0,4},{1,5},{2,6},{3,7},{4,0},{5,1},{6,2},{7,3},{8,12},{9,13},{10,... | collective-permute-start | bytes 1544 | tf_op jit(solution)/shard_map/ppermute | solution.py:444
  79.6 5.6 %collective-permute-start.17 = (f32[8,128]{1,0:T(8,128)S(1)}, f32[8,128]{1,0:T(8,128)S(1)}, u32[]{:S(2)}, u32[]{:S(2)}) collective-permute-start(f32[8,128]{1,0:T(8,128)S(1)} %get-tuple-element.78), channel_id=1, source_target_pairs={{0,1},{1,0},{2,3},{3,2},{4,5},{5,4},{6,7},{7,6},{8,9},{9,8},{10,11... | collective-permute-start | bytes 12296 | tf_op jit(solution)/shard_map/ppermute | solution.py:444
  79.6 5.6 %collective-permute-start.18 = (f32[8,128]{1,0:T(8,128)S(1)}, f32[8,128]{1,0:T(8,128)S(1)}, u32[]{:S(2)}, u32[]{:S(2)}) collective-permute-start(f32[8,128]{1,0:T(8,128)S(1)} %get-tuple-element.79), channel_id=1, source_target_pairs={{0,2},{1,3},{2,0},{3,1},{4,6},{5,7},{6,4},{7,5},{8,10},{9,11},{10,... | collective-permute-start | bytes 12296 | tf_op jit(solution)/shard_map/ppermute | solution.py:444
  80.5 4.7 %collective-permute-start.19 = (f32[8,128]{1,0:T(8,128)S(1)}, f32[8,128]{1,0:T(8,128)S(1)}, u32[]{:S(2)}, u32[]{:S(2)}) collective-permute-start(f32[8,128]{1,0:T(8,128)S(1)} %get-tuple-element.80), channel_id=1, source_target_pairs={{0,3},{1,2},{2,1},{3,0},{4,7},{5,6},{6,5},{7,4},{8,11},{9,10},{10,... | collective-permute-start | bytes 12296 | tf_op jit(solution)/shard_map/ppermute | solution.py:444

commit v4 on v3

--- a/solution.py
+++ b/solution.py
@@ -1,4 +1,5 @@
 import functools
+import math
 
 import jax
 import jax.numpy as jnp
@@ -245,12 +246,25 @@
     pass
 
 
-def share_kernel(mine_any, other_any, cent_ref, scaled, facts, share, mine_ref, other_ref, sems):
+def prepare_kernel(cent_ref, own_any, near_any, unit_old, units, own, near, sems):
+    copies = fetch(((own_any, own), (near_any, near)), sems)
+    step = 256
+    for start in range(0, cent_ref.shape[0], step):
+        unit_old[start : start + step, :] = unit_wide(cent_ref[start : start + step, :].astype(jnp.float32))
+    me, z, y, core = position()
+    first = jnp.where((z == 0) | (z == 3), 0, 1)
+    copies[0].wait()
+    units[first] = unit_wide(own[...].astype(jnp.float32))
+    copies[1].wait()
+    units[1 - first] = unit_wide(near[...].astype(jnp.float32))
+
+
+def share_kernel(mine_any, other_any, unit_old, scaled, facts, share_low, share_high, mine_ref, other_ref, sems):
     copies = fetch(((mine_any, mine_ref), (other_any, other_ref)), sems)
     me, z, y, core = position()
     half = mine_ref.shape[0]
     count = 2 * half
-    rows, width = cent_ref.shape
+    rows, width = unit_old.shape
     copies[0].wait()
     scaled[0:half, :] = unit_wide(mine_ref[:, 0:width].astype(jnp.float32))
     copies[1].wait()
@@ -262,8 +276,9 @@
     step = 256
     total = jnp.zeros((1, count), jnp.float32)
     for start in range(0, rows, step):
-        old = cent_ref[start : start + step, :].astype(jnp.float32)
-        scores = lax.dot_general(unit_wide(old), scaled[...], NT, preferred_element_type=jnp.float32)
+        scores = lax.dot_general(
+            unit_old[start : start + step, :], scaled[...], NT, preferred_element_type=jnp.float32
+        )
         total = total + jnp.sum(weights(scores, width), axis=0, keepdims=True)
     piece = count // 16
     lane = lax.broadcasted_iota(jnp.int32, (16, count), 1)
@@ -272,7 +287,9 @@
     spot = lax.broadcasted_iota(jnp.int32, (count, 128), 0)
     block = sum((spot >= piece * step).astype(jnp.int32) for step in range(1, 16))
     together = jnp.where(spot - block * piece == lax.broadcasted_iota(jnp.int32, (count, 128), 1), 1.0, 0.0)
-    share[...] = jnp.dot(apart, together, precision=lax.Precision.HIGHEST, preferred_element_type=jnp.float32)
+    share = jnp.dot(apart, together, precision=lax.Precision.HIGHEST, preferred_element_type=jnp.float32)
+    share_low[...] = share[0:8, :]
+    share_high[...] = share[8:16, :]
 
 
 def update_kernel(after, scaled, facts, cent_ref, prior_ref, fresh_rows, fresh_counts):
@@ -296,66 +313,71 @@
         fresh_counts[0:1, start : start + step] = prior_ref[0:1, start : start + step] + gained_row[0:1, :].astype(jnp.int32)
 
 
-def level_sums(two, rows, per):
-    block = two.shape[0] // per
+def level_sums(two, packed, floors, w, per):
+    block, width = two.shape[0] // per, two.shape[1]
     lines = []
     for j in range(per):
-        scores = lax.dot_general(two[j * block : (j + 1) * block, :], rows(j), NT, preferred_element_type=jnp.float32)
-        lines.append(jnp.sum(weights(scores, two.shape[1]), axis=0, keepdims=True))
+        rows = packed[w, j]
+        floor = floors[w, j]
+        scores = lax.dot_general(two[j * block : (j + 1) * block, :], rows, NT, preferred_element_type=jnp.float32)
+        power = lax.dot_general(
+            jnp.ones((8, width), jnp.bfloat16), rows * rows, NT, preferred_element_type=jnp.float32
+        ) + lax.dot_general(
+            jnp.ones((8, floor.shape[1]), jnp.bfloat16), floor * floor, NT, preferred_element_type=jnp.float32
+        )
+        power = jnp.where(power > 0.0, power, 1.0) * (1.0 / width)
+        lines.append(jnp.sum(weights(scores * lax.rsqrt(power[0:1, :]), width), axis=0, keepdims=True))
     return jnp.concatenate(lines, axis=0)
 
 
-def redo(cap, per, scaled, facts_in, me, refs, firsts, packed):
+def redo(cap, per, scaled, facts_in, me, refs, firsts, packed, floors):
     part = per * cap
     planes = packed.shape[0]
     count = planes * part
+    width = scaled.shape[1]
     probe0 = facts_in[0:1, :]
     slots = facts_in[8:9, :] * 32 + facts_in[9:10, :]
+    lane = lax.broadcasted_iota(jnp.int32, (count, 128), 1)
     for r, (ref, first) in enumerate(zip(refs, firsts)):
         facts = jnp.transpose(ref[ref.shape[0] - META :, first : first + count].astype(jnp.float32))
         hits = (facts[:, 0:1] * 32.0 + facts[:, 1:2]).astype(jnp.int32) == jnp.where(probe0 == (me ^ r), slots + 1, -1)
-        hits = one_hot(hits)
-        gained = jnp.sum(hits.astype(jnp.float32), axis=1, keepdims=True)
+        gained = jnp.sum(jnp.where(hits, 1.0, 0.0), axis=1, keepdims=True)
         ahead = facts[:, 2:3]
-        fresh = jnp.maximum(ahead + gained, 1.0)
-        floor = fresh * fresh * 1e-06
-        added = jnp.dot(hits, scaled[...], preferred_element_type=jnp.float32)
-        whole = ahead * ref[0:count, :].astype(jnp.float32) + added
-        power = jnp.mean(whole * whole, axis=-1, keepdims=True) + floor
-        unit = (whole * lax.rsqrt(power)).astype(jnp.bfloat16)
+        floor = (ahead + gained) * math.sqrt(1e-06 * width)
+        floor = jnp.where(lane == 0, floor, 0.0).astype(jnp.bfloat16)
+        added = jnp.dot(one_hot(hits), scaled[...], preferred_element_type=jnp.float32)
+        whole = (ahead * ref[0:count, :].astype(jnp.float32) + added).astype(jnp.bfloat16)
         for w in range(planes):
             for j in range(per):
                 start = w * part + j * cap
-                packed[w, j, r * cap : (r + 1) * cap, :] = unit[start : start + cap, :]
+                packed[w, j, r * cap : (r + 1) * cap, :] = whole[start : start + cap, :]
+                floors[w, j, r * cap : (r + 1) * cap, :] = floor[start : start + cap, :]
 
 
 def early_kernel(
-    cap, per, scaled, facts_in, own_any, near_any, cross_any, passed_any, any0, any1, any2, any3,
-    sums, rows0, rows1, rows2, rows3, two, two_more, two_last, packed, sems,
+    cap, per, scaled, facts_in, units_any, cross_any, passed_any, any0, any1, any2, any3,
+    sums, rows0, rows1, rows2, rows3, units, two_last, packed, floors, sems,
 ):
     me, z, y, core = position()
     end = (z == 0) | (z == 3)
     refs = (rows0, rows1, rows2, rows3)
-    at_end = pltpu.make_async_copy(passed_any, two_last, sems.at[6])
-    at_mid = pltpu.make_async_copy(cross_any, two_last, sems.at[6])
-    copies = fetch(list(zip((any0, any1, any2, any3, own_any, near_any), (*refs, two, two_more))), sems)
+    at_end = pltpu.make_async_copy(passed_any, two_last, sems.at[5])
+    at_mid = pltpu.make_async_copy(cross_any, two_last, sems.at[5])
+    copies = fetch(list(zip((any0, any1, any2, any3, units_any), (*refs, units))), sems)
     pl.when(end)(at_end.start)
     pl.when(jnp.logical_not(end))(at_mid.start)
     for copy in copies:
         copy.wait()
-    redo(cap, per, scaled, facts_in, me, refs, (0, 0, 0, 0), packed)
-    own_unit = unit_wide(two[...].astype(jnp.float32))
-    near_unit = unit_wide(two_more[...].astype(jnp.float32))
-    first = jnp.where(end, 0, 1)
-    sums[pl.ds(first * 8, per), :] = level_sums(own_unit, lambda j: packed[first, j], per)
-    sums[pl.ds(8 - first * 8, per), :] = level_sums(near_unit, lambda j: packed[1 - first, j], per)
     pl.when(end)(at_end.wait)
     pl.when(jnp.logical_not(end))(at_mid.wait)
-    sums[16 : 16 + per, :] = level_sums(unit_wide(two_last[...].astype(jnp.float32)), lambda j: packed[2, j], per)
+    redo(cap, per, scaled, facts_in, me, refs, (0, 0, 0, 0), packed, floors)
+    third = unit_wide(two_last[...].astype(jnp.float32))
+    for w, two in enumerate((units[0], units[1], third)):
+        sums[8 * w : 8 * w + per, :] = level_sums(two, packed, floors, w, per)
 
 
 def late_kernel(
-    cap, per, scaled, facts_in, any0, any1, any2, any3, after, packed, rows0, rows1, rows2, rows3, sems
+    cap, per, scaled, facts_in, any0, any1, any2, any3, after, packed, floors, rows0, rows1, rows2, rows3, sems
 ):
     me, z, y, core = position()
     part = per * cap
@@ -364,10 +386,10 @@
     copies = fetch(list(zip((any0.at[tail], any1.at[tail], any2, any3), refs)), sems)
     for copy in copies:
         copy.wait()
-    redo(cap, per, scaled, facts_in, me, refs, (3 * part, 3 * part, 0, 0), packed)
-
-
-def third_kernel(cap, per, early, kept_any, last_any, far_any, out0, out1, out2, out3, kept, two, sems):
+    redo(cap, per, scaled, facts_in, me, refs, (3 * part, 3 * part, 0, 0), packed, floors)
+
+
+def third_kernel(cap, per, early, floors, kept_any, last_any, far_any, out0, out1, out2, out3, kept, two, sems):
     me, z, y, core = position()
     end = (z == 0) | (z == 3)
     at_end = pltpu.make_async_copy(far_any, two, sems.at[1])
@@ -379,7 +401,7 @@
     pl.when(jnp.logical_not(end))(at_mid.wait)
     two_unit = unit_wide(two[...].astype(jnp.float32))
     copies[0].wait()
-    final = level_sums(two_unit, lambda j: kept[0, j], per)
+    final = level_sums(two_unit, kept, floors, 0, per)
     lines = [early[8 * w : 8 * w + per, :] for w in range(3)] + [final]
     together = jnp.concatenate(lines + [jnp.zeros((16 - 4 * per, 4 * cap), jnp.float32)], axis=0)
     lane = lax.broadcasted_iota(jnp.int32, together.shape, 1)
@@ -482,54 +504,70 @@
     mine = jnp.concatenate([mine, exchange(mine, 2)], axis=0)
     late2, late3 = exchange(late2, 2), exchange(late3, 3)
     rows1 = exchange(rows1, 1)
-    passed, last_set, mine = in_order(passed, last_set, mine)
+    set_rows = per * BLOCK2
+    block_set = pltpu.VMEM((set_rows, width), bf16)
+    unit_old, units = call(
+        prepare_kernel,
+        (shape((rows, width), bf16), shape((2, set_rows, width), bf16)),
+        [block_set, block_set, pltpu.SemaphoreType.DMA((2,))],
+        in_specs=[VMEM, HBM, ANY],
+    )(centroids, centroids2, near_set)
+    passed, last_set, mine, unit_old, units = in_order(passed, last_set, mine, unit_old, units)
     far_set = exchange(last_set, 4, mids)
     other = exchange(mine, 1)
     gathered = pltpu.VMEM((8 * emb_rows, width + 128), bf16)
-    scaled, facts, share = call(
+    scaled, facts, share, share_high = call(
         share_kernel,
         (
             shape((16 * emb_rows, width), bf16),
             shape((16, 16 * emb_rows), i32),
-            shape((16, 4 * cap), f32),
+            shape((8, 4 * cap), f32),
+            shape((8, 4 * cap), f32),
         ),
         [gathered, gathered, pltpu.SemaphoreType.DMA((2,))],
         in_specs=[ANY, ANY, VMEM],
         cost_estimate=lasting(3),
-    )(mine, other, centroids)
+    )(mine, other, unit_old)
+    share = share + exchange(share_high, 1)
 
     def gather(share, apart):
         half = share.shape[0] // 2
         return share[:half] + exchange(share[half:], apart)
 
-    block_set = pltpu.VMEM((per * BLOCK2, width), bf16)
-    packed = pltpu.VMEM((3, per, 4 * cap, width), bf16)
     early = call(
         functools.partial(early_kernel, cap, per),
         shape((24, 4 * cap), f32),
-        [room(rows_of(4))] * 2 + [room(rows_of(3))] * 2 + [block_set] * 3 + [packed, pltpu.SemaphoreType.DMA((7,))],
-        in_specs=[VMEM, VMEM, HBM] + [ANY] * 7,
+        [room(rows_of(4))] * 2
+        + [room(rows_of(3))] * 2
+        + [
+            pltpu.VMEM((2, set_rows, width), bf16),
+            block_set,
+            pltpu.VMEM((3, per, 4 * cap, width), bf16),
+            pltpu.VMEM((3, per, 4 * cap, 128), bf16),
+            pltpu.SemaphoreType.DMA((6,)),
+        ],
+        in_specs=[VMEM, VMEM] + [ANY] * 7,
         cost_estimate=lasting(7),
-    )(scaled, facts, centroids2, near_set, cross_set, passed, rows0, rows1, early2, early3)
-    share, early = in_order(gather(share, 1), early)
+    )(scaled, facts, units, cross_set, passed, rows0, rows1, early2, early3)
+    share, early = in_order(gather(share, 2), early)
     kept = shape((1, per, 4 * cap, width), bf16)
-    kept_rows = call(
+    kept_rows, floors = call(
         functools.partial(late_kernel, cap, per),
-        kept,
+        (kept, shape((1, per, 4 * cap, 128), bf16)),
         [room(rows_of(1))] * 4 + [pltpu.SemaphoreType.DMA((4,))],
         in_specs=[VMEM] * 2 + [ANY] * 5,
         cost_estimate=lasting(3),
     )(scaled, facts, rows0, rows1, late2, late3, early)
-    share, kept_rows = in_order(gather(share, 2), kept_rows)
+    share, kept_rows = in_order(gather(share, 12), kept_rows)
     tile = shape((8, 4 * cap), f32)
     tiles = call(
         functools.partial(third_kernel, cap, per),
         (tile,) * 4,
         [room(kept), block_set, pltpu.SemaphoreType.DMA((2,))],
-        in_specs=[VMEM, ANY, ANY, ANY],
+        in_specs=[VMEM, VMEM, ANY, ANY, ANY],
         cost_estimate=lasting(1),
-    )(early, kept_rows, last_set, far_set)
-    share, *tiles = in_order(gather(share, 12), *tiles)
+    )(early, floors, kept_rows, last_set, far_set)
+    share, *tiles = in_order(share, *tiles)
     new_centroids, counts = call(
         update_kernel, (shape((rows, width), bf16), shape((1, rows), i32)), in_specs=[ANY] + [VMEM] * 4
     )(tiles[0], scaled, facts, centroids, prior_row)

time: 86.5 us -> 83.5 us (0.965)
  waiting for transfers between devices: 33 us -> 29.6 us
  Pallas kernels: 26 us -> 27.3 us
  local copies, waits for them, and re-layouts: 1.08 us -> 0.04 us
    ppermute x21, waiting for transfers between devices: 33 us -> 29.6 us  [exchange(): return lax.ppermute(value, 'shard', [(i, i ^ apart) for i in sources])]
    pallas_call x14 -> x15, Pallas kernels: 26 us -> 27.3 us  [run(): pl.pallas_call(kernel, out_shape=outs, in_specs=specs, scratch_shapes=lis...]
    unnamed x8, local copies, waits for them, and re-layouts: 1.06 us -> 0.02 us
  transfers between devices with their start and end apart: 21 -> 21, of which waited for: 7 -> 7; matrix products, arithmetic and copies ran while one was open for 0% -> 0% of each run, Pallas kernels for 28% -> 30%
where the time goes in v4:
time: 83.5 us; the launch traced here: 83.2 us
  waiting for transfers between devices  29.6 us (35%)
  Pallas kernels  27.3 us (33%)
  starting transfers between devices  25.3 us (30%)
  between operations  0.88 us (1%)
    ppermute x21, waiting for transfers between devices, exchange(): return lax.ppermute(value, 'shard', [(i, i ^ apart) for i in sources])  29.6 us
    pallas_call x15, Pallas kernels, run(): pl.pallas_call(kernel, out_shape=outs, in_specs=specs, scratch_shapes=lis...  27.3 us
    ppermute x21, starting transfers between devices, exchange(): return lax.ppermute(value, 'shard', [(i, i ^ apart) for i in sources])  25.3 us
  transfers between devices with their start and end apart: 21, of which 7 were waited for; matrix products, arithmetic and copies ran while one was open for 0% of the time, Pallas kernels for 30%

profile of v4, /device:TPU:0, one launch (start us, length us, event | category | flops | bytes accessed | tf_op | source)
XLA Modules:
  0.0 83.2 jit_solution(12216761636770210443)
XLA Ops:
  0.6 0.0 copy-start
  0.6 0.0 copy-start.3
  0.7 3.1 %collective-permute-start = (bf16[384,1024]{1,0:T(8,128)(2,1)}, bf16[384,1024]{1,0:T(8,128)(2,1)S(1)}, u32[]{:S(2)}, u32[]{:S(2)}) collective-permute-start(bf16[384,1024]{1,0:T(8,128)(2,1)} %own_any.1), channel_id=1, source_target_pairs={{0,4},{1,5},{2,6},{3,7},{4,0},{5,1},{6,2},{7,3},{8,12},{9,13},{10,... | collective-permute-start | bytes 2359304 | tf_op jit(solution)/shard_map/ppermute | solution.py:466
  3.7 0.7 collective-permute-start.1
  4.5 3.4 %shard_map.102 = (bf16[40,1152]{1,0:T(8,128)(2,1)S(1)}, bf16[304,1024]{1,0:T(8,128)(2,1)S(1)}, bf16[304,1024]{1,0:T(8,128)(2,1)S(1)}, s32[8,1024]{1,0:T(8,128)S(1)}) custom-call(s32[1,1024]{1,0:T(1,128)} %bitcast.10, bf16[40,1024]{1,0:T(8,128)(2,1)} %emb_any.1, s32[8,40]{1,0:T(8,128)} %bitcast.11, s32[1,40]{1,0:T(1,128)} %bitcast.12, s32[1,1024]{1,0:T(1,128)} %bitcast.7, ...), custom_call_target="tpu_custom_call" | custom-call | tf_op jit(solution)/shard_map/pallas_call | solution.py:432
  7.8 4.4 %collective-permute-start.2 = (bf16[40,1152]{1,0:T(8,128)(2,1)S(1)}, bf16[40,1152]{1,0:T(8,128)(2,1)S(1)}, u32[]{:S(2)}, u32[]{:S(2)}) collective-permute-start(bf16[40,1152]{1,0:T(8,128)(2,1)S(1)} %get-tuple-element.53), channel_id=1, source_target_pairs={{0,4},{1,5},{2,6},{3,7},{4,0},{5,1},{6,2},{7,3},{8,12},{9,13},{10,... | collective-permute-start | bytes 276488 | tf_op jit(solution)/shard_map/ppermute | solution.py:466
  12.3 1.5 %collective-permute-start.6 = (bf16[304,1024]{1,0:T(8,128)(2,1)S(1)}, bf16[304,1024]{1,0:T(8,128)(2,1)S(1)}, u32[]{:S(2)}, u32[]{:S(2)}) collective-permute-start(bf16[304,1024]{1,0:T(8,128)(2,1)S(1)} %get-tuple-element.58), channel_id=1, source_target_pairs={{0,2},{1,3},{2,0},{3,1},{4,6},{5,7},{6,4},{7,5},{8,10},{9,11},{10,... | collective-permute-start | bytes 1867784 | tf_op jit(solution)/shard_map/ppermute | solution.py:466
  13.8 0.0 collective-permute-start.7
  13.8 0.0 copy-done
  13.8 0.0 copy-done.3
  13.8 2.9 %shard_map.103 = (bf16[400,1024]{1,0:T(8,128)(2,1)S(1)}, bf16[400,1024]{1,0:T(8,128)(2,1)S(1)}, bf16[112,1024]{1,0:T(8,128)(2,1)S(1)}, bf16[112,1024]{1,0:T(8,128)(2,1)S(1)}) custom-call(s32[8,1024]{1,0:T(8,128)S(1)} %get-tuple-element.52.info, s32[1,1024]{1,0:T(1,128)S(1)} %bitcast.8, bf16[1024,1024]{1,0:T(8,128)(2,1)S(1)} %copy-done), custom_call_target="tpu_custom_call" | custom-call | tf_op jit(solution)/shard_map/pallas_call | solution.py:432
  16.7 6.8 %collective-permute-done.2 = bf16[40,1152]{1,0:T(8,128)(2,1)S(1)} collective-permute-done((bf16[40,1152]{1,0:T(8,128)(2,1)S(1)}, bf16[40,1152]{1,0:T(8,128)(2,1)S(1)}, u32[]{:S(2)}, u32[]{:S(2)}) %collective-permute-start.2) | collective-permute-done | bytes 92192 | tf_op jit(solution)/shard_map/ppermute | solution.py:466
  23.5 0.0 collective-permute-done.refs_0_
  23.5 0.0 collective-permute-done.1.refs_1_
  23.5 3.8 %collective-permute-start.5 = (bf16[80,1152]{1,0:T(8,128)(2,1)S(1)}, bf16[80,1152]{1,0:T(8,128)(2,1)S(1)}, u32[]{:S(2)}, u32[]{:S(2)}) collective-permute-start(bf16[80,1152]{1,0:T(8,128)(2,1)S(1)} %get-tuple-element.57), channel_id=1, source_target_pairs={{0,12},{1,13},{2,14},{3,15},{4,8},{5,9},{6,10},{7,11},{8,4},{9,5},... | collective-permute-start | bytes 552968 | tf_op jit(solution)/shard_map/ppermute | solution.py:466
  27.4 1.3 %collective-permute-start.3 = (bf16[384,1024]{1,0:T(8,128)(2,1)S(1)}, bf16[384,1024]{1,0:T(8,128)(2,1)S(1)}, u32[]{:S(2)}, u32[]{:S(2)}) collective-permute-start(bf16[384,1024]{1,0:T(8,128)(2,1)S(1)} %get-tuple-element.55.cross_any), channel_id=1, source_target_pairs={{4,0},{5,1},{6,2},{7,3},{8,12},{9,13},{10,14},{11,15},{20,16},{21,... | collective-permute-start | bytes 2359304 | tf_op jit(solution)/shard_map/ppermute | solution.py:466
  28.6 0.7 collective-permute-start.4
  29.4 2.0 %collective-permute-done.5 = bf16[80,1152]{1,0:T(8,128)(2,1)S(1)} collective-permute-done((bf16[80,1152]{1,0:T(8,128)(2,1)S(1)}, bf16[80,1152]{1,0:T(8,128)(2,1)S(1)}, u32[]{:S(2)}, u32[]{:S(2)}) %collective-permute-start.5) | collective-permute-done | bytes 184352 | tf_op jit(solution)/shard_map/ppermute | solution.py:466
  31.4 0.0 collective-permute-done.6.refs_1_
  31.4 8.1 %collective-permute-done.7.refs_2_ = bf16[304,1024]{1,0:T(8,128)(2,1)S(1)} collective-permute-done((bf16[304,1024]{1,0:T(8,128)(2,1)S(1)}, bf16[304,1024]{1,0:T(8,128)(2,1)S(1)}, u32[]{:S(2)}, u32[]{:S(2)}) %collective-permute-start.7) | collective-permute-done | bytes 622624 | tf_op jit(solution)/shard_map/ppermute | solution.py:466
  39.6 0.5 collective-permute-start.8
  40.1 3.2 %shard_map.106 = (bf16[1024,1024]{1,0:T(8,128)(2,1)S(1)}, bf16[2,384,1024]{2,1,0:T(8,128)(2,1)S(1)}) custom-call(bf16[1024,1024]{1,0:T(8,128)(2,1)} %cent_ref.5, bf16[384,1024]{1,0:T(8,128)(2,1)} %own_any.1, bf16[384,1024]{1,0:T(8,128)(2,1)S(1)} %get-tuple-element.56.near_any), custom_call_target="tpu_custom_call" | custom-call | tf_op jit(solution)/shard_map/pallas_call | solution.py:432
  43.3 1.9 %collective-permute-start.12 = (bf16[400,1024]{1,0:T(8,128)(2,1)S(1)}, bf16[400,1024]{1,0:T(8,128)(2,1)S(1)}, u32[]{:S(2)}, u32[]{:S(2)}) collective-permute-start(bf16[400,1024]{1,0:T(8,128)(2,1)S(1)} %get-tuple-element.75), channel_id=1, source_target_pairs={{0,1},{1,0},{2,3},{3,2},{4,5},{5,4},{6,7},{7,6},{8,9},{9,8},{10,11... | collective-permute-start | bytes 2457608 | tf_op jit(solution)/shard_map/ppermute | solution.py:466
  45.2 5.7 %collective-permute-done.8 = bf16[160,1152]{1,0:T(8,128)(2,1)S(1)} collective-permute-done((bf16[160,1152]{1,0:T(8,128)(2,1)S(1)}, bf16[160,1152]{1,0:T(8,128)(2,1)S(1)}, u32[]{:S(2)}, u32[]{:S(2)}) %collective-permute-start.8) | collective-permute-done | bytes 368672 | tf_op jit(solution)/shard_map/ppermute | solution.py:466
  50.9 0.1 pad_maximum_fusion.refs_2_
  51.0 0.0 collective-permute-done.3.refs_0_
  51.0 0.0 collective-permute-done.4.refs_1_
  51.0 0.0 copy-start.2
  51.0 0.2 collective-permute-start.9
  51.2 1.3 %collective-permute-start.16 = (bf16[384,1024]{1,0:T(8,128)(2,1)S(1)}, bf16[384,1024]{1,0:T(8,128)(2,1)S(1)}, u32[]{:S(2)}, u32[]{:S(2)}) collective-permute-start(bf16[384,1024]{1,0:T(8,128)(2,1)S(1)} %get-tuple-element.86.last_any), channel_id=1, source_target_pairs={{4,0},{5,1},{6,2},{7,3},{8,12},{9,13},{10,14},{11,15},{20,16},{21,... | collective-permute-start | bytes 2359304 | tf_op jit(solution)/shard_map/ppermute | solution.py:466
  52.5 0.8 collective-permute-done.9.other_any
  53.3 3.1 %shard_map.108 = (bf16[640,1024]{1,0:T(8,128)(2,1)S(1)}, s32[16,640]{1,0:T(8,128)S(1)}, f32[8,128]{1,0:T(8,128)S(1)}, f32[8,128]{1,0:T(8,128)S(1)}) custom-call(bf16[320,1152]{1,0:T(8,128)(2,1)S(1)} %get-tuple-element.66.mine_any, bf16[320,1152]{1,0:T(8,128)(2,1)S(1)} %collective-permute-done.9.other_any, bf16[1024,1024]{1,0:T(8,128)(2,1)S(1)} %get-tuple-element.67.unit_old), custom_call_target="tpu_custom_call" | custom-call | bytes 11070000 | tf_op jit(solution)/shard_map/pallas_call | solution.py:432
  56.4 0.0 copy-done.2
  56.4 0.2 collective-permute-start.10
  56.6 0.3 collective-permute-start.14
  56.9 1.4 %collective-permute-start.15 = (bf16[112,1024]{1,0:T(8,128)(2,1)S(1)}, bf16[112,1024]{1,0:T(8,128)(2,1)S(1)}, u32[]{:S(2)}, u32[]{:S(2)}) collective-permute-start(bf16[112,1024]{1,0:T(8,128)(2,1)S(1)} %get-tuple-element.80), channel_id=1, source_target_pairs={{0,3},{1,2},{2,1},{3,0},{4,7},{5,6},{6,5},{7,4},{8,11},{9,10},{10,... | collective-permute-start | bytes 688136 | tf_op jit(solution)/shard_map/ppermute | solution.py:466
  58.4 0.0 collective-permute-done.10
  58.4 0.4 collective-permute-start.11
  58.8 0.0 collective-permute-done.12.any1
  58.8 5.9 %shard_map.109.refs_1_ = f32[24,128]{1,0:T(8,128)S(1)} custom-call(bf16[640,1024]{1,0:T(8,128)(2,1)S(1)} %get-tuple-element.70.scaled, s32[16,640]{1,0:T(8,128)S(1)} %get-tuple-element.71.facts_in.facts, bf16[2,384,1024]{2,1,0:T(8,128)(2,1)} %copy-done.2, bf16[384,1024]{1,0:T(8,128)(2,1)S(1)} %get-tuple-element.55.cross_any, ...), custom_call_target="tpu_custom_call" | custom-call | bytes 25830000 | tf_op jit(solution)/shard_map/pallas_call | solution.py:432
  64.7 4.7 %collective-permute-done.11 = f32[4,128]{1,0:T(4,128)S(1)} collective-permute-done((f32[4,128]{1,0:T(4,128)S(1)}, f32[4,128]{1,0:T(4,128)S(1)}, u32[]{:S(2)}, u32[]{:S(2)}) %collective-permute-start.11) | collective-permute-done | bytes 2080 | tf_op jit(solution)/shard_map/ppermute | solution.py:466
  69.5 1.3 %collective-permute-start.13 = (f32[2,128]{1,0:T(2,128)S(1)}, f32[2,128]{1,0:T(2,128)S(1)}, u32[]{:S(2)}, u32[]{:S(2)}) collective-permute-start(f32[2,128]{1,0:T(2,128)S(1)} %slice.21), channel_id=1, source_target_pairs={{0,12},{1,13},{2,14},{3,15},{4,8},{5,9},{6,10},{7,11},{8,4},{9,5},... | collective-permute-start | bytes 3080 | tf_op jit(solution)/shard_map/ppermute | solution.py:466
  70.7 0.0 collective-permute-done.14.any2
  70.8 0.0 collective-permute-done.15.any3
  70.8 2.8 %shard_map.111 = (bf16[1,3,128,1024]{3,2,1,0:T(8,128)(2,1)S(1)}, bf16[1,3,128,128]{3,2,1,0:T(8,128)(2,1)S(1)}) custom-call(bf16[640,1024]{1,0:T(8,128)(2,1)S(1)} %get-tuple-element.70.scaled, s32[16,640]{1,0:T(8,128)S(1)} %get-tuple-element.71.facts_in.facts, bf16[400,1024]{1,0:T(8,128)(2,1)S(1)} %get-tuple-element.74.any0, ...), custom_call_target="tpu_custom_call" | custom-call | bytes 11070000 | tf_op jit(solution)/shard_map/pallas_call | solution.py:432
  73.6 1.4 %collective-permute-done.13 = f32[2,128]{1,0:T(2,128)S(1)} collective-permute-done((f32[2,128]{1,0:T(2,128)S(1)}, f32[2,128]{1,0:T(2,128)S(1)}, u32[]{:S(2)}, u32[]{:S(2)}) %collective-permute-start.13) | collective-permute-done | bytes 1056 | tf_op jit(solution)/shard_map/ppermute | solution.py:466
  74.9 0.0 copy-start.1
  74.9 0.0 collective-permute-done.16.far_any
  74.9 1.1 %shard_map.113 = (f32[8,128]{1,0:T(8,128)S(1)}, f32[8,128]{1,0:T(8,128)S(1)}, f32[8,128]{1,0:T(8,128)S(1)}, f32[8,128]{1,0:T(8,128)S(1)}) custom-call(f32[24,128]{1,0:T(8,128)S(1)} %get-tuple-element.81.after.early, bf16[1,3,128,128]{3,2,1,0:T(8,128)(2,1)S(1)} %get-tuple-element.84.floors, bf16[1,3,128,1024]{3,2,1,0:T(8,128)(2,1)S(1)} %get-tuple-element.85.kept_any, ...), custom_call_target="tpu_custom_call" | custom-call | bytes 3690000 | tf_op jit(solution)/shard_map/pallas_call | solution.py:432
  76.1 0.5 collective-permute-start.20
  76.6 0.0 collective-permute-start.17
  76.6 1.5 %collective-permute-start.18 = (f32[8,128]{1,0:T(8,128)S(1)}, f32[8,128]{1,0:T(8,128)S(1)}, u32[]{:S(2)}, u32[]{:S(2)}) collective-permute-start(f32[8,128]{1,0:T(8,128)S(1)} %get-tuple-element.93), channel_id=1, source_target_pairs={{0,2},{1,3},{2,0},{3,1},{4,6},{5,7},{6,4},{7,5},{8,10},{9,11},{10,... | collective-permute-start | bytes 12296 | tf_op jit(solution)/shard_map/ppermute | solution.py:466
  78.1 0.3 collective-permute-start.19
  78.5 0.0 copy-done.1
  78.5 3.7 %shard_map.116 = (bf16[1024,1024]{1,0:T(8,128)(2,1)}, s32[1,1024]{1,0:T(1,128)}) custom-call(f32[8,128]{1,0:T(8,128)S(1)} %get-tuple-element.91.got0.after, bf16[640,1024]{1,0:T(8,128)(2,1)S(1)} %get-tuple-element.70.scaled, s32[16,640]{1,0:T(8,128)S(1)} %get-tuple-element.71.facts_in.facts, bf16[1024,1024]{1,0:T(8,128)(2,1)S(1)} %copy-done.1, ...), custom_call_target="tpu_custom_call" | custom-call | tf_op jit(solution)/shard_map/pallas_call | solution.py:432
  82.1 0.0 collective-permute-done.20
  82.1 0.0 collective-permute-done.17.got1
  82.1 0.0 collective-permute-done.18.got2
  82.2 0.0 collective-permute-done.19.got3
  82.2 1.0 %shard_map.115 = (f32[1,40]{1,0:T(1,128)}, f32[1,1024]{1,0:T(1,128)}) custom-call(s32[8,1024]{1,0:T(8,128)S(1)} %get-tuple-element.52.info, f32[8,128]{1,0:T(8,128)S(1)} %get-tuple-element.91.got0.after, f32[8,128]{1,0:T(8,128)S(1)} %collective-permute-done.17.got1, f32[8,128]{1,0:T(8,128)S(1)} %collective-permute-done.18.got2, ...), custom_call_target="tpu_custom_call" | custom-call | tf_op jit(solution)/shard_map/pallas_call | solution.py:432
  (15 shorter events, 0.1 us)
Async XLA Ops:
  0.6 13.1 %copy-start = (bf16[1024,1024]{1,0:T(8,128)(2,1)S(1)}, bf16[1024,1024]{1,0:T(8,128)(2,1)}, u32[]{:S(2)}) copy-start(bf16[1024,1024]{1,0:T(8,128)(2,1)} %cent_ref.5) | copy-start | bytes 6291460
  0.6 13.1 %copy-start.3 = (s32[1024]{0:T(1024)S(1)}, s32[1024]{0:T(1024)}, u32[]{:S(2)}) copy-start(s32[1024]{0:T(1024)} %param.10) | copy-start | bytes 12292
  0.7 22.8 %collective-permute-start = (bf16[384,1024]{1,0:T(8,128)(2,1)}, bf16[384,1024]{1,0:T(8,128)(2,1)S(1)}, u32[]{:S(2)}, u32[]{:S(2)}) collective-permute-start(bf16[384,1024]{1,0:T(8,128)(2,1)} %own_any.1), channel_id=1, source_target_pairs={{0,4},{1,5},{2,6},{3,7},{4,0},{5,1},{6,2},{7,3},{8,12},{9,13},{10,... | collective-permute-start | bytes 2359304 | tf_op jit(solution)/shard_map/ppermute | solution.py:466
  3.7 19.8 %collective-permute-start.1 = (bf16[384,1024]{1,0:T(8,128)(2,1)}, bf16[384,1024]{1,0:T(8,128)(2,1)S(1)}, u32[]{:S(2)}, u32[]{:S(2)}) collective-permute-start(bf16[384,1024]{1,0:T(8,128)(2,1)} %own_any.1), channel_id=1, source_target_pairs={{4,8},{5,9},{6,10},{7,11},{8,4},{9,5},{10,6},{11,7},{20,24},{21,25... | collective-permute-start | bytes 2359304 | tf_op jit(solution)/shard_map/ppermute | solution.py:466
  7.8 15.6 %collective-permute-start.2 = (bf16[40,1152]{1,0:T(8,128)(2,1)S(1)}, bf16[40,1152]{1,0:T(8,128)(2,1)S(1)}, u32[]{:S(2)}, u32[]{:S(2)}) collective-permute-start(bf16[40,1152]{1,0:T(8,128)(2,1)S(1)} %get-tuple-element.53), channel_id=1, source_target_pairs={{0,4},{1,5},{2,6},{3,7},{4,0},{5,1},{6,2},{7,3},{8,12},{9,13},{10,... | collective-permute-start | bytes 276488 | tf_op jit(solution)/shard_map/ppermute | solution.py:466
  12.3 19.2 %collective-permute-start.6 = (bf16[304,1024]{1,0:T(8,128)(2,1)S(1)}, bf16[304,1024]{1,0:T(8,128)(2,1)S(1)}, u32[]{:S(2)}, u32[]{:S(2)}) collective-permute-start(bf16[304,1024]{1,0:T(8,128)(2,1)S(1)} %get-tuple-element.58), channel_id=1, source_target_pairs={{0,2},{1,3},{2,0},{3,1},{4,6},{5,7},{6,4},{7,5},{8,10},{9,11},{10,... | collective-permute-start | bytes 1867784 | tf_op jit(solution)/shard_map/ppermute | solution.py:466
  13.8 25.8 %collective-permute-start.7 = (bf16[304,1024]{1,0:T(8,128)(2,1)S(1)}, bf16[304,1024]{1,0:T(8,128)(2,1)S(1)}, u32[]{:S(2)}, u32[]{:S(2)}) collective-permute-start(bf16[304,1024]{1,0:T(8,128)(2,1)S(1)} %get-tuple-element.59), channel_id=1, source_target_pairs={{0,3},{1,2},{2,1},{3,0},{4,7},{5,6},{6,5},{7,4},{8,11},{9,10},{10,... | collective-permute-start | bytes 1867784 | tf_op jit(solution)/shard_map/ppermute | solution.py:466
  23.5 7.9 %collective-permute-start.5 = (bf16[80,1152]{1,0:T(8,128)(2,1)S(1)}, bf16[80,1152]{1,0:T(8,128)(2,1)S(1)}, u32[]{:S(2)}, u32[]{:S(2)}) collective-permute-start(bf16[80,1152]{1,0:T(8,128)(2,1)S(1)} %get-tuple-element.57), channel_id=1, source_target_pairs={{0,12},{1,13},{2,14},{3,15},{4,8},{5,9},{6,10},{7,11},{8,4},{9,5},... | collective-permute-start | bytes 552968 | tf_op jit(solution)/shard_map/ppermute | solution.py:466
  27.4 23.6 %collective-permute-start.3 = (bf16[384,1024]{1,0:T(8,128)(2,1)S(1)}, bf16[384,1024]{1,0:T(8,128)(2,1)S(1)}, u32[]{:S(2)}, u32[]{:S(2)}) collective-permute-start(bf16[384,1024]{1,0:T(8,128)(2,1)S(1)} %get-tuple-element.55.cross_any), channel_id=1, source_target_pairs={{4,0},{5,1},{6,2},{7,3},{8,12},{9,13},{10,14},{11,15},{20,16},{21,... | collective-permute-start | bytes 2359304 | tf_op jit(solution)/shard_map/ppermute | solution.py:466
  28.6 22.4 %collective-permute-start.4 = (bf16[384,1024]{1,0:T(8,128)(2,1)S(1)}, bf16[384,1024]{1,0:T(8,128)(2,1)S(1)}, u32[]{:S(2)}, u32[]{:S(2)}) collective-permute-start(bf16[384,1024]{1,0:T(8,128)(2,1)S(1)} %get-tuple-element.56.near_any), channel_id=1, source_target_pairs={{4,8},{5,9},{6,10},{7,11},{8,4},{9,5},{10,6},{11,7},{20,24},{21,25... | collective-permute-start | bytes 2359304 | tf_op jit(solution)/shard_map/ppermute | solution.py:466
  39.6 11.4 %collective-permute-start.8 = (bf16[160,1152]{1,0:T(8,128)(2,1)S(1)}, bf16[160,1152]{1,0:T(8,128)(2,1)S(1)}, u32[]{:S(2)}, u32[]{:S(2)}) collective-permute-start(bf16[160,1152]{1,0:T(8,128)(2,1)S(1)} %get-tuple-element.63), channel_id=1, source_target_pairs={{0,2},{1,3},{2,0},{3,1},{4,6},{5,7},{6,4},{7,5},{8,10},{9,11},{10,... | collective-permute-start | bytes 1105928 | tf_op jit(solution)/shard_map/ppermute | solution.py:466
  43.3 15.5 %collective-permute-start.12 = (bf16[400,1024]{1,0:T(8,128)(2,1)S(1)}, bf16[400,1024]{1,0:T(8,128)(2,1)S(1)}, u32[]{:S(2)}, u32[]{:S(2)}) collective-permute-start(bf16[400,1024]{1,0:T(8,128)(2,1)S(1)} %get-tuple-element.75), channel_id=1, source_target_pairs={{0,1},{1,0},{2,3},{3,2},{4,5},{5,4},{6,7},{7,6},{8,9},{9,8},{10,11... | collective-permute-start | bytes 2457608 | tf_op jit(solution)/shard_map/ppermute | solution.py:466
  51.0 5.4 %copy-start.2 = (bf16[2,384,1024]{2,1,0:T(8,128)(2,1)}, bf16[2,384,1024]{2,1,0:T(8,128)(2,1)S(1)}, u32[]{:S(2)}) copy-start(bf16[2,384,1024]{2,1,0:T(8,128)(2,1)S(1)} %get-tuple-element.72.units_any) | copy-start | bytes 4718596
  51.0 2.3 %collective-permute-start.9 = (bf16[320,1152]{1,0:T(8,128)(2,1)S(1)}, bf16[320,1152]{1,0:T(8,128)(2,1)S(1)}, u32[]{:S(2)}, u32[]{:S(2)}) collective-permute-start(bf16[320,1152]{1,0:T(8,128)(2,1)S(1)} %get-tuple-element.66.mine_any), channel_id=1, source_target_pairs={{0,1},{1,0},{2,3},{3,2},{4,5},{5,4},{6,7},{7,6},{8,9},{9,8},{10,11... | collective-permute-start | bytes 2211848 | tf_op jit(solution)/shard_map/ppermute | solution.py:466
  51.2 23.7 %collective-permute-start.16 = (bf16[384,1024]{1,0:T(8,128)(2,1)S(1)}, bf16[384,1024]{1,0:T(8,128)(2,1)S(1)}, u32[]{:S(2)}, u32[]{:S(2)}) collective-permute-start(bf16[384,1024]{1,0:T(8,128)(2,1)S(1)} %get-tuple-element.86.last_any), channel_id=1, source_target_pairs={{4,0},{5,1},{6,2},{7,3},{8,12},{9,13},{10,14},{11,15},{20,16},{21,... | collective-permute-start | bytes 2359304 | tf_op jit(solution)/shard_map/ppermute | solution.py:466
  56.4 1.9 %collective-permute-start.10 = (f32[8,128]{1,0:T(8,128)S(1)}, f32[8,128]{1,0:T(8,128)S(1)}, u32[]{:S(2)}, u32[]{:S(2)}) collective-permute-start(f32[8,128]{1,0:T(8,128)S(1)} %get-tuple-element.69), channel_id=1, source_target_pairs={{0,1},{1,0},{2,3},{3,2},{4,5},{5,4},{6,7},{7,6},{8,9},{9,8},{10,11... | collective-permute-start | bytes 12296 | tf_op jit(solution)/shard_map/ppermute | solution.py:466
  56.6 14.1 %collective-permute-start.14 = (bf16[112,1024]{1,0:T(8,128)(2,1)S(1)}, bf16[112,1024]{1,0:T(8,128)(2,1)S(1)}, u32[]{:S(2)}, u32[]{:S(2)}) collective-permute-start(bf16[112,1024]{1,0:T(8,128)(2,1)S(1)} %get-tuple-element.79), channel_id=1, source_target_pairs={{0,2},{1,3},{2,0},{3,1},{4,6},{5,7},{6,4},{7,5},{8,10},{9,11},{10,... | collective-permute-start | bytes 688136 | tf_op jit(solution)/shard_map/ppermute | solution.py:466
  56.9 13.8 %collective-permute-start.15 = (bf16[112,1024]{1,0:T(8,128)(2,1)S(1)}, bf16[112,1024]{1,0:T(8,128)(2,1)S(1)}, u32[]{:S(2)}, u32[]{:S(2)}) collective-permute-start(bf16[112,1024]{1,0:T(8,128)(2,1)S(1)} %get-tuple-element.80), channel_id=1, source_target_pairs={{0,3},{1,2},{2,1},{3,0},{4,7},{5,6},{6,5},{7,4},{8,11},{9,10},{10,... | collective-permute-start | bytes 688136 | tf_op jit(solution)/shard_map/ppermute | solution.py:466
  58.4 11.1 %collective-permute-start.11 = (f32[4,128]{1,0:T(4,128)S(1)}, f32[4,128]{1,0:T(4,128)S(1)}, u32[]{:S(2)}, u32[]{:S(2)}) collective-permute-start(f32[4,128]{1,0:T(4,128)S(1)} %slice.19), channel_id=1, source_target_pairs={{0,2},{1,3},{2,0},{3,1},{4,6},{5,7},{6,4},{7,5},{8,10},{9,11},{10,... | collective-permute-start | bytes 6152 | tf_op jit(solution)/shard_map/ppermute | solution.py:466
  69.5 5.4 %collective-permute-start.13 = (f32[2,128]{1,0:T(2,128)S(1)}, f32[2,128]{1,0:T(2,128)S(1)}, u32[]{:S(2)}, u32[]{:S(2)}) collective-permute-start(f32[2,128]{1,0:T(2,128)S(1)} %slice.21), channel_id=1, source_target_pairs={{0,12},{1,13},{2,14},{3,15},{4,8},{5,9},{6,10},{7,11},{8,4},{9,5},... | collective-permute-start | bytes 3080 | tf_op jit(solution)/shard_map/ppermute | solution.py:466
  74.9 3.5 %copy-start.1 = (bf16[1024,1024]{1,0:T(8,128)(2,1)S(1)}, bf16[1024,1024]{1,0:T(8,128)(2,1)}, u32[]{:S(2)}) copy-start(bf16[1024,1024]{1,0:T(8,128)(2,1)} %cent_ref.5) | copy-start | bytes 6291460
  76.1 6.0 %collective-permute-start.20 = (f32[1,128]{1,0:T(1,128)S(1)}, f32[1,128]{1,0:T(1,128)S(1)}, u32[]{:S(2)}, u32[]{:S(2)}) collective-permute-start(f32[1,128]{1,0:T(1,128)S(1)} %slice.23), channel_id=1, source_target_pairs={{0,4},{1,5},{2,6},{3,7},{4,0},{5,1},{6,2},{7,3},{8,12},{9,13},{10,... | collective-permute-start | bytes 1544 | tf_op jit(solution)/shard_map/ppermute | solution.py:466
  76.6 5.5 %collective-permute-start.17 = (f32[8,128]{1,0:T(8,128)S(1)}, f32[8,128]{1,0:T(8,128)S(1)}, u32[]{:S(2)}, u32[]{:S(2)}) collective-permute-start(f32[8,128]{1,0:T(8,128)S(1)} %get-tuple-element.92), channel_id=1, source_target_pairs={{0,1},{1,0},{2,3},{3,2},{4,5},{5,4},{6,7},{7,6},{8,9},{9,8},{10,11... | collective-permute-start | bytes 12296 | tf_op jit(solution)/shard_map/ppermute | solution.py:466
  76.6 5.5 %collective-permute-start.18 = (f32[8,128]{1,0:T(8,128)S(1)}, f32[8,128]{1,0:T(8,128)S(1)}, u32[]{:S(2)}, u32[]{:S(2)}) collective-permute-start(f32[8,128]{1,0:T(8,128)S(1)} %get-tuple-element.93), channel_id=1, source_target_pairs={{0,2},{1,3},{2,0},{3,1},{4,6},{5,7},{6,4},{7,5},{8,10},{9,11},{10,... | collective-permute-start | bytes 12296 | tf_op jit(solution)/shard_map/ppermute | solution.py:466
  78.1 4.0 %collective-permute-start.19 = (f32[8,128]{1,0:T(8,128)S(1)}, f32[8,128]{1,0:T(8,128)S(1)}, u32[]{:S(2)}, u32[]{:S(2)}) collective-permute-start(f32[8,128]{1,0:T(8,128)S(1)} %get-tuple-element.94), channel_id=1, source_target_pairs={{0,3},{1,2},{2,1},{3,0},{4,7},{5,6},{6,5},{7,4},{8,11},{9,10},{10,... | collective-permute-start | bytes 12296 | tf_op jit(solution)/shard_map/ppermute | solution.py:466

commit v5 on v4

--- a/solution.py
+++ b/solution.py
@@ -237,8 +237,8 @@
     pack(slot, prior_ref[...], cent_ref[...], 3 * 4 * per * cap, rows3)
 
 
-def pack_more_kernel(part, info, prior_ref, cent_ref, rows0, rows1, late2, late3):
-    for first, out in ((0, rows0), (4 * part, rows1), (11 * part, late2), (15 * part, late3)):
+def pack_more_kernel(part, info, prior_ref, cent_ref, rows0, rows1, late3):
+    for first, out in ((0, rows0), (4 * part, rows1), (15 * part, late3)):
         pack(info[0:1, :], prior_ref[...], cent_ref[...], first, out)
 
 
@@ -383,10 +383,10 @@
     part = per * cap
     tail = pl.ds(3 * part, part + META)
     refs = (rows0, rows1, rows2, rows3)
-    copies = fetch(list(zip((any0.at[tail], any1.at[tail], any2, any3), refs)), sems)
+    copies = fetch(list(zip((any0.at[tail], any1.at[tail], any2.at[tail], any3), refs)), sems)
     for copy in copies:
         copy.wait()
-    redo(cap, per, scaled, facts_in, me, refs, (3 * part, 3 * part, 0, 0), packed, floors)
+    redo(cap, per, scaled, facts_in, me, refs, (3 * part, 3 * part, 3 * part, 0), packed, floors)
 
 
 def third_kernel(cap, per, early, floors, kept_any, last_any, far_any, out0, out1, out2, out3, kept, two, sems):
@@ -476,9 +476,9 @@
     cross_set = exchange(centroids2, 12, mids)
     prior_row = prior_counts.reshape(1, rows)
     line = pltpu.VMEM((1, rows), i32)
-    mine, early2, early3, info = call(
+    mine, rows2, early3, info = call(
         functools.partial(pack_kernel, cap, per),
-        (shape((emb_rows, width + 128), bf16), rows_of(3), rows_of(3), shape((8, rows), i32)),
+        (shape((emb_rows, width + 128), bf16), rows_of(4), rows_of(3), shape((8, rows), i32)),
         [
             line,
             pltpu.VMEM((emb_rows, width), bf16),
@@ -490,9 +490,9 @@
         ],
         in_specs=[HBM] * 6,
     )(candidates.reshape(1, rows), embeddings, probes.T, assigned.reshape(1, emb_rows), prior_row, centroids)
-    early2, early3 = exchange(early2, 2), exchange(early3, 3)
-    rows0, rows1, late2, late3 = call(
-        functools.partial(pack_more_kernel, part), (rows_of(4), rows_of(4), rows_of(1), rows_of(1))
+    rows2, early3 = exchange(rows2, 2), exchange(early3, 3)
+    rows0, rows1, late3 = call(
+        functools.partial(pack_more_kernel, part), (rows_of(4), rows_of(4), rows_of(1))
     )(info, prior_row, centroids)
     mine = jnp.concatenate([mine, exchange(mine, 4)], axis=0)
     near_set, cross_set, mine, rows0 = in_order(near_set, cross_set, mine, rows0)
@@ -500,9 +500,9 @@
     passed = exchange(cross_set, 4, mids)
     last_set = exchange(near_set, 12, mids)
     mine = jnp.concatenate([mine, across], axis=0)
-    mine, early2, early3, late2, late3, rows1 = in_order(mine, early2, early3, late2, late3, rows1)
+    mine, rows2, early3, late3, rows1 = in_order(mine, rows2, early3, late3, rows1)
     mine = jnp.concatenate([mine, exchange(mine, 2)], axis=0)
-    late2, late3 = exchange(late2, 2), exchange(late3, 3)
+    late3 = exchange(late3, 3)
     rows1 = exchange(rows1, 1)
     set_rows = per * BLOCK2
     block_set = pltpu.VMEM((set_rows, width), bf16)
@@ -537,8 +537,8 @@
     early = call(
         functools.partial(early_kernel, cap, per),
         shape((24, 4 * cap), f32),
-        [room(rows_of(4))] * 2
-        + [room(rows_of(3))] * 2
+        [room(rows_of(4))] * 3
+        + [room(rows_of(3))]
         + [
             pltpu.VMEM((2, set_rows, width), bf16),
             block_set,
@@ -548,7 +548,7 @@
         ],
         in_specs=[VMEM, VMEM] + [ANY] * 7,
         cost_estimate=lasting(7),
-    )(scaled, facts, units, cross_set, passed, rows0, rows1, early2, early3)
+    )(scaled, facts, units, cross_set, passed, rows0, rows1, rows2, early3)
     share, early = in_order(gather(share, 2), early)
     kept = shape((1, per, 4 * cap, width), bf16)
     kept_rows, floors = call(
@@ -557,7 +557,7 @@
         [room(rows_of(1))] * 4 + [pltpu.SemaphoreType.DMA((4,))],
         in_specs=[VMEM] * 2 + [ANY] * 5,
         cost_estimate=lasting(3),
-    )(scaled, facts, rows0, rows1, late2, late3, early)
+    )(scaled, facts, rows0, rows1, rows2, late3, early)
     share, kept_rows = in_order(gather(share, 12), kept_rows)
     tile = shape((8, 4 * cap), f32)
     tiles = call(

time: 83.5 us -> 83.6 us (level)
    ppermute x21 -> x20, starting transfers between devices: 25.3 us -> 25.9 us  [exchange(): return lax.ppermute(value, 'shard', [(i, i ^ apart) for i in sources])]
    ppermute x21 -> x20, waiting for transfers between devices: 29.6 us -> 29.2 us  [exchange(): return lax.ppermute(value, 'shard', [(i, i ^ apart) for i in sources])]
  transfers between devices with their start and end apart: 21 -> 20, of which waited for: 7 -> 7; matrix products, arithmetic and copies ran while one was open for 0% -> 0% of each run, Pallas kernels for 30% -> 30%
where the time goes in v5:
time: 83.6 us; the launch traced here: 83.3 us
  waiting for transfers between devices  29.2 us (35%)
  Pallas kernels  27.1 us (32%)
  starting transfers between devices  25.9 us (31%)
  between operations  0.94 us (1%)
    ppermute x20, waiting for transfers between devices, exchange(): return lax.ppermute(value, 'shard', [(i, i ^ apart) for i in sources])  29.2 us
    pallas_call x15, Pallas kernels, run(): pl.pallas_call(kernel, out_shape=outs, in_specs=specs, scratch_shapes=lis...  27.1 us
    ppermute x20, starting transfers between devices, exchange(): return lax.ppermute(value, 'shard', [(i, i ^ apart) for i in sources])  25.9 us
  transfers between devices with their start and end apart: 20, of which 7 were waited for; matrix products, arithmetic and copies ran while one was open for 0% of the time, Pallas kernels for 30%

profile of v5, /device:TPU:0, one launch (start us, length us, event | category | flops | bytes accessed | tf_op | source)
XLA Modules:
  0.0 83.3 jit_solution(95025142715372543)
XLA Ops:
  0.6 0.0 copy-start
  0.6 0.0 copy-start.3
  0.7 3.1 %collective-permute-start = (bf16[384,1024]{1,0:T(8,128)(2,1)}, bf16[384,1024]{1,0:T(8,128)(2,1)S(1)}, u32[]{:S(2)}, u32[]{:S(2)}) collective-permute-start(bf16[384,1024]{1,0:T(8,128)(2,1)} %own_any.1), channel_id=1, source_target_pairs={{0,4},{1,5},{2,6},{3,7},{4,0},{5,1},{6,2},{7,3},{8,12},{9,13},{10,... | collective-permute-start | bytes 2359304 | tf_op jit(solution)/shard_map/ppermute | solution.py:466
  3.7 0.7 collective-permute-start.1
  4.5 3.6 %shard_map.102 = (bf16[40,1152]{1,0:T(8,128)(2,1)S(1)}, bf16[400,1024]{1,0:T(8,128)(2,1)S(1)}, bf16[304,1024]{1,0:T(8,128)(2,1)S(1)}, s32[8,1024]{1,0:T(8,128)S(1)}) custom-call(s32[1,1024]{1,0:T(1,128)} %bitcast.10, bf16[40,1024]{1,0:T(8,128)(2,1)} %emb_any.1, s32[8,40]{1,0:T(8,128)} %bitcast.11, s32[1,40]{1,0:T(1,128)} %bitcast.12, s32[1,1024]{1,0:T(1,128)} %bitcast.7, ...), custom_call_target="tpu_custom_call" | custom-call | tf_op jit(solution)/shard_map/pallas_call | solution.py:432
  8.1 1.6 %collective-permute-start.6 = (bf16[400,1024]{1,0:T(8,128)(2,1)S(1)}, bf16[400,1024]{1,0:T(8,128)(2,1)S(1)}, u32[]{:S(2)}, u32[]{:S(2)}) collective-permute-start(bf16[400,1024]{1,0:T(8,128)(2,1)S(1)} %get-tuple-element.56), channel_id=1, source_target_pairs={{0,2},{1,3},{2,0},{3,1},{4,6},{5,7},{6,4},{7,5},{8,10},{9,11},{10,... | collective-permute-start | bytes 2457608 | tf_op jit(solution)/shard_map/ppermute | solution.py:466
  9.7 4.4 %collective-permute-start.2 = (bf16[40,1152]{1,0:T(8,128)(2,1)S(1)}, bf16[40,1152]{1,0:T(8,128)(2,1)S(1)}, u32[]{:S(2)}, u32[]{:S(2)}) collective-permute-start(bf16[40,1152]{1,0:T(8,128)(2,1)S(1)} %get-tuple-element.51), channel_id=1, source_target_pairs={{0,4},{1,5},{2,6},{3,7},{4,0},{5,1},{6,2},{7,3},{8,12},{9,13},{10,... | collective-permute-start | bytes 276488 | tf_op jit(solution)/shard_map/ppermute | solution.py:466
  14.0 0.0 collective-permute-start.7
  14.0 0.0 copy-done
  14.0 0.0 copy-done.3
  14.0 2.6 %shard_map.103 = (bf16[400,1024]{1,0:T(8,128)(2,1)S(1)}, bf16[400,1024]{1,0:T(8,128)(2,1)S(1)}, bf16[112,1024]{1,0:T(8,128)(2,1)S(1)}) custom-call(s32[8,1024]{1,0:T(8,128)S(1)} %get-tuple-element.50.info, s32[1,1024]{1,0:T(1,128)S(1)} %bitcast.8, bf16[1024,1024]{1,0:T(8,128)(2,1)S(1)} %copy-done), custom_call_target="tpu_custom_call" | custom-call | tf_op jit(solution)/shard_map/pallas_call | solution.py:432
  16.6 6.9 %collective-permute-done.2 = bf16[40,1152]{1,0:T(8,128)(2,1)S(1)} collective-permute-done((bf16[40,1152]{1,0:T(8,128)(2,1)S(1)}, bf16[40,1152]{1,0:T(8,128)(2,1)S(1)}, u32[]{:S(2)}, u32[]{:S(2)}) %collective-permute-start.2) | collective-permute-done | bytes 92192 | tf_op jit(solution)/shard_map/ppermute | solution.py:466
  23.5 0.0 collective-permute-done.refs_0_
  23.5 0.0 collective-permute-done.1.refs_1_
  23.5 3.8 %collective-permute-start.5 = (bf16[80,1152]{1,0:T(8,128)(2,1)S(1)}, bf16[80,1152]{1,0:T(8,128)(2,1)S(1)}, u32[]{:S(2)}, u32[]{:S(2)}) collective-permute-start(bf16[80,1152]{1,0:T(8,128)(2,1)S(1)} %get-tuple-element.55), channel_id=1, source_target_pairs={{0,12},{1,13},{2,14},{3,15},{4,8},{5,9},{6,10},{7,11},{8,4},{9,5},... | collective-permute-start | bytes 552968 | tf_op jit(solution)/shard_map/ppermute | solution.py:466
  27.4 1.3 %collective-permute-start.3 = (bf16[384,1024]{1,0:T(8,128)(2,1)S(1)}, bf16[384,1024]{1,0:T(8,128)(2,1)S(1)}, u32[]{:S(2)}, u32[]{:S(2)}) collective-permute-start(bf16[384,1024]{1,0:T(8,128)(2,1)S(1)} %get-tuple-element.53.cross_any), channel_id=1, source_target_pairs={{4,0},{5,1},{6,2},{7,3},{8,12},{9,13},{10,14},{11,15},{20,16},{21,... | collective-permute-start | bytes 2359304 | tf_op jit(solution)/shard_map/ppermute | solution.py:466
  28.6 0.7 collective-permute-start.4
  29.4 2.0 %collective-permute-done.5 = bf16[80,1152]{1,0:T(8,128)(2,1)S(1)} collective-permute-done((bf16[80,1152]{1,0:T(8,128)(2,1)S(1)}, bf16[80,1152]{1,0:T(8,128)(2,1)S(1)}, u32[]{:S(2)}, u32[]{:S(2)}) %collective-permute-start.5) | collective-permute-done | bytes 184352 | tf_op jit(solution)/shard_map/ppermute | solution.py:466
  31.4 8.8 %collective-permute-done.7.refs_2_ = bf16[304,1024]{1,0:T(8,128)(2,1)S(1)} collective-permute-done((bf16[304,1024]{1,0:T(8,128)(2,1)S(1)}, bf16[304,1024]{1,0:T(8,128)(2,1)S(1)}, u32[]{:S(2)}, u32[]{:S(2)}) %collective-permute-start.7) | collective-permute-done | bytes 622624 | tf_op jit(solution)/shard_map/ppermute | solution.py:466
  40.2 0.0 collective-permute-done.6.refs_1_
  40.3 1.0 %collective-permute-start.8 = (bf16[160,1152]{1,0:T(8,128)(2,1)S(1)}, bf16[160,1152]{1,0:T(8,128)(2,1)S(1)}, u32[]{:S(2)}, u32[]{:S(2)}) collective-permute-start(bf16[160,1152]{1,0:T(8,128)(2,1)S(1)} %get-tuple-element.60), channel_id=1, source_target_pairs={{0,2},{1,3},{2,0},{3,1},{4,6},{5,7},{6,4},{7,5},{8,10},{9,11},{10,... | collective-permute-start | bytes 1105928 | tf_op jit(solution)/shard_map/ppermute | solution.py:466
  41.3 3.2 %shard_map.106 = (bf16[1024,1024]{1,0:T(8,128)(2,1)S(1)}, bf16[2,384,1024]{2,1,0:T(8,128)(2,1)S(1)}) custom-call(bf16[1024,1024]{1,0:T(8,128)(2,1)} %cent_ref.5, bf16[384,1024]{1,0:T(8,128)(2,1)} %own_any.1, bf16[384,1024]{1,0:T(8,128)(2,1)S(1)} %get-tuple-element.54.near_any), custom_call_target="tpu_custom_call" | custom-call | tf_op jit(solution)/shard_map/pallas_call | solution.py:432
  44.5 1.4 %collective-permute-start.12 = (bf16[400,1024]{1,0:T(8,128)(2,1)S(1)}, bf16[400,1024]{1,0:T(8,128)(2,1)S(1)}, u32[]{:S(2)}, u32[]{:S(2)}) collective-permute-start(bf16[400,1024]{1,0:T(8,128)(2,1)S(1)} %get-tuple-element.72), channel_id=1, source_target_pairs={{0,1},{1,0},{2,3},{3,2},{4,5},{5,4},{6,7},{7,6},{8,9},{9,8},{10,11... | collective-permute-start | bytes 2457608 | tf_op jit(solution)/shard_map/ppermute | solution.py:466
  45.9 5.7 %collective-permute-done.8 = bf16[160,1152]{1,0:T(8,128)(2,1)S(1)} collective-permute-done((bf16[160,1152]{1,0:T(8,128)(2,1)S(1)}, bf16[160,1152]{1,0:T(8,128)(2,1)S(1)}, u32[]{:S(2)}, u32[]{:S(2)}) %collective-permute-start.8) | collective-permute-done | bytes 368672 | tf_op jit(solution)/shard_map/ppermute | solution.py:466
  51.6 0.1 pad_maximum_fusion.refs_2_
  51.7 0.0 collective-permute-done.3.refs_0_
  51.7 0.0 collective-permute-done.4.refs_1_
  51.7 0.0 copy-start.2
  51.7 0.2 collective-permute-start.9
  51.9 1.3 %collective-permute-start.15 = (bf16[384,1024]{1,0:T(8,128)(2,1)S(1)}, bf16[384,1024]{1,0:T(8,128)(2,1)S(1)}, u32[]{:S(2)}, u32[]{:S(2)}) collective-permute-start(bf16[384,1024]{1,0:T(8,128)(2,1)S(1)} %get-tuple-element.82.last_any), channel_id=1, source_target_pairs={{4,0},{5,1},{6,2},{7,3},{8,12},{9,13},{10,14},{11,15},{20,16},{21,... | collective-permute-start | bytes 2359304 | tf_op jit(solution)/shard_map/ppermute | solution.py:466
  53.2 0.8 collective-permute-done.9.other_any
  54.0 3.1 %shard_map.108 = (bf16[640,1024]{1,0:T(8,128)(2,1)S(1)}, s32[16,640]{1,0:T(8,128)S(1)}, f32[8,128]{1,0:T(8,128)S(1)}, f32[8,128]{1,0:T(8,128)S(1)}) custom-call(bf16[320,1152]{1,0:T(8,128)(2,1)S(1)} %get-tuple-element.63.mine_any, bf16[320,1152]{1,0:T(8,128)(2,1)S(1)} %collective-permute-done.9.other_any, bf16[1024,1024]{1,0:T(8,128)(2,1)S(1)} %get-tuple-element.64.unit_old), custom_call_target="tpu_custom_call" | custom-call | bytes 11070000 | tf_op jit(solution)/shard_map/pallas_call | solution.py:432
  57.1 0.0 copy-done.2
  57.1 0.2 collective-permute-start.10
  57.3 0.5 collective-permute-start.14
  57.9 0.5 collective-permute-done.10
  58.4 1.0 %collective-permute-start.11 = (f32[4,128]{1,0:T(4,128)S(1)}, f32[4,128]{1,0:T(4,128)S(1)}, u32[]{:S(2)}, u32[]{:S(2)}) collective-permute-start(f32[4,128]{1,0:T(4,128)S(1)} %slice.19), channel_id=1, source_target_pairs={{0,2},{1,3},{2,0},{3,1},{4,6},{5,7},{6,4},{7,5},{8,10},{9,11},{10,... | collective-permute-start | bytes 6152 | tf_op jit(solution)/shard_map/ppermute | solution.py:466
  59.4 0.0 collective-permute-done.12.any1
  59.4 5.9 %shard_map.109.refs_1_ = f32[24,128]{1,0:T(8,128)S(1)} custom-call(bf16[640,1024]{1,0:T(8,128)(2,1)S(1)} %get-tuple-element.67.scaled, s32[16,640]{1,0:T(8,128)S(1)} %get-tuple-element.68.facts_in.facts, bf16[2,384,1024]{2,1,0:T(8,128)(2,1)} %copy-done.2, bf16[384,1024]{1,0:T(8,128)(2,1)S(1)} %get-tuple-element.53.cross_any, ...), custom_call_target="tpu_custom_call" | custom-call | bytes 25830000 | tf_op jit(solution)/shard_map/pallas_call | solution.py:432
  65.3 0.0 collective-permute-done.11
  65.3 2.7 %collective-permute-start.13 = (f32[2,128]{1,0:T(2,128)S(1)}, f32[2,128]{1,0:T(2,128)S(1)}, u32[]{:S(2)}, u32[]{:S(2)}) collective-permute-start(f32[2,128]{1,0:T(2,128)S(1)} %slice.21), channel_id=1, source_target_pairs={{0,12},{1,13},{2,14},{3,15},{4,8},{5,9},{6,10},{7,11},{8,4},{9,5},... | collective-permute-start | bytes 3080 | tf_op jit(solution)/shard_map/ppermute | solution.py:466
  68.0 0.0 collective-permute-done.14.any3
  68.0 2.8 %shard_map.111 = (bf16[1,3,128,1024]{3,2,1,0:T(8,128)(2,1)S(1)}, bf16[1,3,128,128]{3,2,1,0:T(8,128)(2,1)S(1)}) custom-call(bf16[640,1024]{1,0:T(8,128)(2,1)S(1)} %get-tuple-element.67.scaled, s32[16,640]{1,0:T(8,128)S(1)} %get-tuple-element.68.facts_in.facts, bf16[400,1024]{1,0:T(8,128)(2,1)S(1)} %get-tuple-element.71.any0, ...), custom_call_target="tpu_custom_call" | custom-call | bytes 11070000 | tf_op jit(solution)/shard_map/pallas_call | solution.py:432
  70.9 0.0 collective-permute-done.13
  70.9 0.0 copy-start.1
  70.9 4.4 %collective-permute-done.15.far_any = bf16[384,1024]{1,0:T(8,128)(2,1)S(1)} collective-permute-done((bf16[384,1024]{1,0:T(8,128)(2,1)S(1)}, bf16[384,1024]{1,0:T(8,128)(2,1)S(1)}, u32[]{:S(2)}, u32[]{:S(2)}) %collective-permute-start.15) | collective-permute-done | bytes 786464 | tf_op jit(solution)/shard_map/ppermute | solution.py:466
  75.4 1.1 %shard_map.113 = (f32[8,128]{1,0:T(8,128)S(1)}, f32[8,128]{1,0:T(8,128)S(1)}, f32[8,128]{1,0:T(8,128)S(1)}, f32[8,128]{1,0:T(8,128)S(1)}) custom-call(f32[24,128]{1,0:T(8,128)S(1)} %get-tuple-element.77.after.early, bf16[1,3,128,128]{3,2,1,0:T(8,128)(2,1)S(1)} %get-tuple-element.80.floors, bf16[1,3,128,1024]{3,2,1,0:T(8,128)(2,1)S(1)} %get-tuple-element.81.kept_any, ...), custom_call_target="tpu_custom_call" | custom-call | bytes 3690000 | tf_op jit(solution)/shard_map/pallas_call | solution.py:432
  76.5 0.1 collective-permute-start.19
  76.6 0.1 collective-permute-start.16
  76.7 0.2 collective-permute-start.17
  76.9 1.6 %collective-permute-start.18 = (f32[8,128]{1,0:T(8,128)S(1)}, f32[8,128]{1,0:T(8,128)S(1)}, u32[]{:S(2)}, u32[]{:S(2)}) collective-permute-start(f32[8,128]{1,0:T(8,128)S(1)} %get-tuple-element.90), channel_id=1, source_target_pairs={{0,3},{1,2},{2,1},{3,0},{4,7},{5,6},{6,5},{7,4},{8,11},{9,10},{10,... | collective-permute-start | bytes 12296 | tf_op jit(solution)/shard_map/ppermute | solution.py:466
  78.5 0.0 copy-done.1
  78.5 3.7 %shard_map.116 = (bf16[1024,1024]{1,0:T(8,128)(2,1)}, s32[1,1024]{1,0:T(1,128)}) custom-call(f32[8,128]{1,0:T(8,128)S(1)} %get-tuple-element.87.got0.after, bf16[640,1024]{1,0:T(8,128)(2,1)S(1)} %get-tuple-element.67.scaled, s32[16,640]{1,0:T(8,128)S(1)} %get-tuple-element.68.facts_in.facts, bf16[1024,1024]{1,0:T(8,128)(2,1)S(1)} %copy-done.1, ...), custom_call_target="tpu_custom_call" | custom-call | tf_op jit(solution)/shard_map/pallas_call | solution.py:432
  82.2 0.0 collective-permute-done.19
  82.2 0.0 collective-permute-done.16.got1
  82.2 0.0 collective-permute-done.17.got2
  82.2 0.0 collective-permute-done.18.got3
  82.2 1.0 %shard_map.115 = (f32[1,40]{1,0:T(1,128)}, f32[1,1024]{1,0:T(1,128)}) custom-call(s32[8,1024]{1,0:T(8,128)S(1)} %get-tuple-element.50.info, f32[8,128]{1,0:T(8,128)S(1)} %get-tuple-element.87.got0.after, f32[8,128]{1,0:T(8,128)S(1)} %collective-permute-done.16.got1, f32[8,128]{1,0:T(8,128)S(1)} %collective-permute-done.17.got2, ...), custom_call_target="tpu_custom_call" | custom-call | tf_op jit(solution)/shard_map/pallas_call | solution.py:432
  (15 shorter events, 0.1 us)
Async XLA Ops:
  0.6 13.4 %copy-start = (bf16[1024,1024]{1,0:T(8,128)(2,1)S(1)}, bf16[1024,1024]{1,0:T(8,128)(2,1)}, u32[]{:S(2)}) copy-start(bf16[1024,1024]{1,0:T(8,128)(2,1)} %cent_ref.5) | copy-start | bytes 6291460
  0.6 13.4 %copy-start.3 = (s32[1024]{0:T(1024)S(1)}, s32[1024]{0:T(1024)}, u32[]{:S(2)}) copy-start(s32[1024]{0:T(1024)} %param.10) | copy-start | bytes 12292
  0.7 22.8 %collective-permute-start = (bf16[384,1024]{1,0:T(8,128)(2,1)}, bf16[384,1024]{1,0:T(8,128)(2,1)S(1)}, u32[]{:S(2)}, u32[]{:S(2)}) collective-permute-start(bf16[384,1024]{1,0:T(8,128)(2,1)} %own_any.1), channel_id=1, source_target_pairs={{0,4},{1,5},{2,6},{3,7},{4,0},{5,1},{6,2},{7,3},{8,12},{9,13},{10,... | collective-permute-start | bytes 2359304 | tf_op jit(solution)/shard_map/ppermute | solution.py:466
  3.7 19.8 %collective-permute-start.1 = (bf16[384,1024]{1,0:T(8,128)(2,1)}, bf16[384,1024]{1,0:T(8,128)(2,1)S(1)}, u32[]{:S(2)}, u32[]{:S(2)}) collective-permute-start(bf16[384,1024]{1,0:T(8,128)(2,1)} %own_any.1), channel_id=1, source_target_pairs={{4,8},{5,9},{6,10},{7,11},{8,4},{9,5},{10,6},{11,7},{20,24},{21,25... | collective-permute-start | bytes 2359304 | tf_op jit(solution)/shard_map/ppermute | solution.py:466
  8.1 32.2 %collective-permute-start.6 = (bf16[400,1024]{1,0:T(8,128)(2,1)S(1)}, bf16[400,1024]{1,0:T(8,128)(2,1)S(1)}, u32[]{:S(2)}, u32[]{:S(2)}) collective-permute-start(bf16[400,1024]{1,0:T(8,128)(2,1)S(1)} %get-tuple-element.56), channel_id=1, source_target_pairs={{0,2},{1,3},{2,0},{3,1},{4,6},{5,7},{6,4},{7,5},{8,10},{9,11},{10,... | collective-permute-start | bytes 2457608 | tf_op jit(solution)/shard_map/ppermute | solution.py:466
  9.7 13.8 %collective-permute-start.2 = (bf16[40,1152]{1,0:T(8,128)(2,1)S(1)}, bf16[40,1152]{1,0:T(8,128)(2,1)S(1)}, u32[]{:S(2)}, u32[]{:S(2)}) collective-permute-start(bf16[40,1152]{1,0:T(8,128)(2,1)S(1)} %get-tuple-element.51), channel_id=1, source_target_pairs={{0,4},{1,5},{2,6},{3,7},{4,0},{5,1},{6,2},{7,3},{8,12},{9,13},{10,... | collective-permute-start | bytes 276488 | tf_op jit(solution)/shard_map/ppermute | solution.py:466
  14.0 26.2 %collective-permute-start.7 = (bf16[304,1024]{1,0:T(8,128)(2,1)S(1)}, bf16[304,1024]{1,0:T(8,128)(2,1)S(1)}, u32[]{:S(2)}, u32[]{:S(2)}) collective-permute-start(bf16[304,1024]{1,0:T(8,128)(2,1)S(1)} %get-tuple-element.57), channel_id=1, source_target_pairs={{0,3},{1,2},{2,1},{3,0},{4,7},{5,6},{6,5},{7,4},{8,11},{9,10},{10,... | collective-permute-start | bytes 1867784 | tf_op jit(solution)/shard_map/ppermute | solution.py:466
  23.5 7.9 %collective-permute-start.5 = (bf16[80,1152]{1,0:T(8,128)(2,1)S(1)}, bf16[80,1152]{1,0:T(8,128)(2,1)S(1)}, u32[]{:S(2)}, u32[]{:S(2)}) collective-permute-start(bf16[80,1152]{1,0:T(8,128)(2,1)S(1)} %get-tuple-element.55), channel_id=1, source_target_pairs={{0,12},{1,13},{2,14},{3,15},{4,8},{5,9},{6,10},{7,11},{8,4},{9,5},... | collective-permute-start | bytes 552968 | tf_op jit(solution)/shard_map/ppermute | solution.py:466
  27.4 24.3 %collective-permute-start.3 = (bf16[384,1024]{1,0:T(8,128)(2,1)S(1)}, bf16[384,1024]{1,0:T(8,128)(2,1)S(1)}, u32[]{:S(2)}, u32[]{:S(2)}) collective-permute-start(bf16[384,1024]{1,0:T(8,128)(2,1)S(1)} %get-tuple-element.53.cross_any), channel_id=1, source_target_pairs={{4,0},{5,1},{6,2},{7,3},{8,12},{9,13},{10,14},{11,15},{20,16},{21,... | collective-permute-start | bytes 2359304 | tf_op jit(solution)/shard_map/ppermute | solution.py:466
  28.6 23.0 %collective-permute-start.4 = (bf16[384,1024]{1,0:T(8,128)(2,1)S(1)}, bf16[384,1024]{1,0:T(8,128)(2,1)S(1)}, u32[]{:S(2)}, u32[]{:S(2)}) collective-permute-start(bf16[384,1024]{1,0:T(8,128)(2,1)S(1)} %get-tuple-element.54.near_any), channel_id=1, source_target_pairs={{4,8},{5,9},{6,10},{7,11},{8,4},{9,5},{10,6},{11,7},{20,24},{21,25... | collective-permute-start | bytes 2359304 | tf_op jit(solution)/shard_map/ppermute | solution.py:466
  40.3 11.4 %collective-permute-start.8 = (bf16[160,1152]{1,0:T(8,128)(2,1)S(1)}, bf16[160,1152]{1,0:T(8,128)(2,1)S(1)}, u32[]{:S(2)}, u32[]{:S(2)}) collective-permute-start(bf16[160,1152]{1,0:T(8,128)(2,1)S(1)} %get-tuple-element.60), channel_id=1, source_target_pairs={{0,2},{1,3},{2,0},{3,1},{4,6},{5,7},{6,4},{7,5},{8,10},{9,11},{10,... | collective-permute-start | bytes 1105928 | tf_op jit(solution)/shard_map/ppermute | solution.py:466
  44.5 14.9 %collective-permute-start.12 = (bf16[400,1024]{1,0:T(8,128)(2,1)S(1)}, bf16[400,1024]{1,0:T(8,128)(2,1)S(1)}, u32[]{:S(2)}, u32[]{:S(2)}) collective-permute-start(bf16[400,1024]{1,0:T(8,128)(2,1)S(1)} %get-tuple-element.72), channel_id=1, source_target_pairs={{0,1},{1,0},{2,3},{3,2},{4,5},{5,4},{6,7},{7,6},{8,9},{9,8},{10,11... | collective-permute-start | bytes 2457608 | tf_op jit(solution)/shard_map/ppermute | solution.py:466
  51.7 5.4 %copy-start.2 = (bf16[2,384,1024]{2,1,0:T(8,128)(2,1)}, bf16[2,384,1024]{2,1,0:T(8,128)(2,1)S(1)}, u32[]{:S(2)}) copy-start(bf16[2,384,1024]{2,1,0:T(8,128)(2,1)S(1)} %get-tuple-element.69.units_any) | copy-start | bytes 4718596
  51.7 2.3 %collective-permute-start.9 = (bf16[320,1152]{1,0:T(8,128)(2,1)S(1)}, bf16[320,1152]{1,0:T(8,128)(2,1)S(1)}, u32[]{:S(2)}, u32[]{:S(2)}) collective-permute-start(bf16[320,1152]{1,0:T(8,128)(2,1)S(1)} %get-tuple-element.63.mine_any), channel_id=1, source_target_pairs={{0,1},{1,0},{2,3},{3,2},{4,5},{5,4},{6,7},{7,6},{8,9},{9,8},{10,11... | collective-permute-start | bytes 2211848 | tf_op jit(solution)/shard_map/ppermute | solution.py:466
  51.9 23.5 %collective-permute-start.15 = (bf16[384,1024]{1,0:T(8,128)(2,1)S(1)}, bf16[384,1024]{1,0:T(8,128)(2,1)S(1)}, u32[]{:S(2)}, u32[]{:S(2)}) collective-permute-start(bf16[384,1024]{1,0:T(8,128)(2,1)S(1)} %get-tuple-element.82.last_any), channel_id=1, source_target_pairs={{4,0},{5,1},{6,2},{7,3},{8,12},{9,13},{10,14},{11,15},{20,16},{21,... | collective-permute-start | bytes 2359304 | tf_op jit(solution)/shard_map/ppermute | solution.py:466
  57.1 1.2 %collective-permute-start.10 = (f32[8,128]{1,0:T(8,128)S(1)}, f32[8,128]{1,0:T(8,128)S(1)}, u32[]{:S(2)}, u32[]{:S(2)}) collective-permute-start(f32[8,128]{1,0:T(8,128)S(1)} %get-tuple-element.66), channel_id=1, source_target_pairs={{0,1},{1,0},{2,3},{3,2},{4,5},{5,4},{6,7},{7,6},{8,9},{9,8},{10,11... | collective-permute-start | bytes 12296 | tf_op jit(solution)/shard_map/ppermute | solution.py:466
  57.3 10.7 %collective-permute-start.14 = (bf16[112,1024]{1,0:T(8,128)(2,1)S(1)}, bf16[112,1024]{1,0:T(8,128)(2,1)S(1)}, u32[]{:S(2)}, u32[]{:S(2)}) collective-permute-start(bf16[112,1024]{1,0:T(8,128)(2,1)S(1)} %get-tuple-element.76), channel_id=1, source_target_pairs={{0,3},{1,2},{2,1},{3,0},{4,7},{5,6},{6,5},{7,4},{8,11},{9,10},{10,... | collective-permute-start | bytes 688136 | tf_op jit(solution)/shard_map/ppermute | solution.py:466
  58.4 6.9 %collective-permute-start.11 = (f32[4,128]{1,0:T(4,128)S(1)}, f32[4,128]{1,0:T(4,128)S(1)}, u32[]{:S(2)}, u32[]{:S(2)}) collective-permute-start(f32[4,128]{1,0:T(4,128)S(1)} %slice.19), channel_id=1, source_target_pairs={{0,2},{1,3},{2,0},{3,1},{4,6},{5,7},{6,4},{7,5},{8,10},{9,11},{10,... | collective-permute-start | bytes 6152 | tf_op jit(solution)/shard_map/ppermute | solution.py:466
  65.3 5.5 %collective-permute-start.13 = (f32[2,128]{1,0:T(2,128)S(1)}, f32[2,128]{1,0:T(2,128)S(1)}, u32[]{:S(2)}, u32[]{:S(2)}) collective-permute-start(f32[2,128]{1,0:T(2,128)S(1)} %slice.21), channel_id=1, source_target_pairs={{0,12},{1,13},{2,14},{3,15},{4,8},{5,9},{6,10},{7,11},{8,4},{9,5},... | collective-permute-start | bytes 3080 | tf_op jit(solution)/shard_map/ppermute | solution.py:466
  70.9 7.6 %copy-start.1 = (bf16[1024,1024]{1,0:T(8,128)(2,1)S(1)}, bf16[1024,1024]{1,0:T(8,128)(2,1)}, u32[]{:S(2)}) copy-start(bf16[1024,1024]{1,0:T(8,128)(2,1)} %cent_ref.5) | copy-start | bytes 6291460
  76.5 5.7 %collective-permute-start.19 = (f32[1,128]{1,0:T(1,128)S(1)}, f32[1,128]{1,0:T(1,128)S(1)}, u32[]{:S(2)}, u32[]{:S(2)}) collective-permute-start(f32[1,128]{1,0:T(1,128)S(1)} %slice.23), channel_id=1, source_target_pairs={{0,4},{1,5},{2,6},{3,7},{4,0},{5,1},{6,2},{7,3},{8,12},{9,13},{10,... | collective-permute-start | bytes 1544 | tf_op jit(solution)/shard_map/ppermute | solution.py:466
  76.6 5.6 %collective-permute-start.16 = (f32[8,128]{1,0:T(8,128)S(1)}, f32[8,128]{1,0:T(8,128)S(1)}, u32[]{:S(2)}, u32[]{:S(2)}) collective-permute-start(f32[8,128]{1,0:T(8,128)S(1)} %get-tuple-element.88), channel_id=1, source_target_pairs={{0,1},{1,0},{2,3},{3,2},{4,5},{5,4},{6,7},{7,6},{8,9},{9,8},{10,11... | collective-permute-start | bytes 12296 | tf_op jit(solution)/shard_map/ppermute | solution.py:466
  76.7 5.5 %collective-permute-start.17 = (f32[8,128]{1,0:T(8,128)S(1)}, f32[8,128]{1,0:T(8,128)S(1)}, u32[]{:S(2)}, u32[]{:S(2)}) collective-permute-start(f32[8,128]{1,0:T(8,128)S(1)} %get-tuple-element.89), channel_id=1, source_target_pairs={{0,2},{1,3},{2,0},{3,1},{4,6},{5,7},{6,4},{7,5},{8,10},{9,11},{10,... | collective-permute-start | bytes 12296 | tf_op jit(solution)/shard_map/ppermute | solution.py:466
  76.9 5.3 %collective-permute-start.18 = (f32[8,128]{1,0:T(8,128)S(1)}, f32[8,128]{1,0:T(8,128)S(1)}, u32[]{:S(2)}, u32[]{:S(2)}) collective-permute-start(f32[8,128]{1,0:T(8,128)S(1)} %get-tuple-element.90), channel_id=1, source_target_pairs={{0,3},{1,2},{2,1},{3,0},{4,7},{5,6},{6,5},{7,4},{8,11},{9,10},{10,... | collective-permute-start | bytes 12296 | tf_op jit(solution)/shard_map/ppermute | solution.py:466

commit v6 on v4

--- a/solution.py
+++ b/solution.py
@@ -288,8 +288,8 @@
     block = sum((spot >= piece * step).astype(jnp.int32) for step in range(1, 16))
     together = jnp.where(spot - block * piece == lax.broadcasted_iota(jnp.int32, (count, 128), 1), 1.0, 0.0)
     share = jnp.dot(apart, together, precision=lax.Precision.HIGHEST, preferred_element_type=jnp.float32)
-    share_low[...] = share[0:8, :]
-    share_high[...] = share[8:16, :]
+    share_low[...] = jnp.concatenate([share[0:4, :], share[8:12, :]], axis=0)
+    share_high[...] = jnp.concatenate([share[4:8, :], share[12:16, :]], axis=0)
 
 
 def update_kernel(after, scaled, facts, cent_ref, prior_ref, fresh_rows, fresh_counts):
@@ -377,7 +377,7 @@
 
 
 def late_kernel(
-    cap, per, scaled, facts_in, any0, any1, any2, any3, after, packed, floors, rows0, rows1, rows2, rows3, sems
+    cap, per, scaled, facts_in, any0, any1, any2, any3, after, updated, packed, floors, rows0, rows1, rows2, rows3, sems
 ):
     me, z, y, core = position()
     part = per * cap
@@ -528,7 +528,7 @@
         in_specs=[ANY, ANY, VMEM],
         cost_estimate=lasting(3),
     )(mine, other, unit_old)
-    share = share + exchange(share_high, 1)
+    share = share + exchange(share_high, 2)
 
     def gather(share, apart):
         half = share.shape[0] // 2
@@ -549,15 +549,18 @@
         in_specs=[VMEM, VMEM] + [ANY] * 7,
         cost_estimate=lasting(7),
     )(scaled, facts, units, cross_set, passed, rows0, rows1, early2, early3)
-    share, early = in_order(gather(share, 2), early)
+    share, early = in_order(gather(share, 1), early)
+    new_centroids, counts = call(
+        update_kernel, (shape((rows, width), bf16), shape((1, rows), i32)), in_specs=[ANY] + [VMEM] * 4
+    )(early, scaled, facts, centroids, prior_row)
     kept = shape((1, per, 4 * cap, width), bf16)
     kept_rows, floors = call(
         functools.partial(late_kernel, cap, per),
         (kept, shape((1, per, 4 * cap, 128), bf16)),
         [room(rows_of(1))] * 4 + [pltpu.SemaphoreType.DMA((4,))],
-        in_specs=[VMEM] * 2 + [ANY] * 5,
+        in_specs=[VMEM] * 2 + [ANY] * 6,
         cost_estimate=lasting(3),
-    )(scaled, facts, rows0, rows1, late2, late3, early)
+    )(scaled, facts, rows0, rows1, late2, late3, early, counts)
     share, kept_rows = in_order(gather(share, 12), kept_rows)
     tile = shape((8, 4 * cap), f32)
     tiles = call(
@@ -567,10 +570,6 @@
         in_specs=[VMEM, VMEM, ANY, ANY, ANY],
         cost_estimate=lasting(1),
     )(early, floors, kept_rows, last_set, far_set)
-    share, *tiles = in_order(share, *tiles)
-    new_centroids, counts = call(
-        update_kernel, (shape((rows, width), bf16), shape((1, rows), i32)), in_specs=[ANY] + [VMEM] * 4
-    )(tiles[0], scaled, facts, centroids, prior_row)
     tiles = [tile if r == 0 else exchange(tile, r) for r, tile in enumerate(tiles)]
     share = gather(share, 4)
     density, level_two = call(

time: 83.5 us -> 83.9 us (level)
  waiting for transfers between devices: 29.6 us -> 26.1 us
  starting transfers between devices: 25.3 us -> 27.5 us
    ppermute x21, waiting for transfers between devices: 29.6 us -> 26.1 us  [exchange(): return lax.ppermute(value, 'shard', [(i, i ^ apart) for i in sources])]
    ppermute x21, starting transfers between devices: 25.3 us -> 27.5 us  [exchange(): return lax.ppermute(value, 'shard', [(i, i ^ apart) for i in sources])]
    pallas_call x15 -> x14, Pallas kernels: 27.3 us -> 28.1 us  [run(): pl.pallas_call(kernel, out_shape=outs, in_specs=specs, scratch_shapes=lis...]
  transfers between devices with their start and end apart: 21 -> 21, of which waited for: 7 -> 8; matrix products, arithmetic and copies ran while one was open for 0% -> 0% of each run, Pallas kernels for 30% -> 32%
where the time goes in v6:
time: 83.9 us; the launch traced here: 83.5 us
  Pallas kernels  28.1 us (33%)
  starting transfers between devices  27.5 us (33%)
  waiting for transfers between devices  26.1 us (31%)
  between operations  0.95 us (1%)
    pallas_call x14, Pallas kernels, run(): pl.pallas_call(kernel, out_shape=outs, in_specs=specs, scratch_shapes=lis...  28.1 us
    ppermute x21, starting transfers between devices, exchange(): return lax.ppermute(value, 'shard', [(i, i ^ apart) for i in sources])  27.5 us
    ppermute x21, waiting for transfers between devices, exchange(): return lax.ppermute(value, 'shard', [(i, i ^ apart) for i in sources])  26.1 us
  transfers between devices with their start and end apart: 21, of which 8 were waited for; matrix products, arithmetic and copies ran while one was open for 0% of the time, Pallas kernels for 32%

profile of v6, /device:TPU:0, one launch (start us, length us, event | category | flops | bytes accessed | tf_op | source)
XLA Modules:
  0.0 83.5 jit_solution(16754377465008124343)
XLA Ops:
  0.6 0.0 copy-start
  0.6 0.0 copy-start.7
  0.7 3.1 %collective-permute-start = (bf16[384,1024]{1,0:T(8,128)(2,1)}, bf16[384,1024]{1,0:T(8,128)(2,1)S(1)}, u32[]{:S(2)}, u32[]{:S(2)}) collective-permute-start(bf16[384,1024]{1,0:T(8,128)(2,1)} %own_any.1), channel_id=1, source_target_pairs={{0,4},{1,5},{2,6},{3,7},{4,0},{5,1},{6,2},{7,3},{8,12},{9,13},{10,... | collective-permute-start | bytes 2359304 | tf_op jit(solution)/shard_map/ppermute | solution.py:466
  3.7 0.7 collective-permute-start.1
  4.5 3.4 %shard_map.102 = (bf16[40,1152]{1,0:T(8,128)(2,1)S(1)}, bf16[304,1024]{1,0:T(8,128)(2,1)S(1)}, bf16[304,1024]{1,0:T(8,128)(2,1)S(1)}, s32[8,1024]{1,0:T(8,128)S(1)}) custom-call(s32[1,1024]{1,0:T(1,128)} %bitcast.11, bf16[40,1024]{1,0:T(8,128)(2,1)} %emb_any.1, s32[8,40]{1,0:T(8,128)} %bitcast.12, s32[1,40]{1,0:T(1,128)} %bitcast.13, s32[1,1024]{1,0:T(1,128)} %bitcast.7, ...), custom_call_target="tpu_custom_call" | custom-call | tf_op jit(solution)/shard_map/pallas_call | solution.py:432
  7.8 4.4 %collective-permute-start.2 = (bf16[40,1152]{1,0:T(8,128)(2,1)S(1)}, bf16[40,1152]{1,0:T(8,128)(2,1)S(1)}, u32[]{:S(2)}, u32[]{:S(2)}) collective-permute-start(bf16[40,1152]{1,0:T(8,128)(2,1)S(1)} %get-tuple-element.48), channel_id=1, source_target_pairs={{0,4},{1,5},{2,6},{3,7},{4,0},{5,1},{6,2},{7,3},{8,12},{9,13},{10,... | collective-permute-start | bytes 276488 | tf_op jit(solution)/shard_map/ppermute | solution.py:466
  12.3 1.5 %collective-permute-start.6 = (bf16[304,1024]{1,0:T(8,128)(2,1)S(1)}, bf16[304,1024]{1,0:T(8,128)(2,1)S(1)}, u32[]{:S(2)}, u32[]{:S(2)}) collective-permute-start(bf16[304,1024]{1,0:T(8,128)(2,1)S(1)} %get-tuple-element.53), channel_id=1, source_target_pairs={{0,2},{1,3},{2,0},{3,1},{4,6},{5,7},{6,4},{7,5},{8,10},{9,11},{10,... | collective-permute-start | bytes 1867784 | tf_op jit(solution)/shard_map/ppermute | solution.py:466
  13.8 0.0 collective-permute-start.7
  13.8 0.0 copy-done
  13.8 0.0 copy-done.7
  13.8 3.7 %shard_map.103 = (bf16[400,1024]{1,0:T(8,128)(2,1)S(1)}, bf16[400,1024]{1,0:T(8,128)(2,1)}, bf16[112,1024]{1,0:T(8,128)(2,1)S(1)}, bf16[112,1024]{1,0:T(8,128)(2,1)S(1)}) custom-call(s32[8,1024]{1,0:T(8,128)S(1)} %get-tuple-element.47.info, s32[1,1024]{1,0:T(1,128)S(1)} %bitcast.8, bf16[1024,1024]{1,0:T(8,128)(2,1)S(1)} %copy-done), custom_call_target="tpu_custom_call" | custom-call | tf_op jit(solution)/shard_map/pallas_call | solution.py:432
  17.5 6.0 %collective-permute-done.2 = bf16[40,1152]{1,0:T(8,128)(2,1)S(1)} collective-permute-done((bf16[40,1152]{1,0:T(8,128)(2,1)S(1)}, bf16[40,1152]{1,0:T(8,128)(2,1)S(1)}, u32[]{:S(2)}, u32[]{:S(2)}) %collective-permute-start.2) | collective-permute-done | bytes 92192 | tf_op jit(solution)/shard_map/ppermute | solution.py:466
  23.5 0.0 collective-permute-done.refs_0_
  23.5 0.0 collective-permute-done.1.refs_1_
  23.5 3.8 %collective-permute-start.5 = (bf16[80,1152]{1,0:T(8,128)(2,1)S(1)}, bf16[80,1152]{1,0:T(8,128)(2,1)S(1)}, u32[]{:S(2)}, u32[]{:S(2)}) collective-permute-start(bf16[80,1152]{1,0:T(8,128)(2,1)S(1)} %get-tuple-element.52), channel_id=1, source_target_pairs={{0,12},{1,13},{2,14},{3,15},{4,8},{5,9},{6,10},{7,11},{8,4},{9,5},... | collective-permute-start | bytes 552968 | tf_op jit(solution)/shard_map/ppermute | solution.py:466
  27.4 1.3 %collective-permute-start.3 = (bf16[384,1024]{1,0:T(8,128)(2,1)S(1)}, bf16[384,1024]{1,0:T(8,128)(2,1)S(1)}, u32[]{:S(2)}, u32[]{:S(2)}) collective-permute-start(bf16[384,1024]{1,0:T(8,128)(2,1)S(1)} %get-tuple-element.50.cross_any), channel_id=1, source_target_pairs={{4,0},{5,1},{6,2},{7,3},{8,12},{9,13},{10,14},{11,15},{20,16},{21,... | collective-permute-start | bytes 2359304 | tf_op jit(solution)/shard_map/ppermute | solution.py:466
  28.6 1.6 %collective-permute-start.4 = (bf16[384,1024]{1,0:T(8,128)(2,1)S(1)}, bf16[384,1024]{1,0:T(8,128)(2,1)}, u32[]{:S(2)}, u32[]{:S(2)}) collective-permute-start(bf16[384,1024]{1,0:T(8,128)(2,1)S(1)} %get-tuple-element.51.near_any), channel_id=1, source_target_pairs={{4,8},{5,9},{6,10},{7,11},{8,4},{9,5},{10,6},{11,7},{20,24},{21,25... | collective-permute-start | bytes 2359304 | tf_op jit(solution)/shard_map/ppermute | solution.py:466
  30.2 1.2 %collective-permute-done.5 = bf16[80,1152]{1,0:T(8,128)(2,1)S(1)} collective-permute-done((bf16[80,1152]{1,0:T(8,128)(2,1)S(1)}, bf16[80,1152]{1,0:T(8,128)(2,1)S(1)}, u32[]{:S(2)}, u32[]{:S(2)}) %collective-permute-start.5) | collective-permute-done | bytes 184352 | tf_op jit(solution)/shard_map/ppermute | solution.py:466
  31.4 0.0 collective-permute-done.6.refs_1_
  31.4 8.1 %collective-permute-done.7.refs_2_ = bf16[304,1024]{1,0:T(8,128)(2,1)S(1)} collective-permute-done((bf16[304,1024]{1,0:T(8,128)(2,1)S(1)}, bf16[304,1024]{1,0:T(8,128)(2,1)S(1)}, u32[]{:S(2)}, u32[]{:S(2)}) %collective-permute-start.7) | collective-permute-done | bytes 622624 | tf_op jit(solution)/shard_map/ppermute | solution.py:466
  39.6 0.5 collective-permute-start.8
  40.1 3.2 %shard_map.106 = (bf16[1024,1024]{1,0:T(8,128)(2,1)S(1)}, bf16[2,384,1024]{2,1,0:T(8,128)(2,1)S(1)}) custom-call(bf16[1024,1024]{1,0:T(8,128)(2,1)} %cent_ref.5, bf16[384,1024]{1,0:T(8,128)(2,1)} %own_any.1, bf16[384,1024]{1,0:T(8,128)(2,1)S(1)} %get-tuple-element.51.near_any), custom_call_target="tpu_custom_call" | custom-call | tf_op jit(solution)/shard_map/pallas_call | solution.py:432
  43.3 0.0 copy-done.3
  43.3 0.0 copy-done.5
  43.3 1.9 %collective-permute-start.12 = (bf16[400,1024]{1,0:T(8,128)(2,1)}, bf16[400,1024]{1,0:T(8,128)(2,1)S(1)}, u32[]{:S(2)}, u32[]{:S(2)}) collective-permute-start(bf16[400,1024]{1,0:T(8,128)(2,1)} %get-tuple-element.70), channel_id=1, source_target_pairs={{0,1},{1,0},{2,3},{3,2},{4,5},{5,4},{6,7},{7,6},{8,9},{9,8},{10,11... | collective-permute-start | bytes 2457608 | tf_op jit(solution)/shard_map/ppermute | solution.py:466
  45.2 5.7 %collective-permute-done.8 = bf16[160,1152]{1,0:T(8,128)(2,1)S(1)} collective-permute-done((bf16[160,1152]{1,0:T(8,128)(2,1)S(1)}, bf16[160,1152]{1,0:T(8,128)(2,1)S(1)}, u32[]{:S(2)}, u32[]{:S(2)}) %collective-permute-start.8) | collective-permute-done | bytes 368672 | tf_op jit(solution)/shard_map/ppermute | solution.py:466
  50.9 0.1 pad_maximum_fusion.refs_2_
  51.0 0.0 collective-permute-done.3.refs_0_
  51.0 0.0 collective-permute-done.4.refs_1_
  51.0 0.0 copy-start.2
  51.0 0.2 collective-permute-start.9
  51.2 1.3 %collective-permute-start.16 = (bf16[384,1024]{1,0:T(8,128)(2,1)}, bf16[384,1024]{1,0:T(8,128)(2,1)S(1)}, u32[]{:S(2)}, u32[]{:S(2)}) collective-permute-start(bf16[384,1024]{1,0:T(8,128)(2,1)} %get-tuple-element.81.last_any), channel_id=1, source_target_pairs={{4,0},{5,1},{6,2},{7,3},{8,12},{9,13},{10,14},{11,15},{20,16},{21,... | collective-permute-start | bytes 2359304 | tf_op jit(solution)/shard_map/ppermute | solution.py:466
  52.5 0.8 collective-permute-done.9.other_any
  53.3 3.1 %shard_map.108 = (bf16[640,1024]{1,0:T(8,128)(2,1)S(1)}, s32[16,640]{1,0:T(8,128)S(1)}, f32[8,128]{1,0:T(8,128)S(1)}, f32[8,128]{1,0:T(8,128)S(1)}) custom-call(bf16[320,1152]{1,0:T(8,128)(2,1)S(1)} %get-tuple-element.61.mine_any, bf16[320,1152]{1,0:T(8,128)(2,1)S(1)} %collective-permute-done.9.other_any, bf16[1024,1024]{1,0:T(8,128)(2,1)S(1)} %get-tuple-element.62.unit_old), custom_call_target="tpu_custom_call" | custom-call | bytes 11070000 | tf_op jit(solution)/shard_map/pallas_call | solution.py:432
  56.5 0.1 collective-permute-start.10
  56.6 1.9 %collective-permute-start.13 = (bf16[112,1024]{1,0:T(8,128)(2,1)S(1)}, bf16[112,1024]{1,0:T(8,128)(2,1)S(1)}, u32[]{:S(2)}, u32[]{:S(2)}) collective-permute-start(bf16[112,1024]{1,0:T(8,128)(2,1)S(1)} %get-tuple-element.74), channel_id=1, source_target_pairs={{0,2},{1,3},{2,0},{3,1},{4,6},{5,7},{6,4},{7,5},{8,10},{9,11},{10,... | collective-permute-start | bytes 688136 | tf_op jit(solution)/shard_map/ppermute | solution.py:466
  58.5 0.0 collective-permute-start.14
  58.5 1.6 %collective-permute-done.10 = f32[8,128]{1,0:T(8,128)S(1)} collective-permute-done((f32[8,128]{1,0:T(8,128)S(1)}, f32[8,128]{1,0:T(8,128)S(1)}, u32[]{:S(2)}, u32[]{:S(2)}) %collective-permute-start.10) | collective-permute-done | bytes 4128 | tf_op jit(solution)/shard_map/ppermute | solution.py:466
  60.1 0.0 collective-permute-start.11
  60.1 0.0 collective-permute-done.12.any1
  60.2 0.0 copy-done.4
  60.2 0.0 copy-done.6
  60.2 0.0 copy-start.1
  60.2 6.0 %shard_map.109.refs_1_ = f32[24,128]{1,0:T(8,128)S(1)} custom-call(bf16[640,1024]{1,0:T(8,128)(2,1)S(1)} %get-tuple-element.65.scaled, s32[16,640]{1,0:T(8,128)S(1)} %get-tuple-element.66.facts_in.facts, bf16[2,384,1024]{2,1,0:T(8,128)(2,1)} %copy-done.2, bf16[384,1024]{1,0:T(8,128)(2,1)S(1)} %get-tuple-element.50.cross_any, ...), custom_call_target="tpu_custom_call" | custom-call | bytes 25830000 | tf_op jit(solution)/shard_map/pallas_call | solution.py:432
  66.2 0.0 collective-permute-done.11
  66.3 1.3 %collective-permute-start.15 = (f32[2,128]{1,0:T(2,128)S(1)}, f32[2,128]{1,0:T(2,128)S(1)}, u32[]{:S(2)}, u32[]{:S(2)}) collective-permute-start(f32[2,128]{1,0:T(2,128)S(1)} %slice.21), channel_id=1, source_target_pairs={{0,12},{1,13},{2,14},{3,15},{4,8},{5,9},{6,10},{7,11},{8,4},{9,5},... | collective-permute-start | bytes 3080 | tf_op jit(solution)/shard_map/ppermute | solution.py:466
  67.6 0.0 copy-done.1
  67.6 3.7 %shard_map.111 = (bf16[1024,1024]{1,0:T(8,128)(2,1)}, s32[1,1024]{1,0:T(1,128)}) custom-call(f32[24,128]{1,0:T(8,128)S(1)} %get-tuple-element.73.after.early, bf16[640,1024]{1,0:T(8,128)(2,1)S(1)} %get-tuple-element.65.scaled, s32[16,640]{1,0:T(8,128)S(1)} %get-tuple-element.66.facts_in.facts, bf16[1024,1024]{1,0:T(8,128)(2,1)S(1)} %copy-done.1, ...), custom_call_target="tpu_custom_call" | custom-call | tf_op jit(solution)/shard_map/pallas_call | solution.py:432
  71.3 0.0 collective-permute-done.13.any2
  71.3 0.0 collective-permute-done.14.any3
  71.3 0.7 copy-done.8
  72.0 2.8 %shard_map.112 = (bf16[1,3,128,1024]{3,2,1,0:T(8,128)(2,1)S(1)}, bf16[1,3,128,128]{3,2,1,0:T(8,128)(2,1)S(1)}) custom-call(bf16[640,1024]{1,0:T(8,128)(2,1)S(1)} %get-tuple-element.65.scaled, s32[16,640]{1,0:T(8,128)S(1)} %get-tuple-element.66.facts_in.facts, bf16[400,1024]{1,0:T(8,128)(2,1)S(1)} %get-tuple-element.69.any0, ...), custom_call_target="tpu_custom_call" | custom-call | bytes 11070000 | tf_op jit(solution)/shard_map/pallas_call | solution.py:432
  74.8 0.0 collective-permute-done.15
  74.8 2.0 %collective-permute-start.20 = (f32[1,128]{1,0:T(1,128)S(1)}, f32[1,128]{1,0:T(1,128)S(1)}, u32[]{:S(2)}, u32[]{:S(2)}) collective-permute-start(f32[1,128]{1,0:T(1,128)S(1)} %slice.23), channel_id=1, source_target_pairs={{0,4},{1,5},{2,6},{3,7},{4,0},{5,1},{6,2},{7,3},{8,12},{9,13},{10,... | collective-permute-start | bytes 1544 | tf_op jit(solution)/shard_map/ppermute | solution.py:466
  76.8 0.0 collective-permute-done.16.far_any
  76.8 1.1 %shard_map.114 = (f32[8,128]{1,0:T(8,128)S(1)}, f32[8,128]{1,0:T(8,128)S(1)}, f32[8,128]{1,0:T(8,128)S(1)}, f32[8,128]{1,0:T(8,128)S(1)}) custom-call(f32[24,128]{1,0:T(8,128)S(1)} %get-tuple-element.73.after.early, bf16[1,3,128,128]{3,2,1,0:T(8,128)(2,1)S(1)} %get-tuple-element.77.floors, bf16[1,3,128,1024]{3,2,1,0:T(8,128)(2,1)S(1)} %get-tuple-element.80.kept_any, ...), custom_call_target="tpu_custom_call" | custom-call | bytes 3690000 | tf_op jit(solution)/shard_map/pallas_call | solution.py:432
  77.9 0.1 collective-permute-start.17
  78.0 1.5 %collective-permute-start.18 = (f32[8,128]{1,0:T(8,128)S(1)}, f32[8,128]{1,0:T(8,128)S(1)}, u32[]{:S(2)}, u32[]{:S(2)}) collective-permute-start(f32[8,128]{1,0:T(8,128)S(1)} %get-tuple-element.84), channel_id=1, source_target_pairs={{0,2},{1,3},{2,0},{3,1},{4,6},{5,7},{6,4},{7,5},{8,10},{9,11},{10,... | collective-permute-start | bytes 12296 | tf_op jit(solution)/shard_map/ppermute | solution.py:466
  79.5 0.4 collective-permute-start.19
  79.8 0.0 collective-permute-done.20
  79.9 0.0 collective-permute-done.17.got1
  79.9 1.8 %collective-permute-done.18.got2 = f32[8,128]{1,0:T(8,128)S(1)} collective-permute-done((f32[8,128]{1,0:T(8,128)S(1)}, f32[8,128]{1,0:T(8,128)S(1)}, u32[]{:S(2)}, u32[]{:S(2)}) %collective-permute-start.18) | collective-permute-done | bytes 4128 | tf_op jit(solution)/shard_map/ppermute | solution.py:466
  81.7 0.8 collective-permute-done.19.got3
  82.5 1.0 %shard_map.115 = (f32[1,40]{1,0:T(1,128)}, f32[1,1024]{1,0:T(1,128)}) custom-call(s32[8,1024]{1,0:T(8,128)S(1)} %get-tuple-element.47.info, f32[8,128]{1,0:T(8,128)S(1)} %get-tuple-element.82.got0, f32[8,128]{1,0:T(8,128)S(1)} %collective-permute-done.17.got1, f32[8,128]{1,0:T(8,128)S(1)} %collective-permute-done.18.got2, ...), custom_call_target="tpu_custom_call" | custom-call | tf_op jit(solution)/shard_map/pallas_call | solution.py:432
  (20 shorter events, 0.1 us)
Async XLA Ops:
  0.6 13.1 %copy-start = (bf16[1024,1024]{1,0:T(8,128)(2,1)S(1)}, bf16[1024,1024]{1,0:T(8,128)(2,1)}, u32[]{:S(2)}) copy-start(bf16[1024,1024]{1,0:T(8,128)(2,1)} %cent_ref.5) | copy-start | bytes 6291460
  0.6 13.1 %copy-start.7 = (s32[1024]{0:T(1024)S(1)}, s32[1024]{0:T(1024)}, u32[]{:S(2)}) copy-start(s32[1024]{0:T(1024)} %param.10) | copy-start | bytes 12292
  0.7 22.8 %collective-permute-start = (bf16[384,1024]{1,0:T(8,128)(2,1)}, bf16[384,1024]{1,0:T(8,128)(2,1)S(1)}, u32[]{:S(2)}, u32[]{:S(2)}) collective-permute-start(bf16[384,1024]{1,0:T(8,128)(2,1)} %own_any.1), channel_id=1, source_target_pairs={{0,4},{1,5},{2,6},{3,7},{4,0},{5,1},{6,2},{7,3},{8,12},{9,13},{10,... | collective-permute-start | bytes 2359304 | tf_op jit(solution)/shard_map/ppermute | solution.py:466
  3.7 19.8 %collective-permute-start.1 = (bf16[384,1024]{1,0:T(8,128)(2,1)}, bf16[384,1024]{1,0:T(8,128)(2,1)S(1)}, u32[]{:S(2)}, u32[]{:S(2)}) collective-permute-start(bf16[384,1024]{1,0:T(8,128)(2,1)} %own_any.1), channel_id=1, source_target_pairs={{4,8},{5,9},{6,10},{7,11},{8,4},{9,5},{10,6},{11,7},{20,24},{21,25... | collective-permute-start | bytes 2359304 | tf_op jit(solution)/shard_map/ppermute | solution.py:466
  7.8 15.6 %collective-permute-start.2 = (bf16[40,1152]{1,0:T(8,128)(2,1)S(1)}, bf16[40,1152]{1,0:T(8,128)(2,1)S(1)}, u32[]{:S(2)}, u32[]{:S(2)}) collective-permute-start(bf16[40,1152]{1,0:T(8,128)(2,1)S(1)} %get-tuple-element.48), channel_id=1, source_target_pairs={{0,4},{1,5},{2,6},{3,7},{4,0},{5,1},{6,2},{7,3},{8,12},{9,13},{10,... | collective-permute-start | bytes 276488 | tf_op jit(solution)/shard_map/ppermute | solution.py:466
  12.3 19.2 %collective-permute-start.6 = (bf16[304,1024]{1,0:T(8,128)(2,1)S(1)}, bf16[304,1024]{1,0:T(8,128)(2,1)S(1)}, u32[]{:S(2)}, u32[]{:S(2)}) collective-permute-start(bf16[304,1024]{1,0:T(8,128)(2,1)S(1)} %get-tuple-element.53), channel_id=1, source_target_pairs={{0,2},{1,3},{2,0},{3,1},{4,6},{5,7},{6,4},{7,5},{8,10},{9,11},{10,... | collective-permute-start | bytes 1867784 | tf_op jit(solution)/shard_map/ppermute | solution.py:466
  13.8 25.8 %collective-permute-start.7 = (bf16[304,1024]{1,0:T(8,128)(2,1)S(1)}, bf16[304,1024]{1,0:T(8,128)(2,1)S(1)}, u32[]{:S(2)}, u32[]{:S(2)}) collective-permute-start(bf16[304,1024]{1,0:T(8,128)(2,1)S(1)} %get-tuple-element.54), channel_id=1, source_target_pairs={{0,3},{1,2},{2,1},{3,0},{4,7},{5,6},{6,5},{7,4},{8,11},{9,10},{10,... | collective-permute-start | bytes 1867784 | tf_op jit(solution)/shard_map/ppermute | solution.py:466
  23.5 7.9 %collective-permute-start.5 = (bf16[80,1152]{1,0:T(8,128)(2,1)S(1)}, bf16[80,1152]{1,0:T(8,128)(2,1)S(1)}, u32[]{:S(2)}, u32[]{:S(2)}) collective-permute-start(bf16[80,1152]{1,0:T(8,128)(2,1)S(1)} %get-tuple-element.52), channel_id=1, source_target_pairs={{0,12},{1,13},{2,14},{3,15},{4,8},{5,9},{6,10},{7,11},{8,4},{9,5},... | collective-permute-start | bytes 552968 | tf_op jit(solution)/shard_map/ppermute | solution.py:466
  27.4 23.6 %collective-permute-start.3 = (bf16[384,1024]{1,0:T(8,128)(2,1)S(1)}, bf16[384,1024]{1,0:T(8,128)(2,1)S(1)}, u32[]{:S(2)}, u32[]{:S(2)}) collective-permute-start(bf16[384,1024]{1,0:T(8,128)(2,1)S(1)} %get-tuple-element.50.cross_any), channel_id=1, source_target_pairs={{4,0},{5,1},{6,2},{7,3},{8,12},{9,13},{10,14},{11,15},{20,16},{21,... | collective-permute-start | bytes 2359304 | tf_op jit(solution)/shard_map/ppermute | solution.py:466
  28.6 22.4 %collective-permute-start.4 = (bf16[384,1024]{1,0:T(8,128)(2,1)S(1)}, bf16[384,1024]{1,0:T(8,128)(2,1)}, u32[]{:S(2)}, u32[]{:S(2)}) collective-permute-start(bf16[384,1024]{1,0:T(8,128)(2,1)S(1)} %get-tuple-element.51.near_any), channel_id=1, source_target_pairs={{4,8},{5,9},{6,10},{7,11},{8,4},{9,5},{10,6},{11,7},{20,24},{21,25... | collective-permute-start | bytes 2359304 | tf_op jit(solution)/shard_map/ppermute | solution.py:466
  39.6 3.8 %copy-start.3 = (bf16[304,1024]{1,0:T(8,128)(2,1)}, bf16[304,1024]{1,0:T(8,128)(2,1)S(1)}, u32[]{:S(2)}) copy-start(bf16[304,1024]{1,0:T(8,128)(2,1)S(1)} %get-tuple-element.71.any2) | copy-start | bytes 1867780
  39.6 3.8 %copy-start.5 = (bf16[304,1024]{1,0:T(8,128)(2,1)}, bf16[304,1024]{1,0:T(8,128)(2,1)S(1)}, u32[]{:S(2)}) copy-start(bf16[304,1024]{1,0:T(8,128)(2,1)S(1)} %get-tuple-element.72.any3) | copy-start | bytes 1867780
  39.6 11.4 %collective-permute-start.8 = (bf16[160,1152]{1,0:T(8,128)(2,1)S(1)}, bf16[160,1152]{1,0:T(8,128)(2,1)S(1)}, u32[]{:S(2)}, u32[]{:S(2)}) collective-permute-start(bf16[160,1152]{1,0:T(8,128)(2,1)S(1)} %get-tuple-element.58), channel_id=1, source_target_pairs={{0,2},{1,3},{2,0},{3,1},{4,6},{5,7},{6,4},{7,5},{8,10},{9,11},{10,... | collective-permute-start | bytes 1105928 | tf_op jit(solution)/shard_map/ppermute | solution.py:466
  43.3 16.8 %collective-permute-start.12 = (bf16[400,1024]{1,0:T(8,128)(2,1)}, bf16[400,1024]{1,0:T(8,128)(2,1)S(1)}, u32[]{:S(2)}, u32[]{:S(2)}) collective-permute-start(bf16[400,1024]{1,0:T(8,128)(2,1)} %get-tuple-element.70), channel_id=1, source_target_pairs={{0,1},{1,0},{2,3},{3,2},{4,5},{5,4},{6,7},{7,6},{8,9},{9,8},{10,11... | collective-permute-start | bytes 2457608 | tf_op jit(solution)/shard_map/ppermute | solution.py:466
  51.0 5.4 %copy-start.2 = (bf16[2,384,1024]{2,1,0:T(8,128)(2,1)}, bf16[2,384,1024]{2,1,0:T(8,128)(2,1)S(1)}, u32[]{:S(2)}) copy-start(bf16[2,384,1024]{2,1,0:T(8,128)(2,1)S(1)} %get-tuple-element.67.units_any) | copy-start | bytes 4718596
  51.0 2.3 %collective-permute-start.9 = (bf16[320,1152]{1,0:T(8,128)(2,1)S(1)}, bf16[320,1152]{1,0:T(8,128)(2,1)S(1)}, u32[]{:S(2)}, u32[]{:S(2)}) collective-permute-start(bf16[320,1152]{1,0:T(8,128)(2,1)S(1)} %get-tuple-element.61.mine_any), channel_id=1, source_target_pairs={{0,1},{1,0},{2,3},{3,2},{4,5},{5,4},{6,7},{7,6},{8,9},{9,8},{10,11... | collective-permute-start | bytes 2211848 | tf_op jit(solution)/shard_map/ppermute | solution.py:466
  51.2 25.6 %collective-permute-start.16 = (bf16[384,1024]{1,0:T(8,128)(2,1)}, bf16[384,1024]{1,0:T(8,128)(2,1)S(1)}, u32[]{:S(2)}, u32[]{:S(2)}) collective-permute-start(bf16[384,1024]{1,0:T(8,128)(2,1)} %get-tuple-element.81.last_any), channel_id=1, source_target_pairs={{4,0},{5,1},{6,2},{7,3},{8,12},{9,13},{10,14},{11,15},{20,16},{21,... | collective-permute-start | bytes 2359304 | tf_op jit(solution)/shard_map/ppermute | solution.py:466
  53.3 6.8 %copy-start.4 = (bf16[304,1024]{1,0:T(8,128)(2,1)S(1)}, bf16[304,1024]{1,0:T(8,128)(2,1)}, u32[]{:S(2)}) copy-start(bf16[304,1024]{1,0:T(8,128)(2,1)} %copy-done.3) | copy-start | bytes 1867780
  53.3 6.9 %copy-start.6 = (bf16[304,1024]{1,0:T(8,128)(2,1)S(1)}, bf16[304,1024]{1,0:T(8,128)(2,1)}, u32[]{:S(2)}) copy-start(bf16[304,1024]{1,0:T(8,128)(2,1)} %copy-done.5) | copy-start | bytes 1867780
  56.5 3.7 %collective-permute-start.10 = (f32[8,128]{1,0:T(8,128)S(1)}, f32[8,128]{1,0:T(8,128)S(1)}, u32[]{:S(2)}, u32[]{:S(2)}) collective-permute-start(f32[8,128]{1,0:T(8,128)S(1)} %get-tuple-element.64), channel_id=1, source_target_pairs={{0,2},{1,3},{2,0},{3,1},{4,6},{5,7},{6,4},{7,5},{8,10},{9,11},{10,... | collective-permute-start | bytes 12296 | tf_op jit(solution)/shard_map/ppermute | solution.py:466
  56.6 14.7 %collective-permute-start.13 = (bf16[112,1024]{1,0:T(8,128)(2,1)S(1)}, bf16[112,1024]{1,0:T(8,128)(2,1)S(1)}, u32[]{:S(2)}, u32[]{:S(2)}) collective-permute-start(bf16[112,1024]{1,0:T(8,128)(2,1)S(1)} %get-tuple-element.74), channel_id=1, source_target_pairs={{0,2},{1,3},{2,0},{3,1},{4,6},{5,7},{6,4},{7,5},{8,10},{9,11},{10,... | collective-permute-start | bytes 688136 | tf_op jit(solution)/shard_map/ppermute | solution.py:466
  58.5 12.7 %collective-permute-start.14 = (bf16[112,1024]{1,0:T(8,128)(2,1)S(1)}, bf16[112,1024]{1,0:T(8,128)(2,1)S(1)}, u32[]{:S(2)}, u32[]{:S(2)}) collective-permute-start(bf16[112,1024]{1,0:T(8,128)(2,1)S(1)} %get-tuple-element.75), channel_id=1, source_target_pairs={{0,3},{1,2},{2,1},{3,0},{4,7},{5,6},{6,5},{7,4},{8,11},{9,10},{10,... | collective-permute-start | bytes 688136 | tf_op jit(solution)/shard_map/ppermute | solution.py:466
  60.1 6.1 %collective-permute-start.11 = (f32[4,128]{1,0:T(4,128)S(1)}, f32[4,128]{1,0:T(4,128)S(1)}, u32[]{:S(2)}, u32[]{:S(2)}) collective-permute-start(f32[4,128]{1,0:T(4,128)S(1)} %slice.19), channel_id=1, source_target_pairs={{0,1},{1,0},{2,3},{3,2},{4,5},{5,4},{6,7},{7,6},{8,9},{9,8},{10,11... | collective-permute-start | bytes 6152 | tf_op jit(solution)/shard_map/ppermute | solution.py:466
  60.2 7.4 %copy-start.1 = (bf16[1024,1024]{1,0:T(8,128)(2,1)S(1)}, bf16[1024,1024]{1,0:T(8,128)(2,1)}, u32[]{:S(2)}) copy-start(bf16[1024,1024]{1,0:T(8,128)(2,1)} %cent_ref.5) | copy-start | bytes 6291460
  66.3 8.5 %collective-permute-start.15 = (f32[2,128]{1,0:T(2,128)S(1)}, f32[2,128]{1,0:T(2,128)S(1)}, u32[]{:S(2)}, u32[]{:S(2)}) collective-permute-start(f32[2,128]{1,0:T(2,128)S(1)} %slice.21), channel_id=1, source_target_pairs={{0,12},{1,13},{2,14},{3,15},{4,8},{5,9},{6,10},{7,11},{8,4},{9,5},... | collective-permute-start | bytes 3080 | tf_op jit(solution)/shard_map/ppermute | solution.py:466
  71.3 0.7 copy-start.8
  74.8 5.0 %collective-permute-start.20 = (f32[1,128]{1,0:T(1,128)S(1)}, f32[1,128]{1,0:T(1,128)S(1)}, u32[]{:S(2)}, u32[]{:S(2)}) collective-permute-start(f32[1,128]{1,0:T(1,128)S(1)} %slice.23), channel_id=1, source_target_pairs={{0,4},{1,5},{2,6},{3,7},{4,0},{5,1},{6,2},{7,3},{8,12},{9,13},{10,... | collective-permute-start | bytes 1544 | tf_op jit(solution)/shard_map/ppermute | solution.py:466
  77.9 2.0 %collective-permute-start.17 = (f32[8,128]{1,0:T(8,128)S(1)}, f32[8,128]{1,0:T(8,128)S(1)}, u32[]{:S(2)}, u32[]{:S(2)}) collective-permute-start(f32[8,128]{1,0:T(8,128)S(1)} %get-tuple-element.83), channel_id=1, source_target_pairs={{0,1},{1,0},{2,3},{3,2},{4,5},{5,4},{6,7},{7,6},{8,9},{9,8},{10,11... | collective-permute-start | bytes 12296 | tf_op jit(solution)/shard_map/ppermute | solution.py:466
  78.0 3.7 %collective-permute-start.18 = (f32[8,128]{1,0:T(8,128)S(1)}, f32[8,128]{1,0:T(8,128)S(1)}, u32[]{:S(2)}, u32[]{:S(2)}) collective-permute-start(f32[8,128]{1,0:T(8,128)S(1)} %get-tuple-element.84), channel_id=1, source_target_pairs={{0,2},{1,3},{2,0},{3,1},{4,6},{5,7},{6,4},{7,5},{8,10},{9,11},{10,... | collective-permute-start | bytes 12296 | tf_op jit(solution)/shard_map/ppermute | solution.py:466
  79.5 3.0 %collective-permute-start.19 = (f32[8,128]{1,0:T(8,128)S(1)}, f32[8,128]{1,0:T(8,128)S(1)}, u32[]{:S(2)}, u32[]{:S(2)}) collective-permute-start(f32[8,128]{1,0:T(8,128)S(1)} %get-tuple-element.85), channel_id=1, source_target_pairs={{0,3},{1,2},{2,1},{3,0},{4,7},{5,6},{6,5},{7,4},{8,11},{9,10},{10,... | collective-permute-start | bytes 12296 | tf_op jit(solution)/shard_map/ppermute | solution.py:466
